TPU v7x, 32 devices: a whole 2x2x4 slice. The times are simulated.
32 devices in a mesh: dp: 8 (over z, x), shard: 4 (over y, core).
Axes of the slice: x: 2, y: 2, z: 4, core: 2. Of those that a mesh axis runs over, the one named last changes fastest.
Arguments:
- codes: int32 [8, 5, 8, 16], P('dp', None, None, 'shard'), may hold values from 0 to 262143
- lengths: int32 [8], P('dp'), may hold values from 1 to 5, 24 in all
- hidden: bfloat16 [8, 5, 8, 16, 512], P('dp', None, None, 'shard'), may hold values from -6 to 6
- embed: bfloat16 [18, 512], replicated, may hold values from -1.5 to 1.5
- conv_weight: bfloat16 [512, 27, 512], P('shard'), may hold values from -0.0546875 to 0.0546875
- gain: float32 [512], replicated, may hold values from 0.1 to 1.9
- bias: float32 [512], replicated, may hold values from -3 to 3
- cotangent: bfloat16 [8, 5, 16, 32, 128], P('dp', None, None, 'shard'), may hold values from -6 to 6
Outputs:
- decoded: bfloat16 [8, 5, 16, 32, 128], P('dp', None, None, 'shard')
- grad_hidden: bfloat16 [8, 5, 8, 16, 512], P('dp', None, None, 'shard')
- grad_conv: float32 [512, 27, 512], P('shard')
- grad_embed: float32 [18, 512], replicated
- grad_gain: float32 [512], replicated
- grad_bias: float32 [512], replicated
Inputs may be any that keep to these rules, and one draw needn't show every extreme that they name: Frames from lengths[c] on are padding; some clip has all 5 frames valid.
All inputs are finite; a program needn't handle non-finite values. No bound on the sum of `lengths` on one device may be relied on, other than what follows from the above.
Results may differ from a plain program's by a relative error of at most 0.02.
Values may be sent and summed in bfloat16 or wider, within the bound.
No kernel may reach another device: no remote copies, remote signals or barrier semaphores. Data moves between devices by JAX's collectives and lax.ppermute only.
A program may use at most 128 MiB of HBM per device.

v0:
```python
import jax
import jax.numpy as jnp
from jax import lax
from jax.sharding import PartitionSpec as P

CODE_BITS = 18
GROUPS = 32


eps_norm = 1e-05


def extended(block, sides, width):
    for axis, dim in sides:
        count = lax.axis_size(axis)
        forward = [(i, i + 1) for i in range(count - 1)]
        backward = [(target, source) for source, target in forward]
        low = lax.ppermute(
            lax.slice_in_dim(block, block.shape[dim] - width, None, axis=dim), axis, forward
        )
        high = lax.ppermute(lax.slice_in_dim(block, 0, width, axis=dim), axis, backward)
        block = jnp.concatenate([low, block, high], axis=dim)
    return block


def forward_taps(padded, frames, height, width):
    taps = []
    for depth_tap in range(3):
        for row_tap in range(3):
            for col_tap in range(3):
                taps.append(
                    padded[
                        depth_tap : depth_tap + frames,
                        row_tap : row_tap + height,
                        col_tap : col_tap + width,
                    ]
                )
    return taps


def backward_taps(padded, frames, height, width):
    taps = []
    for depth_tap in range(3):
        for row_tap in range(3):
            for col_tap in range(3):
                taps.append(
                    padded[
                        2 - depth_tap : 2 - depth_tap + frames,
                        2 - row_tap : 2 - row_tap + height,
                        2 - col_tap : 2 - col_tap + width,
                    ]
                )
    return taps


def own_columns(rimmed, frames, height, width):
    padded = jnp.pad(rimmed, ((2, 0), (1, 1), (0, 0), (0, 0)))
    return jnp.stack(forward_taps(padded, frames, height, width), axis=3)


def slab_columns(spread, frames, height, slab_width):
    padded = jnp.pad(spread, ((2, 0), (1, 1), (1, 1), (0, 0)))
    return jnp.concatenate(forward_taps(padded, frames, height, slab_width), axis=3)


def on_device(codes, lengths, hidden, embed, conv_weight, gain, bias, cotangent):
    frames = codes.shape[1]
    height = codes.shape[2]
    width = codes.shape[3]
    share = conv_weight.shape[0]
    channels = conv_weight.shape[2]
    quarter = channels // 4
    shards = lax.axis_size("shard")
    slab_width = width * shards
    positions = frames * height * width
    groups = GROUPS
    per_group = channels // groups
    frame_mask = (jnp.arange(frames) < lengths[0]).astype(jnp.float32)
    mask_cells = frame_mask[:, None, None, None]
    mask_groups = frame_mask[:, None, None, None, None]
    powers = 2 ** jnp.arange(CODE_BITS, dtype=jnp.int32)
    bits = (codes[0][..., None] // powers % 2 * 2 - 1).astype(jnp.bfloat16)
    embedded = jnp.dot(
        bits.reshape(positions, CODE_BITS), embed, preferred_element_type=jnp.float32
    ).reshape(frames, height, width, channels)
    features = ((embedded + hidden[0].astype(jnp.float32)) * mask_cells).astype(jnp.bfloat16)
    rimmed = extended(features, (("shard", 2),), 1)
    own_patches = own_columns(rimmed, frames, height, width)
    conv_out = jnp.einsum(
        "frwtn,ntc->frwc",
        own_patches,
        lax.all_gather(conv_weight, "shard", axis=0, tiled=True),
        preferred_element_type=jnp.float32,
    )
    grouped = conv_out.reshape(frames, height, width, groups, per_group)
    sum_one, sum_two = lax.psum(
        (
            jnp.sum(grouped * mask_groups, axis=(0, 1, 2, 4)),
            jnp.sum(grouped * grouped * mask_groups, axis=(0, 1, 2, 4)),
        ),
        "shard",
    )
    count = lengths[0].astype(jnp.float32) * (height * width * shards * per_group)
    mean = sum_one / count
    variance = sum_two / count - mean * mean
    inv_std = lax.rsqrt(variance + eps_norm)
    gain_group = gain.reshape(groups, per_group)
    bias_group = bias.reshape(groups, per_group)
    normed = (grouped - mean[:, None]) * inv_std[:, None]
    pre = normed * gain_group + bias_group
    sigma = jax.nn.sigmoid(pre)
    activated = pre * sigma * mask_groups
    decoded = (
        activated.reshape(frames, height, width, 2, 2, quarter)
        .transpose(0, 1, 3, 2, 4, 5)
        .reshape(frames, 2 * height, 2 * width, quarter)
        .astype(jnp.bfloat16)[None]
    )
    upstream = (
        cotangent[0]
        .astype(jnp.float32)
        .reshape(frames, height, 2, width, 2, quarter)
        .transpose(0, 1, 3, 2, 4, 5)
        .reshape(frames, height, width, groups, per_group)
        * mask_groups
    )
    d_pre = upstream * sigma * (1.0 + pre * (1.0 - sigma))
    gain_term = jnp.sum(d_pre * normed, axis=(0, 1, 2)).reshape(channels)
    bias_term = jnp.sum(d_pre, axis=(0, 1, 2)).reshape(channels)
    d_norm = d_pre * gain_group
    tot_one, tot_two = lax.psum(
        (jnp.sum(d_norm, axis=(0, 1, 2, 4)), jnp.sum(d_norm * normed, axis=(0, 1, 2, 4))), "shard"
    )
    d_conv = (
        (
            inv_std[:, None]
            * (d_norm - tot_one[:, None] / count - normed * tot_two[:, None] / count)
            * mask_groups
        )
        .reshape(frames, height, width, channels)
        .astype(jnp.bfloat16)
    )
    spread_back = lax.all_to_all(features, "shard", split_axis=3, concat_axis=2, tiled=True)
    slab_back = slab_columns(spread_back, frames, height, slab_width)
    whole_grad = lax.all_gather(d_conv, "shard", axis=2, tiled=True)
    back_share = jnp.transpose(conv_weight, (2, 1, 0)).reshape(channels, 27 * share)
    tap_images = jnp.dot(
        whole_grad.reshape(-1, channels), back_share, preferred_element_type=jnp.float32
    ).reshape(frames, height, slab_width, 27 * share)
    padded_images = jnp.pad(tap_images, ((0, 2), (1, 1), (1, 1), (0, 0)))
    input_sum = jnp.zeros((frames, height, slab_width, share), jnp.float32)
    for tap_index, shifted in enumerate(backward_taps(padded_images, frames, height, slab_width)):
        input_sum = input_sum + shifted[..., tap_index * share : (tap_index + 1) * share]
    d_features = lax.all_to_all(
        input_sum.astype(jnp.bfloat16), "shard", split_axis=2, concat_axis=3, tiled=True
    )
    clip_part = jnp.einsum(
        "pk,pc->kc",
        slab_back.reshape(-1, 27 * share),
        whole_grad.reshape(-1, channels),
        preferred_element_type=jnp.float32,
    )
    weight_sum = clip_part.reshape(27, share, channels).transpose(1, 0, 2)
    grad_conv = lax.psum(weight_sum.astype(jnp.bfloat16), "dp").astype(jnp.float32)
    grad_hidden = d_features * mask_cells.astype(jnp.bfloat16)
    embed_term = jnp.dot(
        bits.reshape(positions, CODE_BITS).T,
        grad_hidden.reshape(positions, channels),
        preferred_element_type=jnp.float32,
    )
    grad_embed, grad_gain, grad_bias = lax.psum((embed_term, gain_term, bias_term), ("dp", "shard"))
    return (decoded, grad_hidden[None], grad_conv, grad_embed, grad_gain, grad_bias)


def solution(mesh):
    return jax.shard_map(
        on_device,
        mesh=mesh,
        in_specs=(
            P("dp", None, None, "shard"),
            P("dp"),
            P("dp", None, None, "shard", None),
            P(),
            P("shard", None, None),
            P(),
            P(),
            P("dp", None, None, "shard", None),
        ),
        out_specs=(
            P("dp", None, None, "shard", None),
            P("dp", None, None, "shard", None),
            P("shard", None, None),
            P(),
            P(),
            P(),
        ),
        check_vma=False,
    )
```

profile of v0, /device:TPU:0, one launch (start us, length us, event | category | flops | bytes accessed | tf_op | source)
XLA Modules:
  0.0 299.3 jit_solution(15828794804816433913)
XLA Ops:
  9.4 2.0 fusion.9
  12.0 2.3 collective-permute-start
  14.3 1.3 collective-permute-start.1
  15.6 1.4 copy.111
  17.1 3.4 %reshape.296 = bf16[4,2,10240]{2,1,0:T(2,128)(2,1)} reshape(bf16[512,5,4,8]{3,2,1,0:T(4,128)(2,1)S(1)} %bitcast.227) | data formatting | bytes 327680
  20.5 6.1 %all-to-all-start.1 = ((bf16[4,2,10240]{2,1,0:T(2,128)(2,1)}), bf16[4,2,10240]{2,1,0:T(2,128)(2,1)}, u32[]{:S(2)}, u32[]{:S(2)}) async-start(bf16[4,2,10240]{2,1,0:T(2,128)(2,1)} %reshape.296), calls=%async_computation.1 | async-start | bytes 327680 | tf_op jit(solution)/shard_map/all_to_all | solution.py:143
  26.7 1.0 copy.106
  30.0 0.7 fusion.72
  30.7 0.7 fusion.71
  31.5 0.7 fusion.70
  32.2 0.7 fusion.69
  32.9 0.7 fusion.68
  33.6 0.7 fusion.67
  36.4 0.7 fusion.63
  37.1 0.7 fusion.62
  37.8 0.7 fusion.61
  38.5 0.7 fusion.60
  39.2 0.7 fusion.59
  39.9 0.7 fusion.58
  44.7 0.7 fusion.50
  45.4 0.7 fusion.49
  46.2 0.7 fusion.48
  46.9 3.9 %reshape.297 = bf16[512,5,4,8]{3,2,1,0:T(4,128)(2,1)S(1)} reshape(bf16[4,2,10240]{2,1,0:T(2,128)(2,1)} %all-to-all-done.1) | data formatting | bytes 327680
  50.8 1.3 copy.113
  52.1 2.2 copy.136
  56.0 0.7 constant_dynamic-update-slice_fusion.26
  56.7 0.7 constant_dynamic-update-slice_fusion.25
  57.4 0.7 constant_dynamic-update-slice_fusion.24
  67.9 0.7 constant_dynamic-update-slice_fusion.9
  70.8 0.7 constant_dynamic-update-slice_fusion.5
  72.9 0.7 constant_dynamic-update-slice_fusion.2
  75.0 7.2 %copy.141 = bf16[3456,640]{1,0:T(8,128)(2,1)} copy(bf16[3456,640]{0,1:T(8,128)(2,1)} %bitcast.80) | data formatting | bytes 8847360 | tf_op jit(solution)/shard_map/pk,pc->kc/dot_general | solution.py:157
  82.2 22.9 %all-gather.2.cloned.1.call-done = bf16[512,27,512]{2,0,1:T(8,128)(2,1)} async-done(((bf16[128,27,512]{2,0,1:T(8,128)(2,1)}), bf16[512,27,512]{2,0,1:T(8,128)(2,1)}) %all-gather.2.cloned.1.call-update) | async-done | bytes 14155792 | tf_op jit(solution)/shard_map/all_gather | solution.py:92
  105.1 8.8 %fusion = f32[5,8,4,512,1]{3,1,0,2,4:T(8,128)S(1)} fusion(bf16[512,27,512]{2,0,1:T(8,128)(2,1)} %all-gather.2.cloned.1.call-done, bf16[5,8,4,27,512]{4,1,2,0,3:T(8,128)(2,1)} %fusion.48), kind=kOutput, calls=%fused_computation.26 | convolution fusion | flops 2264924160 | bytes 18907136 | tf_op jit(solution)/shard_map/frwtn,ntc->frwc/dot_general | solution.py:89
  114.5 5.9 %all-reduce.5 = (f32[32]{0:T(128)S(1)}, f32[32]{0:T(128)S(1)}) all-reduce(f32[32]{0:T(128)S(1)} %reduce_sum.67, f32[32]{0:T(128)S(1)} %reduce_sum.73), channel_id=1, replica_groups=mesh['dp'=8,'shard'=4] {'shard'}, use_global_device_ids=true, to_apply=%region_2.3 | all-reduce | flops 64 | bytes 512 | tf_op jit(solution)/shard_map/psum | solution.py:96
  120.9 0.9 fusion.42
  122.9 5.8 %all-reduce.4 = (f32[32]{0:T(128)S(1)}, f32[32]{0:T(128)S(1)}) all-reduce(f32[32]{0:T(128)S(1)} %reduce_sum.93, f32[32]{0:T(128)S(1)} %reduce_sum.90), channel_id=1, replica_groups=mesh['dp'=8,'shard'=4] {'shard'}, use_global_device_ids=true, to_apply=%region_11.12 | all-reduce | flops 64 | bytes 512 | tf_op jit(solution)/shard_map/psum | solution.py:131
  129.7 8.1 %all_gather.7 = bf16[5,8,16,512]{3,1,2,0:T(8,128)(2,1)S(1)} all-gather(bf16[5,8,4,512]{3,1,2,0:T(8,128)(2,1)S(1)} %multiply_convert_fusion), channel_id=1, replica_groups=mesh['dp'=8,'shard'=4] {'shard'}, dimensions={2}, use_global_device_ids=true | all-gather | bytes 819200 | tf_op jit(solution)/shard_map/all_gather | solution.py:145
  138.6 6.7 %convert_bitcast_fusion = bf16[128,27,512]{2,0,1:T(8,128)(2,1)} fusion(bf16[27,128,640]{2,1,0:T(8,128)(2,1)} %bitcast.228, bf16[640,512,1]{1,0,2:T(8,128)(2,1)S(1)} %bitcast.234), kind=kOutput, calls=%fused_computation.29 | convolution fusion | flops 2266693632 | bytes 8617984 | tf_op jit(solution)/shard_map/pk,pc->kc/dot_general | solution.py:157
  145.4 3.7 %fusion.99 = f32[5,8,16,3456]{3,2,1,0:T(8,128)S(1)} fusion(bf16[512,3456,1,1]{0,1,3,2:T(8,128)(2,1)S(1)} %bitcast.226, bf16[5,8,16,512]{3,1,2,0:T(8,128)(2,1)} %copy-done.3), kind=kOutput, calls=%fused_computation.242 | convolution fusion | flops 2264924160 | bytes 13041664 | tf_op jit(solution)/shard_map/dot_general | solution.py:147
  150.3 3.3 %all-to-all-start = ((bf16[5,8,16,128]{3,1,0,2:T(8,128)(2,1)}), bf16[5,8,16,128]{3,1,0,2:T(8,128)(2,1)S(1)}, u32[]{:S(2)}, u32[]{:S(2)}) async-start(bf16[5,8,16,128]{3,1,0,2:T(8,128)(2,1)} %copy.109), calls=%async_computation | async-start | bytes 327680 | tf_op jit(solution)/shard_map/all_to_all | solution.py:154
  153.7 0.8 copy.105
  154.5 4.1 %all-to-all-done = bf16[5,8,16,128]{3,1,0,2:T(8,128)(2,1)S(1)} async-done(((bf16[5,8,16,128]{3,1,0,2:T(8,128)(2,1)}), bf16[5,8,16,128]{3,1,0,2:T(8,128)(2,1)S(1)}, u32[]{:S(2)}, u32[]{:S(2)}) %all-to-all-start) | async-done | bytes 163872 | tf_op jit(solution)/shard_map/all_to_all | solution.py:154
  158.8 1.1 convolution_bitcast_fusion
  159.9 42.5 %all-reduce.3 = (f32[18,512]{1,0:T(8,128)}, f32[512]{0:T(512)}, f32[512]{0:T(512)}) all-reduce(f32[18,512]{1,0:T(8,128)S(1)} %convolution_bitcast_fusion, f32[512]{0:T(512)S(1)} %bitcast.272, f32[512]{0:T(512)S(1)} %bitcast.273), channel_id=1, replica_groups=mesh['dp'=8,'shard'=4] {'dp','shard'}, use_global_device_ids=true, to_apply=%region_13.14 | all-reduce | flops 10240 | bytes 81920 | tf_op jit(solution)/shard_map/psum | solution.py:171
  202.4 0.8 broadcast_multiply_fusion
  203.2 83.3 %all-reduce.8.cloned.1.call-done = bf16[128,27,512]{2,0,1:T(8,128)(2,1)} async-done(((bf16[128,27,512]{2,0,1:T(8,128)(2,1)}), bf16[128,27,512]{2,0,1:T(8,128)(2,1)}) %all-reduce.8.cloned.1.call-update) | async-done | bytes 3538960 | tf_op jit(solution)/shard_map/psum | solution.py:164
  286.6 5.9 %convert_element_type.96 = f32[128,27,512]{2,0,1:T(8,128)} convert(bf16[128,27,512]{2,0,1:T(8,128)(2,1)} %all-reduce.8.cloned.1.call-done) | non-fusion elementwise | flops 1769472 | bytes 10616832 | tf_op jit(solution)/shard_map/convert_element_type | solution.py:164
  (138 shorter events, 31.9 us)
Async XLA Ops:
  7.2 2.2 copy-start
  7.2 97.9 %all-gather.2.cloned.1.call-start = ((), (), s32[]{:S(2)}) async-start(), calls=%async_computation.2 | async-start | bytes 17694720 | tf_op jit(solution)/shard_map/all_gather | solution.py:92
  7.9 18.7 %copy-start.4 = (bf16[1,5,16,8,128]{4,3,2,1,0:T(8,128)(2,1)S(1)}, bf16[1,5,16,8,128]{4,3,2,1,0:T(8,128)(2,1)}, u32[]{:S(2)}) copy-start(bf16[1,5,16,8,128]{4,3,2,1,0:T(8,128)(2,1)} %param.15) | copy-start | bytes 491524
  8.6 19.3 %copy-start.11 = (s32[18]{0:T(128)}, s32[18]{0:T(128)S(1)}, u32[]{:S(2)}) copy-start(s32[18]{0:T(128)S(1)} %get-tuple-element.51) | copy-start | bytes 220
  8.7 19.3 %copy-start.13 = (s32[18]{0:T(128)}, s32[18]{0:T(128)S(1)}, u32[]{:S(2)}) copy-start(s32[18]{0:T(128)S(1)} %get-tuple-element.52) | copy-start | bytes 220
  12.0 15.7 %collective-permute-start = (bf16[5,8,1,512]{3,1,2,0:T(8,128)(2,1)}, bf16[5,8,1,512]{3,1,2,0:T(8,128)(2,1)S(1)}, u32[]{:S(2)}, u32[]{:S(2)}) collective-permute-start(bf16[5,8,1,512]{3,1,2,0:T(8,128)(2,1)} %get-tuple-element.49), channel_id=1, source_target_pairs={{0,1},{1,2},{2,3},{4,5},{5,6},{6,7},{8,9},{9,10},{10,11},{12,13},{... | collective-permute-start | bytes 122888 | tf_op jit(solution)/shard_map/ppermute | solution.py:18
  14.3 13.4 %collective-permute-start.1 = (bf16[5,8,1,512]{3,1,2,0:T(8,128)(2,1)}, bf16[5,8,1,512]{3,1,2,0:T(8,128)(2,1)S(1)}, u32[]{:S(2)}, u32[]{:S(2)}) collective-permute-start(bf16[5,8,1,512]{3,1,2,0:T(8,128)(2,1)} %get-tuple-element.50), channel_id=1, source_target_pairs={{1,0},{2,1},{3,2},{5,4},{6,5},{7,6},{9,8},{10,9},{11,10},{13,12},{... | collective-permute-start | bytes 122888 | tf_op jit(solution)/shard_map/ppermute | solution.py:21
  20.5 26.4 %all-to-all-start.1 = ((bf16[4,2,10240]{2,1,0:T(2,128)(2,1)}), bf16[4,2,10240]{2,1,0:T(2,128)(2,1)}, u32[]{:S(2)}, u32[]{:S(2)}) async-start(bf16[4,2,10240]{2,1,0:T(2,128)(2,1)} %reshape.296), calls=%async_computation.1 | async-start | bytes 327680 | tf_op jit(solution)/shard_map/all_to_all | solution.py:143
  26.6 260.0 %all-reduce.8.cloned.1.call-start = ((), (), s32[]{:S(2)}) async-start(), calls=%async_computation.3 | async-start | bytes 7077888 | tf_op jit(solution)/shard_map/psum | solution.py:164
  55.8 15.7 %copy-start.5 = (bf16[5,8,4,4,128]{4,3,2,1,0:T(4,128)(2,1)S(1)}, bf16[5,8,4,4,128]{4,3,2,1,0:T(4,128)(2,1)}, u32[]{:S(2)}) copy-start(bf16[5,8,4,4,128]{4,3,2,1,0:T(4,128)(2,1)} %copy.136) | copy-start | bytes 491524
  82.2 38.7 %copy-start.7 = (f32[512]{0:T(512)S(1)}, f32[512]{0:T(512)}, u32[]{:S(2)}) copy-start(f32[512]{0:T(512)} %param.13) | copy-start | bytes 6148
  82.2 38.7 %copy-start.9 = (f32[512]{0:T(512)S(1)}, f32[512]{0:T(512)}, u32[]{:S(2)}) copy-start(f32[512]{0:T(512)} %param.14) | copy-start | bytes 6148
  137.8 0.9 copy-start.3
  138.6 6.8 %copy-start.2 = (bf16[128,27,512]{2,0,1:T(8,128)(2,1)S(1)}, bf16[128,27,512]{2,0,1:T(8,128)(2,1)}, u32[]{:S(2)}) copy-start(bf16[128,27,512]{2,0,1:T(8,128)(2,1)} %param.12) | copy-start | bytes 10616836
  149.1 4.6 %copy-start.6 = (bf16[5,8,2,4,2,128]{5,1,4,2,3,0:T(8,128)(2,1)S(1)}, bf16[5,8,2,4,2,128]{5,1,4,2,3,0:T(8,128)(2,1)}, u32[]{:S(2)}) copy-start(bf16[5,8,2,4,2,128]{5,1,4,2,3,0:T(8,128)(2,1)} %get-tuple-element.22) | copy-start | bytes 491524
  149.1 9.7 %copy-start.8 = (s32[1,5,8,4]{2,3,1,0:T(4,128)S(1)}, s32[1,5,8,4]{2,3,1,0:T(4,128)}, u32[]{:S(2)}) copy-start(s32[1,5,8,4]{2,3,1,0:T(4,128)} %param.8) | copy-start | bytes 1924
  149.1 9.7 %copy-start.12 = (s32[18]{0:T(128)S(1)}, s32[18]{0:T(128)}, u32[]{:S(2)}) copy-start(s32[18]{0:T(128)} %copy-done.11) | copy-start | bytes 220
  149.1 9.7 %copy-start.14 = (s32[18]{0:T(128)S(1)}, s32[18]{0:T(128)}, u32[]{:S(2)}) copy-start(s32[18]{0:T(128)} %copy-done.13) | copy-start | bytes 220
  149.1 10.8 %copy-start.10 = (f32[2,2,128]{2,1,0:T(2,128)S(1)}, f32[2,2,128]{2,1,0:T(2,128)}, u32[]{:S(2)}) copy-start(f32[2,2,128]{2,1,0:T(2,128)} %get-tuple-element.11) | copy-start | bytes 6148
  150.3 8.3 %all-to-all-start = ((bf16[5,8,16,128]{3,1,0,2:T(8,128)(2,1)}), bf16[5,8,16,128]{3,1,0,2:T(8,128)(2,1)S(1)}, u32[]{:S(2)}, u32[]{:S(2)}) async-start(bf16[5,8,16,128]{3,1,0,2:T(8,128)(2,1)} %copy.109), calls=%async_computation | async-start | bytes 327680 | tf_op jit(solution)/shard_map/all_to_all | solution.py:154
  202.4 90.1 %copy-start.1 = (bf16[18,512]{1,0:T(8,128)(2,1)S(1)}, bf16[18,512]{1,0:T(8,128)(2,1)}, u32[]{:S(2)}) copy-start(bf16[18,512]{1,0:T(8,128)(2,1)} %param.11) | copy-start | bytes 55300
Sparse Core Ops, SparseCore 0:
  9.6 95.4 all-gather.1
  145.5 141.0 all-reduce.7
where the time goes:
time: 300 us; the launch traced here: 299 us
  waiting for transfers between devices  111 us (37%)
  local copies, waits for them, and re-layouts  63 us (21%)
  blocking collectives  62.4 us (21%)
  matrix products  22.2 us (7%)
  between operations  15.3 us (5%)
  starting transfers between devices  13.2 us (4%)
  other arithmetic  12.1 us (4%)
    psum x1, waiting for transfers between devices, on_device(): lax.psum(weight_sum.astype(jnp.bfloat16), 'dp').astype(jnp.float32)  83.3 us
    unnamed x82, local copies, waits for them, and re-layouts  43.2 us
    psum x1, blocking collectives, on_device(): lax.psum((embed_term, gain_term, bias_term), ('dp', 'shard'))  42.5 us
    all_gather x1, waiting for transfers between devices, on_device(): lax.all_gather(conv_weight, 'shard', axis=0, tiled=True)  22.9 us
    dot_general x1, matrix products, on_device(): jnp.einsum('frwtn,ntc->frwc', own_patches, lax.all_gather(conv_weight, 's...  8.81 us
    all_gather x1, blocking collectives, on_device(): whole_grad = lax.all_gather(d_conv, 'shard', axis=2, tiled=True)  8.13 us
    dot_general x1, local copies, waits for them, and re-layouts, on_device(): jnp.einsum('pk,pc->kc', slab_back.reshape(-1, 27 * share), whole_grad.res...  7.23 us
    dot_general x1, matrix products, on_device(): jnp.einsum('pk,pc->kc', slab_back.reshape(-1, 27 * share), whole_grad.res...  6.73 us
  transfers between devices with their start and end apart: 6, of which 3 were waited for; matrix products, arithmetic and copies ran while one was open for 24% of the time, Pallas kernels for 0%

commit v1 on v0

--- a/solution.py
+++ b/solution.py
@@ -1,13 +1,455 @@
 import jax
 import jax.numpy as jnp
 from jax import lax
+from jax.experimental import pallas as pl
+from jax.experimental.pallas import tpu as pltpu
 from jax.sharding import PartitionSpec as P
 
 CODE_BITS = 18
 GROUPS = 32
-
+LANES = 128
+VMEM_BYTES = 56 * 1024 * 1024
 
 eps_norm = 1e-05
+
+bf16 = jnp.bfloat16
+f32 = jnp.float32
+
+
+def kernel_call(body, outs, args, scratch=(), scalars=1, flops=0, aliases=None):
+    specs = [pl.BlockSpec(memory_space=pltpu.SMEM)] * scalars
+    specs += [pl.BlockSpec(memory_space=pltpu.VMEM)] * (len(args) - scalars)
+    moved = sum(a.size * a.dtype.itemsize for a in args)
+    moved += sum(o.size * o.dtype.itemsize for o in outs)
+    return pl.pallas_call(
+        body,
+        out_shape=outs,
+        in_specs=specs,
+        out_specs=[pl.BlockSpec(memory_space=pltpu.VMEM)] * len(outs),
+        scratch_shapes=scratch,
+        input_output_aliases=aliases or {},
+        compiler_params=pltpu.CompilerParams(vmem_limit_bytes=VMEM_BYTES),
+        cost_estimate=pl.CostEstimate(flops=flops, bytes_accessed=moved, transcendentals=0),
+    )(*args)
+
+
+def shaped(shape, dtype):
+    return jax.ShapeDtypeStruct(shape, dtype)
+
+
+def swap(block, hop):
+    pairs = [(i, i ^ hop) for i in range(lax.axis_size("shard"))]
+    return lax.ppermute(block, "shard", pairs)
+
+
+def step_rows(slab, first, count, step):
+    return slab[pl.ds(first, count, stride=step), :]
+
+def frame_rows_below(rows, limit):
+    return (lax.broadcasted_iota(jnp.int32, (rows, 1), 0) < limit).astype(f32)
+
+
+def embed_body(shards, width, frame_rows, info, codes, hidden, embed, cot, *rest):
+    sends, (chunks, cot_wide, part) = rest[:shards], rest[shards:]
+    rows = codes.shape[0]
+    cells = rows // width
+    lanes = lax.broadcasted_iota(jnp.int32, (rows, LANES), 1)
+    spread = jnp.broadcast_to(codes[...], (rows, LANES))
+    bit = lax.bitwise_and(lax.shift_right_logical(spread, jnp.minimum(lanes, 31)), 1)
+    bits = jnp.where(lanes < CODE_BITS, 2 * bit - 1, 0).astype(f32).astype(bf16)
+    embedded = jnp.dot(bits, embed[...], preferred_element_type=f32)
+    mask = frame_rows_below(rows, info[0] * frame_rows)
+    features = ((embedded + hidden[...].astype(f32)) * mask).astype(bf16)
+    cot_wide[...] = cot[...].astype(f32)
+    for j in range(shards):
+        chunks[j, :, :LANES] = features[:, j * LANES : (j + 1) * LANES]
+        for w in range(width):
+            first = (j // 2) * (2 * width) + 2 * w + j % 2
+            part[pl.ds(w, cells, stride=width), :] = step_rows(cot_wide, first, cells, 4 * width)
+        chunks[j, :, LANES:] = part[...].astype(bf16)
+    for hop in range(shards):
+        sends[hop][...] = chunks[lax.bitwise_xor(info[1], hop)]
+
+
+def forward_body(shards, width, frames, height, info, *rest):
+    parts, weight = rest[:shards], rest[shards]
+    own_out = rest[shards + 1]
+    sends = rest[shards + 2 : 2 * shards + 1]
+    slab_out, turned_out, cot_out = rest[2 * shards + 1 : 2 * shards + 4]
+    chunks, slab, cot, rims, patches, sums = rest[2 * shards + 4 :]
+    columns = width * shards
+    rows = frames * height * columns
+    cells = frames * height
+    for hop in range(shards):
+        origin = lax.bitwise_xor(info[1], hop)
+        chunks[origin, 0] = parts[hop][:, :LANES].astype(f32)
+        chunks[origin, 1] = parts[hop][:, LANES:].astype(f32)
+    for j in range(shards):
+        for w in range(width):
+            place = pl.ds(width * j + w, cells, stride=columns)
+            slab[place, :] = chunks[j, 0, pl.ds(w, cells, stride=width), :]
+            cot[place, :] = chunks[j, 1, pl.ds(w, cells, stride=width), :]
+    cot_out[...] = cot[...].astype(bf16)
+    middle = slab[...]
+    slab_out[...] = middle.astype(bf16)
+    turned_out[...] = middle.T.astype(bf16)
+    column = lax.broadcasted_iota(jnp.int32, (rows, 1), 0) % columns
+    rims[...] = jnp.zeros_like(rims)
+    shifted = (
+        jnp.where(column > 0, pltpu.roll(middle, 1, 0), 0.0),
+        middle,
+        jnp.where(column < columns - 1, pltpu.roll(middle, rows - 1, 0), 0.0),
+    )
+    for dw in range(3):
+        rims[dw, 2:, 1 : height + 1] = (
+            shifted[dw].astype(bf16).reshape(frames, height, columns, LANES)
+        )
+    for dt in range(3):
+        for dr in range(3):
+            for dw in range(3):
+                tap = (dt * 3 + dr) * 3 + dw
+                patches[:, tap * LANES : (tap + 1) * LANES] = rims[
+                    dw, dt : dt + frames, dr : dr + height
+                ].reshape(rows, LANES)
+    for half in range(shards // 2):
+        total = jnp.dot(
+            patches[...],
+            weight[:, half * 2 * LANES : (half + 1) * 2 * LANES],
+            preferred_element_type=f32,
+        )
+        sums[2 * half] = total[:, :LANES]
+        sums[2 * half + 1] = total[:, LANES:]
+    own_out[...] = sums[info[1]]
+    for hop in range(1, shards):
+        sends[hop - 1][...] = sums[lax.bitwise_xor(info[1], hop)].astype(bf16)
+
+
+def group_total(values, per_group):
+    lane = lax.broadcasted_iota(jnp.int32, values.shape, 1)
+    step = 1
+    while step < per_group:
+        above = pltpu.roll(values, LANES - step, 1)
+        below = pltpu.roll(values, step, 1)
+        values = values + jnp.where(lax.bitwise_and(lane, step) == 0, above, below)
+        step *= 2
+    return values
+
+
+def column_total(values):
+    return jnp.broadcast_to(jnp.sum(values, axis=0, keepdims=True), (8, LANES))
+
+
+def norm_body(shards, width, frames, height, per_group, info, *rest):
+    own, parts = rest[0], rest[1:shards]
+    gain, bias, cot, d_conv_out, terms_out = rest[shards : shards + 5]
+    sends = rest[shards + 5 : 2 * shards + 5]
+    conv, slope, act, part = rest[2 * shards + 5 :]
+    columns = width * shards
+    cells = frames * height
+    block = height * columns
+    length = info[0]
+    sum_one = jnp.zeros((8, LANES), f32)
+    sum_two = jnp.zeros((8, LANES), f32)
+    for t in range(frames):
+        span = pl.ds(t * block, block)
+        values = own[span, :]
+        for received in parts:
+            values = values + received[span, :].astype(f32)
+        conv[span, :] = values
+        mask = (t < length).astype(f32)
+        sum_one += column_total(values) * mask
+        sum_two += column_total(values * values) * mask
+    count = length.astype(f32) * (block * per_group)
+    mean = group_total(sum_one, per_group) / count
+    variance = group_total(sum_two, per_group) / count - mean * mean
+    inv_std = lax.rsqrt(variance + eps_norm)[:1]
+    mean = mean[:1]
+    gain_sum = jnp.zeros((8, LANES), f32)
+    bias_sum = jnp.zeros((8, LANES), f32)
+    for t in range(frames):
+        span = pl.ds(t * block, block)
+        mask = (t < length).astype(f32)
+        normed = (conv[span, :] - mean) * inv_std
+        pre = normed * gain[...] + bias[...]
+        sigma = jax.nn.sigmoid(pre)
+        act[span, :] = pre * sigma * mask
+        d_pre = cot[span, :].astype(f32) * mask * sigma * (1.0 + pre * (1.0 - sigma))
+        conv[span, :] = normed
+        slope[span, :] = d_pre
+        gain_sum += column_total(d_pre * normed)
+        bias_sum += column_total(d_pre)
+    row = lax.broadcasted_iota(jnp.int32, (8, LANES), 0)
+    terms_out[...] = jnp.where(row == 0, gain_sum, jnp.where(row == 1, bias_sum, 0.0))
+    tot_one = (group_total(bias_sum * gain[...], per_group) / count)[:1]
+    tot_two = (group_total(gain_sum * gain[...], per_group) / count)[:1]
+    for t in range(frames):
+        span = pl.ds(t * block, block)
+        mask = (t < length).astype(f32)
+        d_norm = slope[span, :] * gain[...]
+        d_conv_out[span, :] = (
+            inv_std * (d_norm - tot_one - conv[span, :] * tot_two) * mask
+        ).astype(bf16)
+    column_chunks(shards, width, cells, info, act, part, sends)
+
+
+def column_chunks(shards, width, cells, info, slab, part, sends):
+    for j in range(shards):
+        for w in range(width):
+            part[j, pl.ds(w, cells, stride=width), :] = step_rows(
+                slab, width * j + w, cells, width * shards
+            )
+    for hop in range(shards):
+        sends[hop][...] = part[lax.bitwise_xor(info[1], hop)].astype(bf16)
+
+
+def input_grad_body(shards, width, frames, height, info, *rest):
+    parts, weight, codes = rest[:shards], rest[shards], rest[shards + 1 : 2 * shards + 1]
+    embed_out = rest[2 * shards + 1]
+    sends = rest[2 * shards + 2 : 3 * shards + 2]
+    pieces, whole, sums, part = rest[3 * shards + 2 :]
+    columns = width * shards
+    rows = frames * height * columns
+    cells = frames * height
+    for hop in range(shards):
+        pieces[lax.bitwise_xor(info[1], hop)] = parts[hop][...]
+    for j in range(shards):
+        whole[:, j * LANES : (j + 1) * LANES] = pieces[j]
+    sums[...] = jnp.zeros_like(sums)
+    for first in range(0, 27, 2):
+        taps = min(2, 27 - first)
+        images = lax.dot_general(
+            whole[...],
+            weight[first * LANES : (first + taps) * LANES, :],
+            (((1,), (1,)), ((), ())),
+            preferred_element_type=f32,
+        )
+        for tap in range(first, first + taps):
+            dt, dr, dw = tap // 9, tap // 3 % 3, tap % 3
+            image = images[:, (tap - first) * LANES : (tap - first + 1) * LANES]
+            image = image.reshape(frames, height, columns, LANES)
+            low, high = max(0, dr - 1), min(height, height + dr - 1)
+            sums[dw, : frames - 2 + dt, low:high] += image[
+                2 - dt :, low + 1 - dr : high + 1 - dr
+            ]
+    column = lax.broadcasted_iota(jnp.int32, (rows, 1), 0) % columns
+    after = pltpu.roll(sums[0].reshape(rows, LANES), rows - 1, 0)
+    before = pltpu.roll(sums[2].reshape(rows, LANES), 1, 0)
+    total = sums[1].reshape(rows, LANES)
+    total = total + jnp.where(column < columns - 1, after, 0.0)
+    total = total + jnp.where(column > 0, before, 0.0)
+    total = total * frame_rows_below(rows, info[0] * (height * columns))
+    slab = sums.at[1]
+    slab[...] = total.reshape(frames, height, columns, LANES)
+    flat = slab.reshape(rows, LANES)
+    column_chunks(shards, width, cells, info, flat, part, sends)
+    level = lax.broadcasted_iota(jnp.int32, (32, cells * width), 0)
+    embed_term = jnp.zeros((32, LANES), f32)
+    for hop in range(shards):
+        spread = jnp.broadcast_to(codes[hop][...], (32, cells * width))
+        bit = lax.bitwise_and(lax.shift_right_logical(spread, level), 1)
+        bits = jnp.where(level < CODE_BITS, 2 * bit - 1, 0).astype(f32).astype(bf16)
+        embed_term += jnp.dot(bits, sends[hop][...], preferred_element_type=f32)
+    embed_out[...] = embed_term
+
+
+def hidden_body(shards, info, *rest):
+    parts, out, pieces = rest[:shards], rest[shards], rest[shards + 1]
+    for hop in range(shards):
+        pieces[lax.bitwise_xor(info[1], hop)] = parts[hop][...]
+    for j in range(shards):
+        out[:, j * LANES : (j + 1) * LANES] = pieces[j]
+
+
+def decoded_body(shards, width, info, *rest):
+    parts, out, pieces, slab = rest[:shards], rest[shards], rest[shards + 1], rest[shards + 2]
+    cells = parts[0].shape[0] // width
+    for hop in range(shards):
+        pieces[lax.bitwise_xor(info[1], hop)] = parts[hop][...].astype(f32)
+    for j in range(shards):
+        for w in range(width):
+            first = (j // 2) * (2 * width) + 2 * w + j % 2
+            slab[pl.ds(first, cells, stride=4 * width), :] = pieces[
+                j, pl.ds(w, cells, stride=width), :
+            ]
+    out[...] = slab[...].astype(bf16)
+
+
+def weight_grad_body(frames, height, columns, lengths, turned, grads, out, left, *rights):
+    clips = turned.shape[0]
+    shards = grads.shape[1]
+    block = height * columns
+    place = lax.broadcasted_iota(jnp.int32, (1, block), 1)
+    row, column = place // columns, place % columns
+
+    def one_clip(clip, base):
+        length = lengths[clip]
+
+        def one_frame(t, at):
+            here = pl.ds(pl.multiple_of(t * block, block), block)
+            there = pl.ds(pl.multiple_of(at * block, block), block)
+            image = turned[clip, :, here].astype(f32)
+            for dr in range(3):
+                for dw in range(3):
+                    offset = (dr - 1) * columns + dw - 1
+                    moved = pltpu.roll(image, -offset % block, 1) if offset else image
+                    if dr == 0:
+                        moved = jnp.where(row > 0, moved, 0.0)
+                    if dr == 2:
+                        moved = jnp.where(row < height - 1, moved, 0.0)
+                    if dw == 0:
+                        moved = jnp.where(column > 0, moved, 0.0)
+                    if dw == 2:
+                        moved = jnp.where(column < columns - 1, moved, 0.0)
+                    tap = dr * 3 + dw
+                    left[tap * LANES : (tap + 1) * LANES, there] = moved.astype(bf16)
+            for j in range(shards):
+                lanes = slice(j * LANES, (j + 1) * LANES)
+                grad = grads[clip, j, here, :]
+                rights[2][there, lanes] = grad
+                rights[1][there, lanes] = jnp.where(t > 0, grad, jnp.zeros_like(grad))
+                rights[0][there, lanes] = jnp.where(t > 1, grad, jnp.zeros_like(grad))
+            return at + 1
+
+        return lax.fori_loop(0, length, one_frame, base)
+
+    lax.fori_loop(0, clips, one_clip, 0)
+    total = left.shape[1]
+    for dt in range(3):
+        skip = (2 - dt) * block
+        product = jnp.dot(
+            left[:, : total - skip], rights[dt][skip:, :], preferred_element_type=f32
+        )
+        out[dt * 9 : (dt + 1) * 9] = product.reshape(9, LANES, product.shape[1])
+
+
+def by_slices(codes, lengths, hidden, embed, conv_weight, gain, bias, cotangent):
+    _, frames, height, width = codes.shape
+    channels = conv_weight.shape[2]
+    shards = lax.axis_size("shard")
+    clips = lax.axis_size("dp")
+    per_group = channels // GROUPS
+    columns = width * shards
+    cells = frames * height
+    rows = cells * columns
+    own_rows = cells * width
+    block = height * columns
+    here = lax.axis_index("shard")
+    info = jnp.stack([lengths[0], here.astype(jnp.int32)])
+    hops = range(1, shards)
+    flat_weight = conv_weight.transpose(1, 0, 2).reshape(27 * LANES, channels)
+
+    chunk = shaped((own_rows, 2 * LANES), bf16)
+    sent = kernel_call(
+        lambda *refs: embed_body(shards, width, height * width, *refs),
+        [chunk] * shards,
+        [
+            info,
+            codes.reshape(own_rows, 1),
+            hidden.reshape(own_rows, channels),
+            jnp.pad(embed, ((0, LANES - CODE_BITS), (0, 0))),
+            cotangent.reshape(rows, LANES),
+        ],
+        [
+            pltpu.VMEM((shards, own_rows, 2 * LANES), bf16),
+            pltpu.VMEM((rows, LANES), f32),
+            pltpu.VMEM((own_rows, LANES), f32),
+        ],
+        flops=2 * own_rows * LANES * channels,
+    )
+    code_row = codes.reshape(1, own_rows)
+    all_codes = [code_row] + [swap(code_row, hop) for hop in hops]
+    parts = [sent[0]] + [swap(sent[hop], hop) for hop in hops]
+
+    slab = shaped((rows, LANES), bf16)
+    forward = kernel_call(
+        lambda *refs: forward_body(shards, width, frames, height, *refs),
+        [shaped((rows, LANES), f32)] + [slab] * (shards - 1)
+        + [slab, shaped((LANES, rows), bf16), slab],
+        [info, *parts, flat_weight],
+        [
+            pltpu.VMEM((shards, 2, own_rows, LANES), f32),
+            pltpu.VMEM((rows, LANES), f32),
+            pltpu.VMEM((rows, LANES), f32),
+            pltpu.VMEM((3, frames + 2, height + 2, columns, LANES), bf16),
+            pltpu.VMEM((rows, 27 * LANES), bf16),
+            pltpu.VMEM((shards, rows, LANES), f32),
+        ],
+        flops=2 * rows * 27 * LANES * channels,
+    )
+    own_sum, sum_sends = forward[0], forward[1:shards]
+    turned, cot_slab = forward[shards + 1], forward[shards + 2]
+    all_turned = lax.all_gather(turned, "dp", axis=0)
+    all_lengths = lax.all_gather(lengths, "dp", axis=0, tiled=True)
+    sum_parts = [swap(sum_sends[hop - 1], hop) for hop in hops]
+
+    small = shaped((own_rows, LANES), bf16)
+    normed = kernel_call(
+        lambda *refs: norm_body(shards, width, frames, height, per_group, *refs),
+        [slab, shaped((8, LANES), f32)] + [small] * shards,
+        [
+            info,
+            own_sum,
+            *sum_parts,
+            lax.dynamic_slice_in_dim(gain, here * LANES, LANES).reshape(1, LANES),
+            lax.dynamic_slice_in_dim(bias, here * LANES, LANES).reshape(1, LANES),
+            cot_slab,
+        ],
+        [pltpu.VMEM((rows, LANES), f32)] * 3 + [pltpu.VMEM((shards, own_rows, LANES), f32)],
+        flops=rows * LANES * 40,
+    )
+    d_conv, terms, act_sends = normed[0], normed[1], normed[2:]
+    d_parts = [d_conv] + [swap(d_conv, hop) for hop in hops]
+    all_grads = lax.all_gather(d_conv, ("dp", "shard"), axis=0).reshape(
+        clips, shards, rows, LANES
+    )
+    act_parts = [act_sends[0]] + [swap(act_sends[hop], hop) for hop in hops]
+
+    back = kernel_call(
+        lambda *refs: input_grad_body(shards, width, frames, height, *refs),
+        [shaped((32, LANES), f32)] + [small] * shards,
+        [info, *d_parts, flat_weight, *all_codes],
+        [
+            pltpu.VMEM((shards, rows, LANES), bf16),
+            pltpu.VMEM((rows, channels), bf16),
+            pltpu.VMEM((3, frames, height, columns, LANES), f32),
+            pltpu.VMEM((shards, own_rows, LANES), f32),
+        ],
+        flops=2 * rows * 27 * LANES * channels,
+    )
+    embed_term, hidden_sends = back[0], back[1:]
+    hidden_parts = [hidden_sends[0]] + [swap(hidden_sends[hop], hop) for hop in hops]
+    grad_hidden = kernel_call(
+        lambda *refs: hidden_body(shards, *refs),
+        [shaped((own_rows, channels), bf16)],
+        [info, *hidden_parts],
+        [pltpu.VMEM((shards, own_rows, LANES), bf16)],
+    )[0]
+    decoded = kernel_call(
+        lambda *refs: decoded_body(shards, width, *refs),
+        [slab],
+        [info, *act_parts],
+        [pltpu.VMEM((shards, own_rows, LANES), f32), pltpu.VMEM((rows, LANES), f32)],
+    )[0]
+    valid = 3 * clips * block
+    grad_weight = kernel_call(
+        lambda *refs: weight_grad_body(frames, height, columns, *refs),
+        [shaped((27, LANES, channels), f32)],
+        [all_lengths, all_turned, all_grads],
+        [pltpu.VMEM((9 * LANES, valid), bf16)] + [pltpu.VMEM((valid, channels), bf16)] * 3,
+        flops=2 * valid * 27 * LANES * channels,
+    )[0]
+    grad_conv = grad_weight.transpose(1, 0, 2)
+
+    small_sum = lax.psum(jnp.concatenate([embed_term, terms], axis=0), "dp")
+    all_small = lax.all_gather(small_sum, "shard", axis=1, tiled=True)
+    return (
+        decoded.reshape(1, frames, 2 * height, 2 * width, LANES),
+        grad_hidden.reshape(1, frames, height, width, channels),
+        grad_conv,
+        all_small[:CODE_BITS],
+        all_small[32],
+        all_small[33],
+    )
 
 
 def extended(block, sides, width):
@@ -63,7 +505,7 @@
     return jnp.concatenate(forward_taps(padded, frames, height, slab_width), axis=3)
 
 
-def on_device(codes, lengths, hidden, embed, conv_weight, gain, bias, cotangent):
+def by_gathers(codes, lengths, hidden, embed, conv_weight, gain, bias, cotangent):
     frames = codes.shape[1]
     height = codes.shape[2]
     width = codes.shape[3]
@@ -172,6 +614,13 @@
     return (decoded, grad_hidden[None], grad_conv, grad_embed, grad_gain, grad_bias)
 
 
+def on_device(codes, lengths, hidden, embed, conv_weight, gain, bias, cotangent):
+    share = conv_weight.shape[0]
+    block = codes.shape[2] * codes.shape[3] * lax.axis_size("shard")
+    plan = by_slices if share == LANES and block == LANES else by_gathers
+    return plan(codes, lengths, hidden, embed, conv_weight, gain, bias, cotangent)
+
+
 def solution(mesh):
     return jax.shard_map(
         on_device,

time: 300 us -> 170 us (0.57)
  waiting for transfers between devices: 111 us -> 32.2 us
  local copies, waits for them, and re-layouts: 63 us -> 13.4 us
  Pallas kernels: 0 us -> 42.5 us
  matrix products: 22.2 us -> 0 us
  other arithmetic: 12.1 us -> 1.37 us
  blocking collectives: 62.4 us -> 52.4 us
    psum x1 -> x0, waiting for transfers between devices: 83.3 us -> none  [on_device(): lax.psum(weight_sum.astype(jnp.bfloat16), 'dp').astype(jnp.float32)]
    pallas_call x0 -> x7, Pallas kernels: none -> 42.5 us  [kernel_call(): pl.pallas_call(body, out_shape=outs, in_specs=specs, out_specs=[pl.BlockS...]
    unnamed x82 -> x46, local copies, waits for them, and re-layouts: 43.2 us -> 5.41 us
    dot_general x5 -> x0, matrix products: 22.2 us -> none  [the longest x1 8.81 us: on_device(): jnp.einsum('frwtn,ntc->frwc', own_patches, lax.all_gather(conv_weight, 's...]
    psum x3 -> x1, blocking collectives: 54.3 us -> 34.4 us  [by_slices(): small_sum = lax.psum(jnp.concatenate([embed_term, terms], axis=0), 'dp')]
    ppermute x2 -> x18, waiting for transfers between devices: 0.01 us -> 18.8 us  [swap(): return lax.ppermute(block, 'shard', pairs)]
    unnamed x0 -> x1, blocking collectives: none -> 12.5 us
    all_to_all x2 -> x0, starting transfers between devices: 9.49 us -> none  [the longest x1 6.15 us: on_device(): lax.all_to_all(features, 'shard', split_axis=3, concat_axis=2, tiled=True)]
  transfers between devices with their start and end apart: 6 -> 20, of which waited for: 3 -> 7; matrix products, arithmetic and copies ran while one was open for 24% -> 4% of each run, Pallas kernels for 0% -> 7%
where the time goes in v1:
time: 170 us; the launch traced here: 169 us
  blocking collectives  52.4 us (31%)
  Pallas kernels  42.5 us (25%)
  waiting for transfers between devices  32.2 us (19%)
  between operations  14.9 us (9%)
  local copies, waits for them, and re-layouts  13.4 us (8%)
  starting transfers between devices  12.6 us (7%)
    pallas_call x7, Pallas kernels, kernel_call(): pl.pallas_call(body, out_shape=outs, in_specs=specs, out_specs=[pl.BlockS...  42.5 us
    psum x1, blocking collectives, by_slices(): small_sum = lax.psum(jnp.concatenate([embed_term, terms], axis=0), 'dp')  34.4 us
    ppermute x18, waiting for transfers between devices, swap(): return lax.ppermute(block, 'shard', pairs)  18.8 us
    all_gather x1, waiting for transfers between devices, by_slices(): lax.all_gather(d_conv, ('dp', 'shard'), axis=0)  13.4 us
    ppermute x18, starting transfers between devices, swap(): return lax.ppermute(block, 'shard', pairs)  12.5 us
    unnamed x1, blocking collectives  12.5 us
    all_gather x1, blocking collectives, by_slices(): all_small = lax.all_gather(small_sum, 'shard', axis=1, tiled=True)  5.46 us
    unnamed x46, local copies, waits for them, and re-layouts  5.41 us
  transfers between devices with their start and end apart: 20, of which 7 were waited for; matrix products, arithmetic and copies ran while one was open for 4% of the time, Pallas kernels for 7%

profile of v1, /device:TPU:0, one launch (start us, length us, event | category | flops | bytes accessed | tf_op | source)
XLA Modules:
  0.0 169.3 jit_solution(5828553215040667095)
XLA Ops:
  7.9 0.8 copy.16
  8.7 0.7 reshape.60.refs_1_
  9.4 1.6 reshape.43.refs_2_
  11.0 0.6 pad_add_fusion.refs_0_
  11.7 1.4 pad.4.refs_3_
  13.1 2.2 %shard_map.127 = (bf16[160,256]{1,0:T(8,128)(2,1)}, bf16[160,256]{1,0:T(8,128)(2,1)}, bf16[160,256]{1,0:T(8,128)(2,1)}, bf16[160,256]{1,0:T(8,128)(2,1)}) custom-call(s32[2]{0:T(128)} %pad_add_fusion.refs_0_, s32[160,1]{1,0:T(8,128)} %reshape.60.refs_1_, bf16[160,512]{1,0:T(8,128)(2,1)} %reshape.43.refs_2_, bf16[128,512]{1,0:T(8,128)(2,1)} %pad.4.refs_3_, ...), custom_call_target="tpu_custom_call" | custom-call | flops 20971520 | bytes 787080 | tf_op jit(solution)/shard_map/pallas_call | solution.py:24
  15.2 0.5 collective-permute-start
  15.7 2.6 %collective-permute-start.1 = (bf16[160,256]{1,0:T(8,128)(2,1)}, bf16[160,256]{1,0:T(8,128)(2,1)S(1)}, u32[]{:S(2)}, u32[]{:S(2)}) collective-permute-start(bf16[160,256]{1,0:T(8,128)(2,1)} %get-tuple-element.29), channel_id=1, source_target_pairs={{0,2},{1,3},{2,0},{3,1},{4,6},{5,7},{6,4},{7,5},{8,10},{9,11},{10,... | collective-permute-start | bytes 245768 | tf_op jit(solution)/shard_map/ppermute | solution.py:42
  18.2 0.1 collective-permute-start.2
  18.3 3.2 %collective-permute-done.1.refs_3_ = bf16[160,256]{1,0:T(8,128)(2,1)S(1)} collective-permute-done((bf16[160,256]{1,0:T(8,128)(2,1)}, bf16[160,256]{1,0:T(8,128)(2,1)S(1)}, u32[]{:S(2)}, u32[]{:S(2)}) %collective-permute-start.1) | collective-permute-done | bytes 81952 | tf_op jit(solution)/shard_map/ppermute | solution.py:42
  21.5 1.4 collective-permute-done.2.refs_4_
  23.0 0.6 copy-done.16
  23.6 6.2 %shard_map.128 = (f32[640,128]{1,0:T(8,128)}, bf16[640,128]{1,0:T(8,128)(2,1)}, bf16[640,128]{1,0:T(8,128)(2,1)}, bf16[640,128]{1,0:T(8,128)(2,1)}, bf16[640,128...) custom-call(s32[2]{0:T(128)} %pad_add_fusion.refs_0_, ...), custom_call_target="tpu_custom_call" | custom-call | flops 2264924160 | bytes 5177352 | tf_op jit(solution)/shard_map/pallas_call | solution.py:24
  29.9 0.2 collective-permute-start.3
  30.1 1.7 %collective-permute-start.4 = (bf16[640,128]{1,0:T(8,128)(2,1)}, bf16[640,128]{1,0:T(8,128)(2,1)S(1)}, u32[]{:S(2)}, u32[]{:S(2)}) collective-permute-start(bf16[640,128]{1,0:T(8,128)(2,1)} %get-tuple-element.33), channel_id=1, source_target_pairs={{0,2},{1,3},{2,0},{3,1},{4,6},{5,7},{6,4},{7,5},{8,10},{9,11},{10,... | collective-permute-start | bytes 491528 | tf_op jit(solution)/shard_map/ppermute | solution.py:42
  31.8 1.3 dynamic-slice_bitcast_fusion
  33.1 4.1 %collective-permute-done.4.refs_3_ = bf16[640,128]{1,0:T(8,128)(2,1)S(1)} collective-permute-done((bf16[640,128]{1,0:T(8,128)(2,1)}, bf16[640,128]{1,0:T(8,128)(2,1)S(1)}, u32[]{:S(2)}, u32[]{:S(2)}) %collective-permute-start.4) | collective-permute-done | bytes 163872 | tf_op jit(solution)/shard_map/ppermute | solution.py:42
  37.3 2.6 %collective-permute-done.5.refs_4_ = bf16[640,128]{1,0:T(8,128)(2,1)S(1)} collective-permute-done((bf16[640,128]{1,0:T(8,128)(2,1)}, bf16[640,128]{1,0:T(8,128)(2,1)S(1)}, u32[]{:S(2)}, u32[]{:S(2)}) %collective-permute-start.5) | collective-permute-done | bytes 163872 | tf_op jit(solution)/shard_map/ppermute | solution.py:42
  39.9 0.7 copy-done.2
  40.5 3.0 %shard_map.129 = (bf16[640,128]{1,0:T(8,128)(2,1)}, f32[8,128]{1,0:T(8,128)}, bf16[160,128]{1,0:T(8,128)(2,1)}, bf16[160,128]{1,0:T(8,128)(2,1)}, bf16[160,128]{1,0:T(8,128)(2,1)}, /*index=5*/bf16[160,128]{1,0:T(8,128)(2,1)}) custom-call(s32[2]{0:T(128)} %pad_add_fusion.refs_0_, f32[640,128]{1,0:T(8,128)} %get-tuple-element.31.refs_1_, ...), custom_call_target="tpu_custom_call" | custom-call | flops 3276800 | bytes 1315848 | tf_op jit(solution)/shard_map/pallas_call | solution.py:24
  43.5 0.4 collective-permute-start.9
  43.9 1.6 collective-permute-start.10
  45.5 0.5 collective-permute-start.6
  46.0 0.1 reshape.49.refs_6_
  46.2 1.1 collective-permute-done.12.refs_7_
  47.3 1.6 collective-permute-start.7
  48.9 6.3 %collective-permute-done.7.refs_3_ = bf16[160,128]{1,0:T(8,128)(2,1)S(1)} collective-permute-done((bf16[160,128]{1,0:T(8,128)(2,1)}, bf16[160,128]{1,0:T(8,128)(2,1)S(1)}, u32[]{:S(2)}, u32[]{:S(2)}) %collective-permute-start.7) | collective-permute-done | bytes 40992 | tf_op jit(solution)/shard_map/ppermute | solution.py:42
  55.2 1.4 collective-permute-start.13
  56.7 0.6 dynamic-slice
  57.3 0.8 dynamic-update-slice
  58.0 12.5 %all-reduce.1.refs_0_ = s32[8]{0:T(128)} all-reduce(s32[8]{0:T(128)S(1)} %dynamic-update-slice), channel_id=1, replica_groups=mesh['dp'=8,'shard'=4] {'dp'}, use_global_device_ids=true, to_apply=%add.1 | all-reduce | flops 8 | bytes 64
  70.5 1.7 %shard_map.130 = bf16[640,128]{1,0:T(8,128)(2,1)} custom-call(s32[2]{0:T(128)} %pad_add_fusion.refs_0_, bf16[160,128]{1,0:T(8,128)(2,1)} %get-tuple-element.36.refs_1_, bf16[160,128]{1,0:T(8,128)(2,1)} %copy-done.3, bf16[160,128]{1,0:T(8,128)(2,1)} %copy-done.4, bf16[160,128]{1,0:T(8,128)(2,1)} %copy-done.5), custom_call_target="tpu_custom_call" | custom-call | bytes 327688 | tf_op jit(solution)/shard_map/pallas_call | solution.py:24
  72.3 0.5 copy-done.18
  72.8 0.1 copy-done.11
  73.0 0.7 copy-done.13
  73.6 5.9 %shard_map.131 = (f32[32,128]{1,0:T(8,128)}, bf16[160,128]{1,0:T(8,128)(2,1)}, bf16[160,128]{1,0:T(8,128)(2,1)}, bf16[160,128]{1,0:T(8,128)(2,1)}, bf16[160,128]{1,0:T(8,128)(2,1)}) custom-call(s32[2]{0:T(128)} %pad_add_fusion.refs_0_, bf16[640,128]{1,0:T(8,128)(2,1)} %get-tuple-element.40.refs_1_, bf16[640,128]{1,0:T(8,128)(2,1)} %copy-done.11, ...), custom_call_target="tpu_custom_call" | custom-call | flops 2264924160 | bytes 4377096 | tf_op jit(solution)/shard_map/pallas_call | solution.py:24
  79.5 0.6 collective-permute-start.16
  80.2 1.2 collective-permute-start.17
  81.4 0.7 pad_maximum_fusion
  82.1 34.4 %psum.7 = f32[40,128]{1,0:T(8,128)S(1)} all-reduce(f32[40,128]{1,0:T(8,128)S(1)} %pad_maximum_fusion), channel_id=1, replica_groups=mesh['dp'=8,'shard'=4] {'dp'}, use_global_device_ids=true, to_apply=%region_0.1 | all-reduce | flops 5120 | bytes 40960 | tf_op jit(solution)/shard_map/psum | solution.py:443
  116.5 5.5 %all_gather.23 = f32[40,512]{1,0:T(8,128)S(1)} all-gather(f32[40,128]{1,0:T(8,128)S(1)} %psum.7), channel_id=1, replica_groups=mesh['dp'=8,'shard'=4] {'shard'}, dimensions={1}, use_global_device_ids=true | all-gather | bytes 102400 | tf_op jit(solution)/shard_map/all_gather | solution.py:444
  122.0 0.6 fusion
  122.6 0.6 slice.12
  123.3 0.6 copy-done.6
  123.9 1.6 shard_map.132
  125.4 1.6 reshape.50
  127.1 13.4 %all-gather.7.cloned.1.call-done = bf16[20480,128]{1,0:T(8,128)(2,1)} async-done(((bf16[640,128]{1,0:T(8,128)(2,1)}), bf16[20480,128]{1,0:T(8,128)(2,1)}) %all-gather.7.cloned.1.call-update) | async-done | bytes 5242896 | tf_op jit(solution)/shard_map/all_gather | solution.py:402
  140.5 22.0 %shard_map.133 = f32[27,128,512]{2,1,0:T(8,128)} custom-call(s32[8]{0:T(128)} %all-reduce.1.refs_0_, bf16[8,128,640]{2,1,0:T(8,128)(2,1)} %bitcast.27, bf16[8,4,640,128]{3,2,1,0:T(8,128)(2,1)} %bitcast.24), custom_call_target="tpu_custom_call" | custom-call | flops 10871635968 | bytes 13631520 | tf_op jit(solution)/shard_map/pallas_call | solution.py:24
  (60 shorter events, 0.5 us)
Async XLA Ops:
  7.2 119.9 %all-gather.5.cloned.1.call-start = ((), (), s32[]{:S(2)}) async-start(), calls=%async_computation | async-start | bytes 1474560 | tf_op jit(solution)/shard_map/all_gather | solution.py:381
  11.0 45.7 %copy-start.20 = (u32[32]{0:T(128)S(1)}, u32[32]{0:T(128)}, u32[]{:S(2)}) copy-start(u32[32]{0:T(128)} %constant.20) | copy-start | bytes 388
  15.2 3.1 %collective-permute-start = (bf16[160,256]{1,0:T(8,128)(2,1)}, bf16[160,256]{1,0:T(8,128)(2,1)S(1)}, u32[]{:S(2)}, u32[]{:S(2)}) collective-permute-start(bf16[160,256]{1,0:T(8,128)(2,1)} %get-tuple-element.28), channel_id=1, source_target_pairs={{0,1},{1,0},{2,3},{3,2},{4,5},{5,4},{6,7},{7,6},{8,9},{9,8},{10,11... | collective-permute-start | bytes 245768 | tf_op jit(solution)/shard_map/ppermute | solution.py:42
  15.7 5.9 %collective-permute-start.1 = (bf16[160,256]{1,0:T(8,128)(2,1)}, bf16[160,256]{1,0:T(8,128)(2,1)S(1)}, u32[]{:S(2)}, u32[]{:S(2)}) collective-permute-start(bf16[160,256]{1,0:T(8,128)(2,1)} %get-tuple-element.29), channel_id=1, source_target_pairs={{0,2},{1,3},{2,0},{3,1},{4,6},{5,7},{6,4},{7,5},{8,10},{9,11},{10,... | collective-permute-start | bytes 245768 | tf_op jit(solution)/shard_map/ppermute | solution.py:42
  18.2 4.8 %collective-permute-start.2 = (bf16[160,256]{1,0:T(8,128)(2,1)}, bf16[160,256]{1,0:T(8,128)(2,1)S(1)}, u32[]{:S(2)}, u32[]{:S(2)}) collective-permute-start(bf16[160,256]{1,0:T(8,128)(2,1)} %get-tuple-element.30), channel_id=1, source_target_pairs={{0,3},{1,2},{2,1},{3,0},{4,7},{5,6},{6,5},{7,4},{8,11},{9,10},{10,... | collective-permute-start | bytes 245768 | tf_op jit(solution)/shard_map/ppermute | solution.py:42
  18.3 4.6 %copy-start.14 = (bf16[160,256]{1,0:T(8,128)(2,1)}, bf16[160,256]{1,0:T(8,128)(2,1)S(1)}, u32[]{:S(2)}) copy-start(bf16[160,256]{1,0:T(8,128)(2,1)S(1)} %collective-permute-done.refs_2_) | copy-start | bytes 245764
  21.5 1.5 copy-start.15
  23.0 0.6 copy-start.16
  29.8 110.6 %all-gather.7.cloned.1.call-start = ((), (), s32[]{:S(2)}) async-start(), calls=%async_computation.1 | async-start | bytes 5406720 | tf_op jit(solution)/shard_map/all_gather | solution.py:402
  29.9 3.2 %collective-permute-start.3 = (bf16[640,128]{1,0:T(8,128)(2,1)}, bf16[640,128]{1,0:T(8,128)(2,1)S(1)}, u32[]{:S(2)}, u32[]{:S(2)}) collective-permute-start(bf16[640,128]{1,0:T(8,128)(2,1)} %get-tuple-element.32), channel_id=1, source_target_pairs={{0,1},{1,0},{2,3},{3,2},{4,5},{5,4},{6,7},{7,6},{8,9},{9,8},{10,11... | collective-permute-start | bytes 491528 | tf_op jit(solution)/shard_map/ppermute | solution.py:42
  30.1 7.2 %collective-permute-start.4 = (bf16[640,128]{1,0:T(8,128)(2,1)}, bf16[640,128]{1,0:T(8,128)(2,1)S(1)}, u32[]{:S(2)}, u32[]{:S(2)}) collective-permute-start(bf16[640,128]{1,0:T(8,128)(2,1)} %get-tuple-element.33), channel_id=1, source_target_pairs={{0,2},{1,3},{2,0},{3,1},{4,6},{5,7},{6,4},{7,5},{8,10},{9,11},{10,... | collective-permute-start | bytes 491528 | tf_op jit(solution)/shard_map/ppermute | solution.py:42
  31.8 8.0 %collective-permute-start.5 = (bf16[640,128]{1,0:T(8,128)(2,1)}, bf16[640,128]{1,0:T(8,128)(2,1)S(1)}, u32[]{:S(2)}, u32[]{:S(2)}) collective-permute-start(bf16[640,128]{1,0:T(8,128)(2,1)} %get-tuple-element.34), channel_id=1, source_target_pairs={{0,3},{1,2},{2,1},{3,0},{4,7},{5,6},{6,5},{7,4},{8,11},{9,10},{10,... | collective-permute-start | bytes 491528 | tf_op jit(solution)/shard_map/ppermute | solution.py:42
  33.1 6.7 %copy-start = (bf16[640,128]{1,0:T(8,128)(2,1)}, bf16[640,128]{1,0:T(8,128)(2,1)S(1)}, u32[]{:S(2)}) copy-start(bf16[640,128]{1,0:T(8,128)(2,1)S(1)} %collective-permute-done.3.refs_2_) | copy-start | bytes 491524
  37.3 2.6 %copy-start.1 = (bf16[640,128]{1,0:T(8,128)(2,1)}, bf16[640,128]{1,0:T(8,128)(2,1)S(1)}, u32[]{:S(2)}) copy-start(bf16[640,128]{1,0:T(8,128)(2,1)S(1)} %collective-permute-done.4.refs_3_) | copy-start | bytes 491524
  39.8 0.7 copy-start.2
  43.5 37.9 %copy-start.9 = (f32[8,128]{1,0:T(8,128)S(1)}, f32[8,128]{1,0:T(8,128)}, u32[]{:S(2)}) copy-start(f32[8,128]{1,0:T(8,128)} %get-tuple-element.47) | copy-start | bytes 12292
  43.5 28.8 %collective-permute-start.9 = (bf16[640,128]{1,0:T(8,128)(2,1)}, bf16[640,128]{1,0:T(8,128)(2,1)S(1)}, u32[]{:S(2)}, u32[]{:S(2)}) collective-permute-start(bf16[640,128]{1,0:T(8,128)(2,1)} %get-tuple-element.40.refs_1_), channel_id=1, source_target_pairs={{0,1},{1,0},{2,3},{3,2},{4,5},{5,4},{6,7},{7,6},{8,9},{9,8},{10,11... | collective-permute-start | bytes 491528 | tf_op jit(solution)/shard_map/ppermute | solution.py:42
  43.9 28.4 %collective-permute-start.10 = (bf16[640,128]{1,0:T(8,128)(2,1)}, bf16[640,128]{1,0:T(8,128)(2,1)S(1)}, u32[]{:S(2)}, u32[]{:S(2)}) collective-permute-start(bf16[640,128]{1,0:T(8,128)(2,1)} %get-tuple-element.40.refs_1_), channel_id=1, source_target_pairs={{0,2},{1,3},{2,0},{3,1},{4,6},{5,7},{6,4},{7,5},{8,10},{9,11},{10,... | collective-permute-start | bytes 491528 | tf_op jit(solution)/shard_map/ppermute | solution.py:42
  45.4 26.9 %collective-permute-start.11 = (bf16[640,128]{1,0:T(8,128)(2,1)}, bf16[640,128]{1,0:T(8,128)(2,1)S(1)}, u32[]{:S(2)}, u32[]{:S(2)}) collective-permute-start(bf16[640,128]{1,0:T(8,128)(2,1)} %get-tuple-element.40.refs_1_), channel_id=1, source_target_pairs={{0,3},{1,2},{2,1},{3,0},{4,7},{5,6},{6,5},{7,4},{8,11},{9,10},{10,... | collective-permute-start | bytes 491528 | tf_op jit(solution)/shard_map/ppermute | solution.py:42
  45.5 3.5 %collective-permute-start.6 = (bf16[160,128]{1,0:T(8,128)(2,1)}, bf16[160,128]{1,0:T(8,128)(2,1)S(1)}, u32[]{:S(2)}, u32[]{:S(2)}) collective-permute-start(bf16[160,128]{1,0:T(8,128)(2,1)} %get-tuple-element.37), channel_id=1, source_target_pairs={{0,1},{1,0},{2,3},{3,2},{4,5},{5,4},{6,7},{7,6},{8,9},{9,8},{10,11... | collective-permute-start | bytes 122888 | tf_op jit(solution)/shard_map/ppermute | solution.py:42
  46.1 26.2 %copy-start.10 = (s32[1,160]{1,0:T(1,128)}, s32[1,160]{1,0:T(1,128)S(1)}, u32[]{:S(2)}) copy-start(s32[1,160]{1,0:T(1,128)S(1)} %reshape.49.refs_6_) | copy-start | bytes 1924
  46.1 1.2 collective-permute-start.12
  47.3 25.0 %copy-start.17 = (s32[1,160]{1,0:T(1,128)}, s32[1,160]{1,0:T(1,128)S(1)}, u32[]{:S(2)}) copy-start(s32[1,160]{1,0:T(1,128)S(1)} %collective-permute-done.12.refs_7_) | copy-start | bytes 1924
  47.3 7.9 %collective-permute-start.7 = (bf16[160,128]{1,0:T(8,128)(2,1)}, bf16[160,128]{1,0:T(8,128)(2,1)S(1)}, u32[]{:S(2)}, u32[]{:S(2)}) collective-permute-start(bf16[160,128]{1,0:T(8,128)(2,1)} %get-tuple-element.38), channel_id=1, source_target_pairs={{0,2},{1,3},{2,0},{3,1},{4,6},{5,7},{6,4},{7,5},{8,10},{9,11},{10,... | collective-permute-start | bytes 122888 | tf_op jit(solution)/shard_map/ppermute | solution.py:42
  48.9 21.6 %copy-start.3 = (bf16[160,128]{1,0:T(8,128)(2,1)}, bf16[160,128]{1,0:T(8,128)(2,1)S(1)}, u32[]{:S(2)}) copy-start(bf16[160,128]{1,0:T(8,128)(2,1)S(1)} %collective-permute-done.6.refs_2_) | copy-start | bytes 122884
  48.9 7.7 %collective-permute-start.8 = (bf16[160,128]{1,0:T(8,128)(2,1)}, bf16[160,128]{1,0:T(8,128)(2,1)S(1)}, u32[]{:S(2)}, u32[]{:S(2)}) collective-permute-start(bf16[160,128]{1,0:T(8,128)(2,1)} %get-tuple-element.39), channel_id=1, source_target_pairs={{0,3},{1,2},{2,1},{3,0},{4,7},{5,6},{6,5},{7,4},{8,11},{9,10},{10,... | collective-permute-start | bytes 122888 | tf_op jit(solution)/shard_map/ppermute | solution.py:42
  55.2 15.3 %copy-start.4 = (bf16[160,128]{1,0:T(8,128)(2,1)}, bf16[160,128]{1,0:T(8,128)(2,1)S(1)}, u32[]{:S(2)}) copy-start(bf16[160,128]{1,0:T(8,128)(2,1)S(1)} %collective-permute-done.7.refs_3_) | copy-start | bytes 122884
  55.2 17.0 %collective-permute-start.13 = (s32[1,160]{1,0:T(1,128)S(1)}, s32[1,160]{1,0:T(1,128)S(1)}, u32[]{:S(2)}, u32[]{:S(2)}) collective-permute-start(s32[1,160]{1,0:T(1,128)S(1)} %reshape.49.refs_6_), channel_id=1, source_target_pairs={{0,2},{1,3},{2,0},{3,1},{4,6},{5,7},{6,4},{7,5},{8,10},{9,11},{10,... | collective-permute-start | bytes 1928 | tf_op jit(solution)/shard_map/ppermute | solution.py:42
  56.7 13.9 %copy-start.5 = (bf16[160,128]{1,0:T(8,128)(2,1)}, bf16[160,128]{1,0:T(8,128)(2,1)S(1)}, u32[]{:S(2)}) copy-start(bf16[160,128]{1,0:T(8,128)(2,1)S(1)} %collective-permute-done.8.refs_4_) | copy-start | bytes 122884
  56.7 15.6 %collective-permute-start.14 = (s32[1,160]{1,0:T(1,128)S(1)}, s32[1,160]{1,0:T(1,128)S(1)}, u32[]{:S(2)}, u32[]{:S(2)}) collective-permute-start(s32[1,160]{1,0:T(1,128)S(1)} %reshape.49.refs_6_), channel_id=1, source_target_pairs={{0,3},{1,2},{2,1},{3,0},{4,7},{5,6},{6,5},{7,4},{8,11},{9,10},{10,... | collective-permute-start | bytes 1928 | tf_op jit(solution)/shard_map/ppermute | solution.py:42
  72.2 0.6 copy-start.18
  72.2 0.6 copy-start.19
  72.3 0.7 copy-start.11
  72.3 0.7 copy-start.12
  73.0 0.7 copy-start.13
  79.5 43.7 %collective-permute-start.15 = (bf16[160,128]{1,0:T(8,128)(2,1)}, bf16[160,128]{1,0:T(8,128)(2,1)S(1)}, u32[]{:S(2)}, u32[]{:S(2)}) collective-permute-start(bf16[160,128]{1,0:T(8,128)(2,1)} %get-tuple-element.42), channel_id=1, source_target_pairs={{0,1},{1,0},{2,3},{3,2},{4,5},{5,4},{6,7},{7,6},{8,9},{9,8},{10,11... | collective-permute-start | bytes 122888 | tf_op jit(solution)/shard_map/ppermute | solution.py:42
  79.5 43.7 %collective-permute-start.16 = (bf16[160,128]{1,0:T(8,128)(2,1)}, bf16[160,128]{1,0:T(8,128)(2,1)S(1)}, u32[]{:S(2)}, u32[]{:S(2)}) collective-permute-start(bf16[160,128]{1,0:T(8,128)(2,1)} %get-tuple-element.43), channel_id=1, source_target_pairs={{0,2},{1,3},{2,0},{3,1},{4,6},{5,7},{6,4},{7,5},{8,10},{9,11},{10,... | collective-permute-start | bytes 122888 | tf_op jit(solution)/shard_map/ppermute | solution.py:42
  80.2 43.1 %collective-permute-start.17 = (bf16[160,128]{1,0:T(8,128)(2,1)}, bf16[160,128]{1,0:T(8,128)(2,1)S(1)}, u32[]{:S(2)}, u32[]{:S(2)}) collective-permute-start(bf16[160,128]{1,0:T(8,128)(2,1)} %get-tuple-element.44), channel_id=1, source_target_pairs={{0,3},{1,2},{2,1},{3,0},{4,7},{5,6},{6,5},{7,4},{8,11},{9,10},{10,... | collective-permute-start | bytes 122888 | tf_op jit(solution)/shard_map/ppermute | solution.py:42
  123.2 0.6 copy-start.6
  123.2 0.6 copy-start.7
  123.2 0.6 copy-start.8
Sparse Core Ops, SparseCore 0:
  30.0 43.4 all-gather.4
  76.3 64.1 all-gather.6

commit v2 on v1

--- a/solution.py
+++ b/solution.py
@@ -8,6 +8,7 @@
 CODE_BITS = 18
 GROUPS = 32
 LANES = 128
+LENGTH_ROWS = 16
 VMEM_BYTES = 56 * 1024 * 1024
 
 eps_norm = 1e-05
@@ -92,7 +93,8 @@
     cot_out[...] = cot[...].astype(bf16)
     middle = slab[...]
     slab_out[...] = middle.astype(bf16)
-    turned_out[...] = middle.T.astype(bf16)
+    turned_out[:LANES, :] = middle.T.astype(bf16)
+    turned_out[LANES:, :] = jnp.full((LENGTH_ROWS, rows), info[0].astype(f32)).astype(bf16)
     column = lax.broadcasted_iota(jnp.int32, (rows, 1), 0) % columns
     rims[...] = jnp.zeros_like(rims)
     shifted = (
@@ -274,20 +276,40 @@
     out[...] = slab[...].astype(bf16)
 
 
-def weight_grad_body(frames, height, columns, lengths, turned, grads, out, left, *rights):
+def terms_body(shards, info, *rest):
+    parts, (embed_out, gain_out, bias_out) = rest[:shards], rest[shards : shards + 3]
+    pieces = rest[shards + 3]
+    for hop in range(shards):
+        pieces[lax.bitwise_xor(info[1], hop)] = parts[hop][...]
+    for j in range(shards):
+        lanes = slice(j * LANES, (j + 1) * LANES)
+        embed_out[:, lanes] = pieces[j, :CODE_BITS]
+        gain_out[:, lanes] = pieces[j, 32:33]
+        bias_out[:, lanes] = pieces[j, 33:34]
+
+
+def weight_grad_body(frames, height, columns, labels, info, turned, *rest):
+    grads, out = rest[: len(labels)], rest[len(labels)]
+    left, right_two, right_one, right_now, starts = rest[len(labels) + 1 :]
     clips = turned.shape[0]
-    shards = grads.shape[1]
     block = height * columns
     place = lax.broadcasted_iota(jnp.int32, (1, block), 1)
     row, column = place // columns, place % columns
 
-    def one_clip(clip, base):
-        length = lengths[clip]
-
-        def one_frame(t, at):
+    start = jnp.int32(0)
+    for clip in range(clips):
+        starts[clip] = start
+        length = jnp.max(turned[clip, LANES:, :LANES].astype(f32)).astype(jnp.int32)
+        start = start + length
+    starts[clips] = start
+
+    def one_clip(clip, _):
+        base = starts[clip]
+
+        def one_frame(t, _):
             here = pl.ds(pl.multiple_of(t * block, block), block)
-            there = pl.ds(pl.multiple_of(at * block, block), block)
-            image = turned[clip, :, here].astype(f32)
+            there = pl.ds(pl.multiple_of((base + t) * block, block), block)
+            image = turned[clip, :LANES, here].astype(f32)
             for dr in range(3):
                 for dw in range(3):
                     offset = (dr - 1) * columns + dw - 1
@@ -302,24 +324,109 @@
                         moved = jnp.where(column < columns - 1, moved, 0.0)
                     tap = dr * 3 + dw
                     left[tap * LANES : (tap + 1) * LANES, there] = moved.astype(bf16)
-            for j in range(shards):
-                lanes = slice(j * LANES, (j + 1) * LANES)
-                grad = grads[clip, j, here, :]
-                rights[2][there, lanes] = grad
-                rights[1][there, lanes] = jnp.where(t > 0, grad, jnp.zeros_like(grad))
-                rights[0][there, lanes] = jnp.where(t > 1, grad, jnp.zeros_like(grad))
-            return at + 1
-
-        return lax.fori_loop(0, length, one_frame, base)
+            return 0
+
+        return lax.fori_loop(0, starts[clip + 1] - base, one_frame, 0)
 
     lax.fori_loop(0, clips, one_clip, 0)
+    for grad, label in zip(grads, labels):
+        clip, part = piece_origin(info, label, clips)
+        base = starts[clip]
+        lanes = pl.ds(pl.multiple_of(part * LANES, LANES), LANES)
+
+        def one_piece(t, _, grad=grad, base=base, lanes=lanes):
+            here = pl.ds(pl.multiple_of(t * block, block), block)
+            there = pl.ds(pl.multiple_of((base + t) * block, block), block)
+            image = grad[here, :]
+            right_now[there, lanes] = image
+            right_one[there, lanes] = jnp.where(t > 0, image, jnp.zeros_like(image))
+            right_two[there, lanes] = jnp.where(t > 1, image, jnp.zeros_like(image))
+            return 0
+
+        lax.fori_loop(0, starts[clip + 1] - base, one_piece, 0)
     total = left.shape[1]
-    for dt in range(3):
+    for dt, right in enumerate((right_two, right_one, right_now)):
         skip = (2 - dt) * block
         product = jnp.dot(
-            left[:, : total - skip], rights[dt][skip:, :], preferred_element_type=f32
+            left[:, : total - skip], right[skip:, :], preferred_element_type=f32
         )
         out[dt * 9 : (dt + 1) * 9] = product.reshape(9, LANES, product.shape[1])
+
+
+def piece_origin(info, label, clips):
+    kind, hop, partner = label
+    mine = lax.bitwise_xor(info[1], partner)
+    core = lax.bitwise_and(mine, 1)
+    line = lax.rem(info[2] // 2 + clips // 2 - hop, clips // 2)
+    side = lax.rem(info[2], 2)
+    if kind == 0:
+        other_clip, other_part = 0, 0
+    elif kind == 3:
+        other_clip, other_part = 1, 2
+    elif hop == 0:
+        other_clip, other_part = (1, 0) if kind == 1 else (0, 2)
+    elif kind == 1:
+        other_clip, other_part = 1 - core, 2 * core
+    else:
+        other_clip, other_part = core, 2 * (1 - core)
+    return 2 * line + lax.bitwise_xor(side, other_clip), lax.bitwise_xor(mine, other_part)
+
+
+def send(block, target):
+    lines, shards = lax.axis_size("dp") // 2, lax.axis_size("shard")
+    pairs = []
+    for line in range(lines):
+        for side in range(2):
+            for chip in range(shards // 2):
+                for core in range(2):
+                    to_line, to_side, to_chip, to_core = target(line, side, chip, core)
+                    source = (line * 2 + side) * shards + chip * 2 + core
+                    sink = (to_line % lines * 2 + to_side) * shards + to_chip * 2 + to_core
+                    pairs.append((source, sink))
+    return lax.ppermute(block, ("dp", "shard"), pairs)
+
+
+def to_side(line, side, chip, core):
+    return line, 1 - side, chip, core
+
+
+def to_chip(line, side, chip, core):
+    return line, side, 1 - chip, core
+
+
+def to_core(line, side, chip, core):
+    return line, side, chip, 1 - core
+
+
+def to_side_or_chip(line, side, chip, core):
+    return (line, 1 - side, chip, core) if core == 0 else (line, side, 1 - chip, core)
+
+
+def to_chip_or_side(line, side, chip, core):
+    return (line, 1 - side, chip, core) if core == 1 else (line, side, 1 - chip, core)
+
+
+def spread_over_clips(own, other_chip):
+    lines = lax.axis_size("dp") // 2
+    core_zero = lax.axis_index("shard") % 2 == 0
+    held, labels = [], []
+    same = [own]
+    for hop in range(1, lines):
+        same.append(send(own, lambda l, s, c, k, hop=hop: (l + hop, s, c, k)))
+    first = [send(own, to_side)]
+    first += [send(same[hop], to_side_or_chip) for hop in range(1, lines)]
+    second = [other_chip]
+    second += [send(same[hop], to_chip_or_side) for hop in range(1, lines)]
+    third = [send(jnp.where(core_zero, first[0], other_chip), to_chip_or_side)]
+    third += [send(first[hop], to_chip_or_side) for hop in range(1, lines)]
+    for hop in range(lines):
+        for kind, group in enumerate((same, first, second, third)):
+            held.append(group[hop])
+            labels.append((kind, hop, 0))
+            if hop or kind in (1, 3):
+                held.append(send(group[hop], to_core))
+                labels.append((kind, hop, 1))
+    return held, labels
 
 
 def by_slices(codes, lengths, hidden, embed, conv_weight, gain, bias, cotangent):
@@ -334,7 +441,7 @@
     own_rows = cells * width
     block = height * columns
     here = lax.axis_index("shard")
-    info = jnp.stack([lengths[0], here.astype(jnp.int32)])
+    info = jnp.stack([lengths[0], here, lax.axis_index("dp")])
     hops = range(1, shards)
     flat_weight = conv_weight.transpose(1, 0, 2).reshape(27 * LANES, channels)
 
@@ -364,7 +471,7 @@
     forward = kernel_call(
         lambda *refs: forward_body(shards, width, frames, height, *refs),
         [shaped((rows, LANES), f32)] + [slab] * (shards - 1)
-        + [slab, shaped((LANES, rows), bf16), slab],
+        + [slab, shaped((LANES + LENGTH_ROWS, rows), bf16), slab],
         [info, *parts, flat_weight],
         [
             pltpu.VMEM((shards, 2, own_rows, LANES), f32),
@@ -379,7 +486,6 @@
     own_sum, sum_sends = forward[0], forward[1:shards]
     turned, cot_slab = forward[shards + 1], forward[shards + 2]
     all_turned = lax.all_gather(turned, "dp", axis=0)
-    all_lengths = lax.all_gather(lengths, "dp", axis=0, tiled=True)
     sum_parts = [swap(sum_sends[hop - 1], hop) for hop in hops]
 
     small = shaped((own_rows, LANES), bf16)
@@ -398,10 +504,11 @@
         flops=rows * LANES * 40,
     )
     d_conv, terms, act_sends = normed[0], normed[1], normed[2:]
-    d_parts = [d_conv] + [swap(d_conv, hop) for hop in hops]
-    all_grads = lax.all_gather(d_conv, ("dp", "shard"), axis=0).reshape(
-        clips, shards, rows, LANES
-    )
+    far = swap(d_conv, 2)
+    d_parts = [d_conv, swap(d_conv, 1), far, swap(far, 1)]
+    grads, labels = spread_over_clips(d_conv, far)
+    grads += [d_parts[1], d_parts[3]]
+    labels += [(0, 0, 1), (2, 0, 1)]
     act_parts = [act_sends[0]] + [swap(act_sends[hop], hop) for hop in hops]
 
     back = kernel_call(
@@ -432,23 +539,35 @@
     )[0]
     valid = 3 * clips * block
     grad_weight = kernel_call(
-        lambda *refs: weight_grad_body(frames, height, columns, *refs),
+        lambda *refs: weight_grad_body(frames, height, columns, labels, *refs),
         [shaped((27, LANES, channels), f32)],
-        [all_lengths, all_turned, all_grads],
-        [pltpu.VMEM((9 * LANES, valid), bf16)] + [pltpu.VMEM((valid, channels), bf16)] * 3,
+        [info, all_turned, *grads],
+        [pltpu.VMEM((9 * LANES, valid), bf16)]
+        + [pltpu.VMEM((valid, channels), bf16)] * 3
+        + [pltpu.SMEM((clips + 1,), jnp.int32)],
         flops=2 * valid * 27 * LANES * channels,
     )[0]
     grad_conv = grad_weight.transpose(1, 0, 2)
 
-    small_sum = lax.psum(jnp.concatenate([embed_term, terms], axis=0), "dp")
-    all_small = lax.all_gather(small_sum, "shard", axis=1, tiled=True)
+    term = jnp.concatenate([embed_term, terms], axis=0)
+    hop = 1
+    while hop < clips:
+        term = term + lax.ppermute(term, "dp", [(i, i ^ hop) for i in range(clips)])
+        hop *= 2
+    term_parts = [term] + [swap(term, hop) for hop in hops]
+    grad_embed, grad_gain, grad_bias = kernel_call(
+        lambda *refs: terms_body(shards, *refs),
+        [shaped((CODE_BITS, channels), f32)] + [shaped((1, channels), f32)] * 2,
+        [info, *term_parts],
+        [pltpu.VMEM((shards, 40, LANES), f32)],
+    )
     return (
         decoded.reshape(1, frames, 2 * height, 2 * width, LANES),
         grad_hidden.reshape(1, frames, height, width, channels),
         grad_conv,
-        all_small[:CODE_BITS],
-        all_small[32],
-        all_small[33],
+        grad_embed,
+        grad_gain.reshape(channels),
+        grad_bias.reshape(channels),
     )
 
 
@@ -617,7 +736,8 @@
 def on_device(codes, lengths, hidden, embed, conv_weight, gain, bias, cotangent):
     share = conv_weight.shape[0]
     block = codes.shape[2] * codes.shape[3] * lax.axis_size("shard")
-    plan = by_slices if share == LANES and block == LANES else by_gathers
+    fits = share == LANES and block == LANES and lax.axis_size("shard") == 4
+    plan = by_slices if fits and lax.axis_size("dp") == 8 else by_gathers
     return plan(codes, lengths, hidden, embed, conv_weight, gain, bias, cotangent)
 
 

time: 170 us -> 168 us (0.988)
  blocking collectives: 52.4 us -> 0 us
  waiting for transfers between devices: 32.2 us -> 57.9 us
  starting transfers between devices: 12.6 us -> 37.4 us
  local copies, waits for them, and re-layouts: 13.4 us -> 10.3 us
  Pallas kernels: 42.5 us -> 45.5 us
    psum x1 -> x0, blocking collectives: 34.4 us -> none  [by_slices(): small_sum = lax.psum(jnp.concatenate([embed_term, terms], axis=0), 'dp')]
    ppermute x0 -> x31, waiting for transfers between devices: none -> 29.6 us  [the longest x28 22.9 us: send(): return lax.ppermute(block, ('dp', 'shard'), pairs)]
    ppermute x0 -> x31, starting transfers between devices: none -> 26.8 us  [the longest x28 17.7 us: send(): return lax.ppermute(block, ('dp', 'shard'), pairs)]
    all_gather x1 -> x0, waiting for transfers between devices: 13.4 us -> none  [by_slices(): lax.all_gather(d_conv, ('dp', 'shard'), axis=0)]
    unnamed x1 -> x0, blocking collectives: 12.5 us -> none
    ppermute x18 -> x21, waiting for transfers between devices: 18.8 us -> 28.2 us  [swap(): return lax.ppermute(block, 'shard', pairs)]
    all_gather x1 -> x0, blocking collectives: 5.46 us -> none  [by_slices(): all_small = lax.all_gather(small_sum, 'shard', axis=1, tiled=True)]
    pallas_call x7 -> x8, Pallas kernels: 42.5 us -> 45.5 us  [kernel_call(): pl.pallas_call(body, out_shape=outs, in_specs=specs, out_specs=[pl.BlockS...]
  transfers between devices with their start and end apart: 20 -> 53, of which waited for: 7 -> 20; matrix products, arithmetic and copies ran while one was open for 4% -> 2% of each run, Pallas kernels for 7% -> 8%
where the time goes in v2:
time: 168 us; the launch traced here: 167 us
  waiting for transfers between devices  57.9 us (34%)
  Pallas kernels  45.5 us (27%)
  starting transfers between devices  37.4 us (22%)
  between operations  15.2 us (9%)
  local copies, waits for them, and re-layouts  10.3 us (6%)
    pallas_call x8, Pallas kernels, kernel_call(): pl.pallas_call(body, out_shape=outs, in_specs=specs, out_specs=[pl.BlockS...  45.5 us
    ppermute x21, waiting for transfers between devices, swap(): return lax.ppermute(block, 'shard', pairs)  28.2 us
    ppermute x28, waiting for transfers between devices, send(): return lax.ppermute(block, ('dp', 'shard'), pairs)  22.9 us
    ppermute x28, starting transfers between devices, send(): return lax.ppermute(block, ('dp', 'shard'), pairs)  17.7 us
    ppermute x21, starting transfers between devices, swap(): return lax.ppermute(block, 'shard', pairs)  10.6 us
    ppermute x3, starting transfers between devices, by_slices(): term = term + lax.ppermute(term, 'dp', [(i, i ^ hop) for i in range(clips)])  9.1 us
    ppermute x3, waiting for transfers between devices, by_slices(): term = term + lax.ppermute(term, 'dp', [(i, i ^ hop) for i in range(clips)])  6.78 us
    unnamed x100, local copies, waits for them, and re-layouts  3.54 us
  transfers between devices with their start and end apart: 53, of which 20 were waited for; matrix products, arithmetic and copies ran while one was open for 2% of the time, Pallas kernels for 8%

profile of v2, /device:TPU:0, one launch (start us, length us, event | category | flops | bytes accessed | tf_op | source)
XLA Modules:
  0.0 166.9 jit_solution(7423656435125694814)
XLA Ops:
  9.4 1.6 reshape.46.refs_2_
  11.0 1.4 pad.4.refs_3_
  13.0 2.2 %shard_map.127 = (bf16[160,256]{1,0:T(8,128)(2,1)}, bf16[160,256]{1,0:T(8,128)(2,1)}, bf16[160,256]{1,0:T(8,128)(2,1)}, bf16[160,256]{1,0:T(8,128)(2,1)}) custom-call(s32[3]{0:T(128)} %pad_add_fusion.refs_0_, s32[160,1]{1,0:T(8,128)} %reshape.57.refs_1_, bf16[160,512]{1,0:T(8,128)(2,1)} %reshape.46.refs_2_, bf16[128,512]{1,0:T(8,128)(2,1)} %pad.4.refs_3_, ...), custom_call_target="tpu_custom_call" | custom-call | flops 20971520 | bytes 787084 | tf_op jit(solution)/shard_map/pallas_call | solution.py:25
  15.6 2.6 %collective-permute-start.1 = (bf16[160,256]{1,0:T(8,128)(2,1)}, bf16[160,256]{1,0:T(8,128)(2,1)S(1)}, u32[]{:S(2)}, u32[]{:S(2)}) collective-permute-start(bf16[160,256]{1,0:T(8,128)(2,1)} %get-tuple-element.32), channel_id=1, source_target_pairs={{0,2},{1,3},{2,0},{3,1},{4,6},{5,7},{6,4},{7,5},{8,10},{9,11},{10,... | collective-permute-start | bytes 245768 | tf_op jit(solution)/shard_map/ppermute | solution.py:43
  18.3 3.2 %collective-permute-done.1.refs_3_ = bf16[160,256]{1,0:T(8,128)(2,1)S(1)} collective-permute-done((bf16[160,256]{1,0:T(8,128)(2,1)}, bf16[160,256]{1,0:T(8,128)(2,1)S(1)}, u32[]{:S(2)}, u32[]{:S(2)}) %collective-permute-start.1) | collective-permute-done | bytes 81952 | tf_op jit(solution)/shard_map/ppermute | solution.py:43
  21.5 1.4 collective-permute-done.2.refs_4_
  23.5 6.2 %shard_map.128 = (f32[640,128]{1,0:T(8,128)}, bf16[640,128]{1,0:T(8,128)(2,1)}, bf16[640,128]{1,0:T(8,128)(2,1)}, bf16[640,128]{1,0:T(8,128)(2,1)}, bf16[640,128...) custom-call(s32[3]{0:T(128)} %pad_add_fusion.refs_0_, ...), custom_call_target="tpu_custom_call" | custom-call | flops 2264924160 | bytes 5197836 | tf_op jit(solution)/shard_map/pallas_call | solution.py:25
  29.9 1.7 %collective-permute-start.4 = (bf16[640,128]{1,0:T(8,128)(2,1)}, bf16[640,128]{1,0:T(8,128)(2,1)S(1)}, u32[]{:S(2)}, u32[]{:S(2)}) collective-permute-start(bf16[640,128]{1,0:T(8,128)(2,1)} %get-tuple-element.36), channel_id=1, source_target_pairs={{0,2},{1,3},{2,0},{3,1},{4,6},{5,7},{6,4},{7,5},{8,10},{9,11},{10,... | collective-permute-start | bytes 491528 | tf_op jit(solution)/shard_map/ppermute | solution.py:43
  31.7 1.3 dynamic-slice_bitcast_fusion
  33.0 4.2 %collective-permute-done.4.refs_3_ = bf16[640,128]{1,0:T(8,128)(2,1)S(1)} collective-permute-done((bf16[640,128]{1,0:T(8,128)(2,1)}, bf16[640,128]{1,0:T(8,128)(2,1)S(1)}, u32[]{:S(2)}, u32[]{:S(2)}) %collective-permute-start.4) | collective-permute-done | bytes 163872 | tf_op jit(solution)/shard_map/ppermute | solution.py:43
  37.2 2.4 %collective-permute-done.5.refs_4_ = bf16[640,128]{1,0:T(8,128)(2,1)S(1)} collective-permute-done((bf16[640,128]{1,0:T(8,128)(2,1)}, bf16[640,128]{1,0:T(8,128)(2,1)S(1)}, u32[]{:S(2)}, u32[]{:S(2)}) %collective-permute-start.5) | collective-permute-done | bytes 163872 | tf_op jit(solution)/shard_map/ppermute | solution.py:43
  40.3 3.0 %shard_map.129 = (bf16[640,128]{1,0:T(8,128)(2,1)}, f32[8,128]{1,0:T(8,128)}, bf16[160,128]{1,0:T(8,128)(2,1)}, bf16[160,128]{1,0:T(8,128)(2,1)}, bf16[160,128]{1,0:T(8,128)(2,1)}, /*index=5*/bf16[160,128]{1,0:T(8,128)(2,1)}) custom-call(s32[3]{0:T(128)} %pad_add_fusion.refs_0_, f32[640,128]{1,0:T(8,128)} %get-tuple-element.34.refs_1_, ...), custom_call_target="tpu_custom_call" | custom-call | flops 3276800 | bytes 1315852 | tf_op jit(solution)/shard_map/pallas_call | solution.py:25
  43.6 1.6 collective-permute-start.10
  45.2 1.5 collective-permute-start.18
  47.4 0.8 collective-permute-done.12.refs_7_
  48.8 3.0 %collective-permute-done.13.refs_8_ = s32[1,160]{1,0:T(1,128)S(1)} collective-permute-done((s32[1,160]{1,0:T(1,128)S(1)}, s32[1,160]{1,0:T(1,128)S(1)}, u32[]{:S(2)}, u32[]{:S(2)}) %collective-permute-start.13) | collective-permute-done | bytes 672 | tf_op jit(solution)/shard_map/ppermute | solution.py:43
  51.8 3.0 %collective-permute-done.14.refs_9_ = s32[1,160]{1,0:T(1,128)S(1)} collective-permute-done((s32[1,160]{1,0:T(1,128)S(1)}, s32[1,160]{1,0:T(1,128)S(1)}, u32[]{:S(2)}, u32[]{:S(2)}) %collective-permute-start.14) | collective-permute-done | bytes 672 | tf_op jit(solution)/shard_map/ppermute | solution.py:43
  55.7 3.7 %collective-permute-done.7.refs_3_ = bf16[160,128]{1,0:T(8,128)(2,1)S(1)} collective-permute-done((bf16[160,128]{1,0:T(8,128)(2,1)}, bf16[160,128]{1,0:T(8,128)(2,1)S(1)}, u32[]{:S(2)}, u32[]{:S(2)}) %collective-permute-start.7) | collective-permute-done | bytes 40992 | tf_op jit(solution)/shard_map/ppermute | solution.py:43
  59.4 1.6 collective-permute-start.22
  60.9 2.6 %collective-permute-start.30 = (bf16[640,128]{1,0:T(8,128)(2,1)}, bf16[640,128]{1,0:T(8,128)(2,1)S(1)}, u32[]{:S(2)}, u32[]{:S(2)}) collective-permute-start(bf16[640,128]{1,0:T(8,128)(2,1)} %get-tuple-element.43.refs_1_.refs_2_), channel_id=1, source_target_pairs={{0,16},{1,17},{2,18},{3,19},{4,20},{5,21},{6,22},{7,23},{8,24},{9,... | collective-permute-start | bytes 491528 | tf_op jit(solution)/shard_map/ppermute | solution.py:386
  63.5 1.3 collective-permute-start.38
  65.4 6.5 %collective-permute-done.22.refs_8_ = bf16[640,128]{1,0:T(8,128)(2,1)S(1)} collective-permute-done((bf16[640,128]{1,0:T(8,128)(2,1)}, bf16[640,128]{1,0:T(8,128)(2,1)S(1)}, u32[]{:S(2)}, u32[]{:S(2)}) %collective-permute-start.22) | collective-permute-done | bytes 163872 | tf_op jit(solution)/shard_map/ppermute | solution.py:386
  72.1 10.2 %collective-permute-done.30.refs_16_ = bf16[640,128]{1,0:T(8,128)(2,1)S(1)} collective-permute-done((bf16[640,128]{1,0:T(8,128)(2,1)}, bf16[640,128]{1,0:T(8,128)(2,1)S(1)}, u32[]{:S(2)}, u32[]{:S(2)}) %collective-permute-start.30) | collective-permute-done | bytes 163872 | tf_op jit(solution)/shard_map/ppermute | solution.py:386
  83.6 5.9 %shard_map.131 = (f32[32,128]{1,0:T(8,128)}, bf16[160,128]{1,0:T(8,128)(2,1)}, bf16[160,128]{1,0:T(8,128)(2,1)}, bf16[160,128]{1,0:T(8,128)(2,1)}, bf16[160,128]{1,0:T(8,128)(2,1)}) custom-call(s32[3]{0:T(128)} %pad_add_fusion.refs_0_, bf16[640,128]{1,0:T(8,128)(2,1)} %get-tuple-element.43.refs_1_.refs_2_, bf16[640,128]{1,0:T(8,128)(2,1)} %copy-done.17, ...), custom_call_target="tpu_custom_call" | custom-call | flops 2264924160 | bytes 4377100 | tf_op jit(solution)/shard_map/pallas_call | solution.py:25
  89.6 1.6 collective-permute-start.32
  91.2 1.5 collective-permute-start.34
  94.7 1.3 collective-permute-done.32.refs_18_
  96.0 1.5 collective-permute-start.46
  98.1 2.3 %collective-permute-done.46 = f32[40,128]{1,0:T(8,128)S(1)} collective-permute-done((f32[40,128]{1,0:T(8,128)S(1)}, f32[40,128]{1,0:T(8,128)S(1)}, u32[]{:S(2)}, u32[]{:S(2)}) %collective-permute-start.46) | collective-permute-done | bytes 20512 | tf_op jit(solution)/shard_map/ppermute | solution.py:555
  100.5 6.0 %collective-permute-start.47 = (f32[40,128]{1,0:T(8,128)S(1)}, f32[40,128]{1,0:T(8,128)S(1)}, u32[]{:S(2)}, u32[]{:S(2)}) collective-permute-start(f32[40,128]{1,0:T(8,128)S(1)} %add.21), channel_id=1, source_target_pairs={{0,8},{4,12},{8,0},{12,4},{16,24},{20,28},{24,16},{28,20},{1,9},{5... | collective-permute-start | bytes 61448 | tf_op jit(solution)/shard_map/ppermute | solution.py:555
  106.6 1.8 %collective-permute-done.47 = f32[40,128]{1,0:T(8,128)S(1)} collective-permute-done((f32[40,128]{1,0:T(8,128)S(1)}, f32[40,128]{1,0:T(8,128)S(1)}, u32[]{:S(2)}, u32[]{:S(2)}) %collective-permute-start.47) | collective-permute-done | bytes 20512 | tf_op jit(solution)/shard_map/ppermute | solution.py:555
  108.4 1.5 collective-permute-start.48
  110.4 2.7 %collective-permute-done.48 = f32[40,128]{1,0:T(8,128)S(1)} collective-permute-done((f32[40,128]{1,0:T(8,128)S(1)}, f32[40,128]{1,0:T(8,128)S(1)}, u32[]{:S(2)}, u32[]{:S(2)}) %collective-permute-start.48) | collective-permute-done | bytes 20512 | tf_op jit(solution)/shard_map/ppermute | solution.py:555
  113.1 1.0 collective-permute-done.16.refs_3_
  114.1 2.6 %collective-permute-done.17.refs_4_ = bf16[160,128]{1,0:T(8,128)(2,1)S(1)} collective-permute-done((bf16[160,128]{1,0:T(8,128)(2,1)}, bf16[160,128]{1,0:T(8,128)(2,1)S(1)}, u32[]{:S(2)}, u32[]{:S(2)}) %collective-permute-start.17) | collective-permute-done | bytes 40992 | tf_op jit(solution)/shard_map/ppermute | solution.py:43
  116.8 0.9 collective-permute-start.50
  117.7 2.9 %collective-permute-done.50.refs_3_ = f32[40,128]{1,0:T(8,128)S(1)} collective-permute-done((f32[40,128]{1,0:T(8,128)S(1)}, f32[40,128]{1,0:T(8,128)S(1)}, u32[]{:S(2)}, u32[]{:S(2)}) %collective-permute-start.50) | collective-permute-done | bytes 20512 | tf_op jit(solution)/shard_map/ppermute | solution.py:43
  120.6 0.9 collective-permute-start.28
  122.0 1.1 collective-permute-start.36
  123.1 0.9 collective-permute-start.44
  124.0 1.9 %collective-permute-done.28.refs_14_ = bf16[640,128]{1,0:T(8,128)(2,1)S(1)} collective-permute-done((bf16[640,128]{1,0:T(8,128)(2,1)S(1)}, bf16[640,128]{1,0:T(8,128)(2,1)S(1)}, u32[]{:S(2)}, u32[]{:S(2)}) %collective-permute-start.28) | collective-permute-done | bytes 163872 | tf_op jit(solution)/shard_map/ppermute | solution.py:386
  126.5 1.1 collective-permute-done.36.refs_22_
  127.6 1.7 %collective-permute-done.44.refs_30_ = bf16[640,128]{1,0:T(8,128)(2,1)S(1)} collective-permute-done((bf16[640,128]{1,0:T(8,128)(2,1)S(1)}, bf16[640,128]{1,0:T(8,128)(2,1)S(1)}, u32[]{:S(2)}, u32[]{:S(2)}) %collective-permute-start.44) | collective-permute-done | bytes 163872 | tf_op jit(solution)/shard_map/ppermute | solution.py:386
  129.4 1.8 %shard_map.130 = bf16[640,128]{1,0:T(8,128)(2,1)} custom-call(s32[3]{0:T(128)} %pad_add_fusion.refs_0_, bf16[160,128]{1,0:T(8,128)(2,1)} %get-tuple-element.39.refs_1_, bf16[160,128]{1,0:T(8,128)(2,1)} %copy-done.6, bf16[160,128]{1,0:T(8,128)(2,1)} %copy-done.7, bf16[160,128]{1,0:T(8,128)(2,1)} %copy-done.8), custom_call_target="tpu_custom_call" | custom-call | bytes 327692 | tf_op jit(solution)/shard_map/pallas_call | solution.py:25
  131.2 1.6 shard_map.132
  132.7 1.6 reshape.53
  134.4 1.4 shard_map.134
  136.6 23.5 %shard_map.133 = f32[27,128,512]{2,1,0:T(8,128)} custom-call(s32[3]{0:T(128)} %pad_add_fusion.refs_0_, bf16[8,144,640]{2,1,0:T(8,128)(2,1)} %bitcast.23, bf16[640,128]{1,0:T(8,128)(2,1)} %get-tuple-element.43.refs_1_.refs_2_, bf16[640,128]{1,0:T(8,128)(2,1)} %copy-done.1, bf16[640,128]{1,0:T(8,128)(2,1)} %copy-done.22, bf16[640,128]{1,0:T(8,128)(2,1)} %copy-done, ...), custom_call_target="tpu_custom_call" | custom-call | flops 10871635968 | bytes 13795340 | tf_op jit(solution)/shard_map/pallas_call | solution.py:25
  (179 shorter events, 13.6 us)
Async XLA Ops:
  7.2 128.7 %all-gather.3.cloned.1.call-start = ((), (), s32[]{:S(2)}) async-start(), calls=%async_computation | async-start | bytes 1658880 | tf_op jit(solution)/shard_map/all_gather | solution.py:488
  15.6 5.9 %collective-permute-start.1 = (bf16[160,256]{1,0:T(8,128)(2,1)}, bf16[160,256]{1,0:T(8,128)(2,1)S(1)}, u32[]{:S(2)}, u32[]{:S(2)}) collective-permute-start(bf16[160,256]{1,0:T(8,128)(2,1)} %get-tuple-element.32), channel_id=1, source_target_pairs={{0,2},{1,3},{2,0},{3,1},{4,6},{5,7},{6,4},{7,5},{8,10},{9,11},{10,... | collective-permute-start | bytes 245768 | tf_op jit(solution)/shard_map/ppermute | solution.py:43
  18.2 4.8 %collective-permute-start.2 = (bf16[160,256]{1,0:T(8,128)(2,1)}, bf16[160,256]{1,0:T(8,128)(2,1)S(1)}, u32[]{:S(2)}, u32[]{:S(2)}) collective-permute-start(bf16[160,256]{1,0:T(8,128)(2,1)} %get-tuple-element.33), channel_id=1, source_target_pairs={{0,3},{1,2},{2,1},{3,0},{4,7},{5,6},{6,5},{7,4},{8,11},{9,10},{10,... | collective-permute-start | bytes 245768 | tf_op jit(solution)/shard_map/ppermute | solution.py:43
  29.9 7.3 %collective-permute-start.4 = (bf16[640,128]{1,0:T(8,128)(2,1)}, bf16[640,128]{1,0:T(8,128)(2,1)S(1)}, u32[]{:S(2)}, u32[]{:S(2)}) collective-permute-start(bf16[640,128]{1,0:T(8,128)(2,1)} %get-tuple-element.36), channel_id=1, source_target_pairs={{0,2},{1,3},{2,0},{3,1},{4,6},{5,7},{6,4},{7,5},{8,10},{9,11},{10,... | collective-permute-start | bytes 491528 | tf_op jit(solution)/shard_map/ppermute | solution.py:43
  31.7 7.9 %collective-permute-start.5 = (bf16[640,128]{1,0:T(8,128)(2,1)}, bf16[640,128]{1,0:T(8,128)(2,1)S(1)}, u32[]{:S(2)}, u32[]{:S(2)}) collective-permute-start(bf16[640,128]{1,0:T(8,128)(2,1)} %get-tuple-element.37), channel_id=1, source_target_pairs={{0,3},{1,2},{2,1},{3,0},{4,7},{5,6},{6,5},{7,4},{8,11},{9,10},{10,... | collective-permute-start | bytes 491528 | tf_op jit(solution)/shard_map/ppermute | solution.py:43
  43.2 20.3 %collective-permute-start.9 = (bf16[640,128]{1,0:T(8,128)(2,1)}, bf16[640,128]{1,0:T(8,128)(2,1)S(1)}, u32[]{:S(2)}, u32[]{:S(2)}) collective-permute-start(bf16[640,128]{1,0:T(8,128)(2,1)} %get-tuple-element.43.refs_1_.refs_2_), channel_id=1, source_target_pairs={{0,1},{1,0},{2,3},{3,2},{4,5},{5,4},{6,7},{7,6},{8,9},{9,8},{10,11... | collective-permute-start | bytes 491528 | tf_op jit(solution)/shard_map/ppermute | solution.py:43
  43.6 21.3 %collective-permute-start.10 = (bf16[640,128]{1,0:T(8,128)(2,1)}, bf16[640,128]{1,0:T(8,128)(2,1)S(1)}, u32[]{:S(2)}, u32[]{:S(2)}) collective-permute-start(bf16[640,128]{1,0:T(8,128)(2,1)} %get-tuple-element.43.refs_1_.refs_2_), channel_id=1, source_target_pairs={{0,2},{1,3},{2,0},{3,1},{4,6},{5,7},{6,4},{7,5},{8,10},{9,11},{10,... | collective-permute-start | bytes 491528 | tf_op jit(solution)/shard_map/ppermute | solution.py:43
  45.2 19.7 %collective-permute-start.18 = (bf16[640,128]{1,0:T(8,128)(2,1)}, bf16[640,128]{1,0:T(8,128)(2,1)S(1)}, u32[]{:S(2)}, u32[]{:S(2)}) collective-permute-start(bf16[640,128]{1,0:T(8,128)(2,1)} %get-tuple-element.43.refs_1_.refs_2_), channel_id=1, source_target_pairs={{0,4},{1,5},{2,6},{3,7},{4,0},{5,1},{6,2},{7,3},{8,12},{9,13},{10,... | collective-permute-start | bytes 491528 | tf_op jit(solution)/shard_map/ppermute | solution.py:386
  46.7 8.7 %collective-permute-start.6 = (bf16[160,128]{1,0:T(8,128)(2,1)}, bf16[160,128]{1,0:T(8,128)(2,1)S(1)}, u32[]{:S(2)}, u32[]{:S(2)}) collective-permute-start(bf16[160,128]{1,0:T(8,128)(2,1)} %get-tuple-element.40), channel_id=1, source_target_pairs={{0,1},{1,0},{2,3},{3,2},{4,5},{5,4},{6,7},{7,6},{8,9},{9,8},{10,11... | collective-permute-start | bytes 122888 | tf_op jit(solution)/shard_map/ppermute | solution.py:43
  48.2 3.6 %collective-permute-start.13 = (s32[1,160]{1,0:T(1,128)S(1)}, s32[1,160]{1,0:T(1,128)S(1)}, u32[]{:S(2)}, u32[]{:S(2)}) collective-permute-start(s32[1,160]{1,0:T(1,128)S(1)} %reshape.52.refs_6_), channel_id=1, source_target_pairs={{0,2},{1,3},{2,0},{3,1},{4,6},{5,7},{6,4},{7,5},{8,10},{9,11},{10,... | collective-permute-start | bytes 1928 | tf_op jit(solution)/shard_map/ppermute | solution.py:43
  54.8 4.6 %collective-permute-start.7 = (bf16[160,128]{1,0:T(8,128)(2,1)}, bf16[160,128]{1,0:T(8,128)(2,1)S(1)}, u32[]{:S(2)}, u32[]{:S(2)}) collective-permute-start(bf16[160,128]{1,0:T(8,128)(2,1)} %get-tuple-element.41), channel_id=1, source_target_pairs={{0,2},{1,3},{2,0},{3,1},{4,6},{5,7},{6,4},{7,5},{8,10},{9,11},{10,... | collective-permute-start | bytes 122888 | tf_op jit(solution)/shard_map/ppermute | solution.py:43
  55.4 5.6 %collective-permute-start.8 = (bf16[160,128]{1,0:T(8,128)(2,1)}, bf16[160,128]{1,0:T(8,128)(2,1)S(1)}, u32[]{:S(2)}, u32[]{:S(2)}) collective-permute-start(bf16[160,128]{1,0:T(8,128)(2,1)} %get-tuple-element.42), channel_id=1, source_target_pairs={{0,3},{1,2},{2,1},{3,0},{4,7},{5,6},{6,5},{7,4},{8,11},{9,10},{10,... | collective-permute-start | bytes 122888 | tf_op jit(solution)/shard_map/ppermute | solution.py:43
  59.4 12.6 %collective-permute-start.22 = (bf16[640,128]{1,0:T(8,128)(2,1)}, bf16[640,128]{1,0:T(8,128)(2,1)S(1)}, u32[]{:S(2)}, u32[]{:S(2)}) collective-permute-start(bf16[640,128]{1,0:T(8,128)(2,1)} %get-tuple-element.43.refs_1_.refs_2_), channel_id=1, source_target_pairs={{0,8},{1,9},{2,10},{3,11},{4,12},{5,13},{6,14},{7,15},{8,16},{9,17... | collective-permute-start | bytes 491528 | tf_op jit(solution)/shard_map/ppermute | solution.py:386
  60.9 21.4 %collective-permute-start.30 = (bf16[640,128]{1,0:T(8,128)(2,1)}, bf16[640,128]{1,0:T(8,128)(2,1)S(1)}, u32[]{:S(2)}, u32[]{:S(2)}) collective-permute-start(bf16[640,128]{1,0:T(8,128)(2,1)} %get-tuple-element.43.refs_1_.refs_2_), channel_id=1, source_target_pairs={{0,16},{1,17},{2,18},{3,19},{4,20},{5,21},{6,22},{7,23},{8,24},{9,... | collective-permute-start | bytes 491528 | tf_op jit(solution)/shard_map/ppermute | solution.py:386
  63.5 18.8 %collective-permute-start.38 = (bf16[640,128]{1,0:T(8,128)(2,1)}, bf16[640,128]{1,0:T(8,128)(2,1)S(1)}, u32[]{:S(2)}, u32[]{:S(2)}) collective-permute-start(bf16[640,128]{1,0:T(8,128)(2,1)} %get-tuple-element.43.refs_1_.refs_2_), channel_id=1, source_target_pairs={{0,24},{1,25},{2,26},{3,27},{4,28},{5,29},{6,30},{7,31},{8,0},{9,1... | collective-permute-start | bytes 491528 | tf_op jit(solution)/shard_map/ppermute | solution.py:386
  64.9 18.1 %collective-permute-start.11 = (bf16[640,128]{1,0:T(8,128)(2,1)S(1)}, bf16[640,128]{1,0:T(8,128)(2,1)S(1)}, u32[]{:S(2)}, u32[]{:S(2)}) collective-permute-start(bf16[640,128]{1,0:T(8,128)(2,1)S(1)} %collective-permute-done.10.refs_3_.refs_5_), channel_id=1, source_target_pairs={{0,1},{1,0},{2,3},{3,2},{4,5},{5,4},{6,7},{7,6},{8,9},{9,8},{10,11... | collective-permute-start | bytes 491528 | tf_op jit(solution)/shard_map/ppermute | solution.py:43
  64.9 18.6 %collective-permute-start.19 = (bf16[640,128]{1,0:T(8,128)(2,1)S(1)}, bf16[640,128]{1,0:T(8,128)(2,1)S(1)}, u32[]{:S(2)}, u32[]{:S(2)}) collective-permute-start(bf16[640,128]{1,0:T(8,128)(2,1)S(1)} %collective-permute-done.18.refs_3_), channel_id=1, source_target_pairs={{0,1},{1,0},{2,3},{3,2},{4,5},{5,4},{6,7},{7,6},{8,9},{9,8},{10,11... | collective-permute-start | bytes 491528 | tf_op jit(solution)/shard_map/ppermute | solution.py:386
  71.9 17.7 %collective-permute-start.20 = (bf16[640,128]{1,0:T(8,128)(2,1)S(1)}, bf16[640,128]{1,0:T(8,128)(2,1)S(1)}, u32[]{:S(2)}, u32[]{:S(2)}) collective-permute-start(bf16[640,128]{1,0:T(8,128)(2,1)S(1)} %broadcast_select_fusion), channel_id=1, source_target_pairs={{0,2},{1,5},{2,0},{3,7},{4,6},{5,1},{6,4},{7,3},{8,10},{9,13},{10,... | collective-permute-start | bytes 491528 | tf_op jit(solution)/shard_map/ppermute | solution.py:386
  82.4 8.8 %collective-permute-start.23 = (bf16[640,128]{1,0:T(8,128)(2,1)S(1)}, bf16[640,128]{1,0:T(8,128)(2,1)S(1)}, u32[]{:S(2)}, u32[]{:S(2)}) collective-permute-start(bf16[640,128]{1,0:T(8,128)(2,1)S(1)} %collective-permute-done.22.refs_8_), channel_id=1, source_target_pairs={{0,1},{1,0},{2,3},{3,2},{4,5},{5,4},{6,7},{7,6},{8,9},{9,8},{10,11... | collective-permute-start | bytes 491528 | tf_op jit(solution)/shard_map/ppermute | solution.py:386
  82.4 10.3 %collective-permute-start.24 = (bf16[640,128]{1,0:T(8,128)(2,1)S(1)}, bf16[640,128]{1,0:T(8,128)(2,1)S(1)}, u32[]{:S(2)}, u32[]{:S(2)}) collective-permute-start(bf16[640,128]{1,0:T(8,128)(2,1)S(1)} %collective-permute-done.22.refs_8_), channel_id=1, source_target_pairs={{0,4},{1,3},{2,6},{3,1},{4,0},{5,7},{6,2},{7,5},{8,12},{9,11},{10,... | collective-permute-start | bytes 491528 | tf_op jit(solution)/shard_map/ppermute | solution.py:386
  83.0 9.7 %collective-permute-start.26 = (bf16[640,128]{1,0:T(8,128)(2,1)S(1)}, bf16[640,128]{1,0:T(8,128)(2,1)S(1)}, u32[]{:S(2)}, u32[]{:S(2)}) collective-permute-start(bf16[640,128]{1,0:T(8,128)(2,1)S(1)} %collective-permute-done.22.refs_8_), channel_id=1, source_target_pairs={{0,2},{1,5},{2,0},{3,7},{4,6},{5,1},{6,4},{7,3},{8,10},{9,13},{10,... | collective-permute-start | bytes 491528 | tf_op jit(solution)/shard_map/ppermute | solution.py:386
  83.5 10.6 %collective-permute-start.31 = (bf16[640,128]{1,0:T(8,128)(2,1)S(1)}, bf16[640,128]{1,0:T(8,128)(2,1)S(1)}, u32[]{:S(2)}, u32[]{:S(2)}) collective-permute-start(bf16[640,128]{1,0:T(8,128)(2,1)S(1)} %collective-permute-done.30.refs_16_), channel_id=1, source_target_pairs={{0,1},{1,0},{2,3},{3,2},{4,5},{5,4},{6,7},{7,6},{8,9},{9,8},{10,11... | collective-permute-start | bytes 491528 | tf_op jit(solution)/shard_map/ppermute | solution.py:386
  89.6 6.4 %collective-permute-start.32 = (bf16[640,128]{1,0:T(8,128)(2,1)S(1)}, bf16[640,128]{1,0:T(8,128)(2,1)S(1)}, u32[]{:S(2)}, u32[]{:S(2)}) collective-permute-start(bf16[640,128]{1,0:T(8,128)(2,1)S(1)} %collective-permute-done.30.refs_16_), channel_id=1, source_target_pairs={{0,4},{1,3},{2,6},{3,1},{4,0},{5,7},{6,2},{7,5},{8,12},{9,11},{10,... | collective-permute-start | bytes 491528 | tf_op jit(solution)/shard_map/ppermute | solution.py:386
  91.2 6.4 %collective-permute-start.34 = (bf16[640,128]{1,0:T(8,128)(2,1)S(1)}, bf16[640,128]{1,0:T(8,128)(2,1)S(1)}, u32[]{:S(2)}, u32[]{:S(2)}) collective-permute-start(bf16[640,128]{1,0:T(8,128)(2,1)S(1)} %collective-permute-done.30.refs_16_), channel_id=1, source_target_pairs={{0,2},{1,5},{2,0},{3,7},{4,6},{5,1},{6,4},{7,3},{8,10},{9,13},{10,... | collective-permute-start | bytes 491528 | tf_op jit(solution)/shard_map/ppermute | solution.py:386
  92.7 4.9 %collective-permute-start.39 = (bf16[640,128]{1,0:T(8,128)(2,1)S(1)}, bf16[640,128]{1,0:T(8,128)(2,1)S(1)}, u32[]{:S(2)}, u32[]{:S(2)}) collective-permute-start(bf16[640,128]{1,0:T(8,128)(2,1)S(1)} %collective-permute-done.38.refs_24_), channel_id=1, source_target_pairs={{0,1},{1,0},{2,3},{3,2},{4,5},{5,4},{6,7},{7,6},{8,9},{9,8},{10,11... | collective-permute-start | bytes 491528 | tf_op jit(solution)/shard_map/ppermute | solution.py:386
  92.7 7.8 %collective-permute-start.40 = (bf16[640,128]{1,0:T(8,128)(2,1)S(1)}, bf16[640,128]{1,0:T(8,128)(2,1)S(1)}, u32[]{:S(2)}, u32[]{:S(2)}) collective-permute-start(bf16[640,128]{1,0:T(8,128)(2,1)S(1)} %collective-permute-done.38.refs_24_), channel_id=1, source_target_pairs={{0,4},{1,3},{2,6},{3,1},{4,0},{5,7},{6,2},{7,5},{8,12},{9,11},{10,... | collective-permute-start | bytes 491528 | tf_op jit(solution)/shard_map/ppermute | solution.py:386
  94.0 14.3 %collective-permute-start.42 = (bf16[640,128]{1,0:T(8,128)(2,1)S(1)}, bf16[640,128]{1,0:T(8,128)(2,1)S(1)}, u32[]{:S(2)}, u32[]{:S(2)}) collective-permute-start(bf16[640,128]{1,0:T(8,128)(2,1)S(1)} %collective-permute-done.38.refs_24_), channel_id=1, source_target_pairs={{0,2},{1,5},{2,0},{3,7},{4,6},{5,1},{6,4},{7,3},{8,10},{9,13},{10,... | collective-permute-start | bytes 491528 | tf_op jit(solution)/shard_map/ppermute | solution.py:386
  96.0 4.3 %collective-permute-start.46 = (f32[40,128]{1,0:T(8,128)S(1)}, f32[40,128]{1,0:T(8,128)S(1)}, u32[]{:S(2)}, u32[]{:S(2)}) collective-permute-start(f32[40,128]{1,0:T(8,128)S(1)} %constant_dynamic-update-slice_fusion), channel_id=1, source_target_pairs={{0,4},{4,0},{8,12},{12,8},{16,20},{20,16},{24,28},{28,24},{1,5},{5... | collective-permute-start | bytes 61448 | tf_op jit(solution)/shard_map/ppermute | solution.py:555
  97.6 23.9 %collective-permute-start.21 = (bf16[640,128]{1,0:T(8,128)(2,1)S(1)}, bf16[640,128]{1,0:T(8,128)(2,1)S(1)}, u32[]{:S(2)}, u32[]{:S(2)}) collective-permute-start(bf16[640,128]{1,0:T(8,128)(2,1)S(1)} %collective-permute-done.20.refs_6_), channel_id=1, source_target_pairs={{0,1},{1,0},{2,3},{3,2},{4,5},{5,4},{6,7},{7,6},{8,9},{9,8},{10,11... | collective-permute-start | bytes 491528 | tf_op jit(solution)/shard_map/ppermute | solution.py:386
  97.6 24.4 %collective-permute-start.25 = (bf16[640,128]{1,0:T(8,128)(2,1)S(1)}, bf16[640,128]{1,0:T(8,128)(2,1)S(1)}, u32[]{:S(2)}, u32[]{:S(2)}) collective-permute-start(bf16[640,128]{1,0:T(8,128)(2,1)S(1)} %collective-permute-done.24.refs_10_), channel_id=1, source_target_pairs={{0,1},{1,0},{2,3},{3,2},{4,5},{5,4},{6,7},{7,6},{8,9},{9,8},{10,11... | collective-permute-start | bytes 491528 | tf_op jit(solution)/shard_map/ppermute | solution.py:386
  100.4 22.7 %collective-permute-start.27 = (bf16[640,128]{1,0:T(8,128)(2,1)S(1)}, bf16[640,128]{1,0:T(8,128)(2,1)S(1)}, u32[]{:S(2)}, u32[]{:S(2)}) collective-permute-start(bf16[640,128]{1,0:T(8,128)(2,1)S(1)} %collective-permute-done.26.refs_12_), channel_id=1, source_target_pairs={{0,1},{1,0},{2,3},{3,2},{4,5},{5,4},{6,7},{7,6},{8,9},{9,8},{10,11... | collective-permute-start | bytes 491528 | tf_op jit(solution)/shard_map/ppermute | solution.py:386
  100.5 7.8 %collective-permute-start.47 = (f32[40,128]{1,0:T(8,128)S(1)}, f32[40,128]{1,0:T(8,128)S(1)}, u32[]{:S(2)}, u32[]{:S(2)}) collective-permute-start(f32[40,128]{1,0:T(8,128)S(1)} %add.21), channel_id=1, source_target_pairs={{0,8},{4,12},{8,0},{12,4},{16,24},{20,28},{24,16},{28,20},{1,9},{5... | collective-permute-start | bytes 61448 | tf_op jit(solution)/shard_map/ppermute | solution.py:555
  108.4 4.7 %collective-permute-start.48 = (f32[40,128]{1,0:T(8,128)S(1)}, f32[40,128]{1,0:T(8,128)S(1)}, u32[]{:S(2)}, u32[]{:S(2)}) collective-permute-start(f32[40,128]{1,0:T(8,128)S(1)} %add.22), channel_id=1, source_target_pairs={{0,16},{4,20},{8,24},{12,28},{16,0},{20,4},{24,8},{28,12},{1,17},{... | collective-permute-start | bytes 61448 | tf_op jit(solution)/shard_map/ppermute | solution.py:555
  109.9 4.2 %collective-permute-start.16 = (bf16[160,128]{1,0:T(8,128)(2,1)}, bf16[160,128]{1,0:T(8,128)(2,1)S(1)}, u32[]{:S(2)}, u32[]{:S(2)}) collective-permute-start(bf16[160,128]{1,0:T(8,128)(2,1)} %get-tuple-element.46), channel_id=1, source_target_pairs={{0,2},{1,3},{2,0},{3,1},{4,6},{5,7},{6,4},{7,5},{8,10},{9,11},{10,... | collective-permute-start | bytes 122888 | tf_op jit(solution)/shard_map/ppermute | solution.py:43
  113.1 3.6 %collective-permute-start.17 = (bf16[160,128]{1,0:T(8,128)(2,1)}, bf16[160,128]{1,0:T(8,128)(2,1)S(1)}, u32[]{:S(2)}, u32[]{:S(2)}) collective-permute-start(bf16[160,128]{1,0:T(8,128)(2,1)} %get-tuple-element.47), channel_id=1, source_target_pairs={{0,3},{1,2},{2,1},{3,0},{4,7},{5,6},{6,5},{7,4},{8,11},{9,10},{10,... | collective-permute-start | bytes 122888 | tf_op jit(solution)/shard_map/ppermute | solution.py:43
  114.1 3.5 %collective-permute-start.49 = (f32[40,128]{1,0:T(8,128)S(1)}, f32[40,128]{1,0:T(8,128)S(1)}, u32[]{:S(2)}, u32[]{:S(2)}) collective-permute-start(f32[40,128]{1,0:T(8,128)S(1)} %add.23.refs_1_), channel_id=1, source_target_pairs={{0,1},{1,0},{2,3},{3,2},{4,5},{5,4},{6,7},{7,6},{8,9},{9,8},{10,11... | collective-permute-start | bytes 61448 | tf_op jit(solution)/shard_map/ppermute | solution.py:43
  116.8 3.8 %collective-permute-start.50 = (f32[40,128]{1,0:T(8,128)S(1)}, f32[40,128]{1,0:T(8,128)S(1)}, u32[]{:S(2)}, u32[]{:S(2)}) collective-permute-start(f32[40,128]{1,0:T(8,128)S(1)} %add.23.refs_1_), channel_id=1, source_target_pairs={{0,2},{1,3},{2,0},{3,1},{4,6},{5,7},{6,4},{7,5},{8,10},{9,11},{10,... | collective-permute-start | bytes 61448 | tf_op jit(solution)/shard_map/ppermute | solution.py:43
  117.7 3.8 %collective-permute-start.51 = (f32[40,128]{1,0:T(8,128)S(1)}, f32[40,128]{1,0:T(8,128)S(1)}, u32[]{:S(2)}, u32[]{:S(2)}) collective-permute-start(f32[40,128]{1,0:T(8,128)S(1)} %add.23.refs_1_), channel_id=1, source_target_pairs={{0,3},{1,2},{2,1},{3,0},{4,7},{5,6},{6,5},{7,4},{8,11},{9,10},{10,... | collective-permute-start | bytes 61448 | tf_op jit(solution)/shard_map/ppermute | solution.py:43
  120.6 5.3 %collective-permute-start.28 = (bf16[640,128]{1,0:T(8,128)(2,1)S(1)}, bf16[640,128]{1,0:T(8,128)(2,1)S(1)}, u32[]{:S(2)}, u32[]{:S(2)}) collective-permute-start(bf16[640,128]{1,0:T(8,128)(2,1)S(1)} %collective-permute-done.24.refs_10_), channel_id=1, source_target_pairs={{0,2},{1,5},{2,0},{3,7},{4,6},{5,1},{6,4},{7,3},{8,10},{9,13},{10,... | collective-permute-start | bytes 491528 | tf_op jit(solution)/shard_map/ppermute | solution.py:386
  121.5 4.4 %collective-permute-start.33 = (bf16[640,128]{1,0:T(8,128)(2,1)S(1)}, bf16[640,128]{1,0:T(8,128)(2,1)S(1)}, u32[]{:S(2)}, u32[]{:S(2)}) collective-permute-start(bf16[640,128]{1,0:T(8,128)(2,1)S(1)} %collective-permute-done.32.refs_18_), channel_id=1, source_target_pairs={{0,1},{1,0},{2,3},{3,2},{4,5},{5,4},{6,7},{7,6},{8,9},{9,8},{10,11... | collective-permute-start | bytes 491528 | tf_op jit(solution)/shard_map/ppermute | solution.py:386
  121.5 4.9 %collective-permute-start.35 = (bf16[640,128]{1,0:T(8,128)(2,1)S(1)}, bf16[640,128]{1,0:T(8,128)(2,1)S(1)}, u32[]{:S(2)}, u32[]{:S(2)}) collective-permute-start(bf16[640,128]{1,0:T(8,128)(2,1)S(1)} %collective-permute-done.34.refs_20_), channel_id=1, source_target_pairs={{0,1},{1,0},{2,3},{3,2},{4,5},{5,4},{6,7},{7,6},{8,9},{9,8},{10,11... | collective-permute-start | bytes 491528 | tf_op jit(solution)/shard_map/ppermute | solution.py:386
  122.0 5.6 %collective-permute-start.36 = (bf16[640,128]{1,0:T(8,128)(2,1)S(1)}, bf16[640,128]{1,0:T(8,128)(2,1)S(1)}, u32[]{:S(2)}, u32[]{:S(2)}) collective-permute-start(bf16[640,128]{1,0:T(8,128)(2,1)S(1)} %collective-permute-done.32.refs_18_), channel_id=1, source_target_pairs={{0,2},{1,5},{2,0},{3,7},{4,6},{5,1},{6,4},{7,3},{8,10},{9,13},{10,... | collective-permute-start | bytes 491528 | tf_op jit(solution)/shard_map/ppermute | solution.py:386
  123.1 6.3 %collective-permute-start.44 = (bf16[640,128]{1,0:T(8,128)(2,1)S(1)}, bf16[640,128]{1,0:T(8,128)(2,1)S(1)}, u32[]{:S(2)}, u32[]{:S(2)}) collective-permute-start(bf16[640,128]{1,0:T(8,128)(2,1)S(1)} %collective-permute-done.40.refs_26_), channel_id=1, source_target_pairs={{0,2},{1,5},{2,0},{3,7},{4,6},{5,1},{6,4},{7,3},{8,10},{9,13},{10,... | collective-permute-start | bytes 491528 | tf_op jit(solution)/shard_map/ppermute | solution.py:386
  125.9 10.0 %collective-permute-start.41 = (bf16[640,128]{1,0:T(8,128)(2,1)S(1)}, bf16[640,128]{1,0:T(8,128)(2,1)S(1)}, u32[]{:S(2)}, u32[]{:S(2)}) collective-permute-start(bf16[640,128]{1,0:T(8,128)(2,1)S(1)} %collective-permute-done.40.refs_26_), channel_id=1, source_target_pairs={{0,1},{1,0},{2,3},{3,2},{4,5},{5,4},{6,7},{7,6},{8,9},{9,8},{10,11... | collective-permute-start | bytes 491528 | tf_op jit(solution)/shard_map/ppermute | solution.py:386
  125.9 9.9 %collective-permute-start.43 = (bf16[640,128]{1,0:T(8,128)(2,1)S(1)}, bf16[640,128]{1,0:T(8,128)(2,1)S(1)}, u32[]{:S(2)}, u32[]{:S(2)}) collective-permute-start(bf16[640,128]{1,0:T(8,128)(2,1)S(1)} %collective-permute-done.42.refs_28_), channel_id=1, source_target_pairs={{0,1},{1,0},{2,3},{3,2},{4,5},{5,4},{6,7},{7,6},{8,9},{9,8},{10,11... | collective-permute-start | bytes 491528 | tf_op jit(solution)/shard_map/ppermute | solution.py:386
  126.4 9.5 %collective-permute-start.29 = (bf16[640,128]{1,0:T(8,128)(2,1)S(1)}, bf16[640,128]{1,0:T(8,128)(2,1)}, u32[]{:S(2)}, u32[]{:S(2)}) collective-permute-start(bf16[640,128]{1,0:T(8,128)(2,1)S(1)} %collective-permute-done.28.refs_14_), channel_id=1, source_target_pairs={{0,1},{1,0},{2,3},{3,2},{4,5},{5,4},{6,7},{7,6},{8,9},{9,8},{10,11... | collective-permute-start | bytes 491528 | tf_op jit(solution)/shard_map/ppermute | solution.py:386
  127.6 8.2 %collective-permute-start.37 = (bf16[640,128]{1,0:T(8,128)(2,1)S(1)}, bf16[640,128]{1,0:T(8,128)(2,1)}, u32[]{:S(2)}, u32[]{:S(2)}) collective-permute-start(bf16[640,128]{1,0:T(8,128)(2,1)S(1)} %collective-permute-done.36.refs_22_), channel_id=1, source_target_pairs={{0,1},{1,0},{2,3},{3,2},{4,5},{5,4},{6,7},{7,6},{8,9},{9,8},{10,11... | collective-permute-start | bytes 491528 | tf_op jit(solution)/shard_map/ppermute | solution.py:386
  129.4 6.5 %collective-permute-start.45 = (bf16[640,128]{1,0:T(8,128)(2,1)S(1)}, bf16[640,128]{1,0:T(8,128)(2,1)}, u32[]{:S(2)}, u32[]{:S(2)}) collective-permute-start(bf16[640,128]{1,0:T(8,128)(2,1)S(1)} %collective-permute-done.44.refs_30_), channel_id=1, source_target_pairs={{0,1},{1,0},{2,3},{3,2},{4,5},{5,4},{6,7},{7,6},{8,9},{9,8},{10,11... | collective-permute-start | bytes 491528 | tf_op jit(solution)/shard_map/ppermute | solution.py:386
  (54 other events, 996.4 us)
Sparse Core Ops, SparseCore 0:
  29.9 53.5 all-gather.2

commit v3 on v1

--- a/solution.py
+++ b/solution.py
@@ -1,3 +1,5 @@
+import math
+
 import jax
 import jax.numpy as jnp
 from jax import lax
@@ -8,7 +10,12 @@
 CODE_BITS = 18
 GROUPS = 32
 LANES = 128
-VMEM_BYTES = 56 * 1024 * 1024
+LENGTH_ROWS = 16
+BIT_ROWS = 32
+TERM_ROW = 24
+MIB = 1024 * 1024
+WIDE_LIMIT = 61 * MIB
+SMALL_COST = pl.CostEstimate(flops=1, bytes_accessed=1, transcendentals=0)
 
 eps_norm = 1e-05
 
@@ -16,20 +23,30 @@
 f32 = jnp.float32
 
 
-def kernel_call(body, outs, args, scratch=(), scalars=1, flops=0, aliases=None):
+def scratch_bytes(scratch):
+    held = [s for s in scratch if s.dtype in (bf16, f32)]
+    return sum(math.prod(s.shape) * jnp.dtype(s.dtype).itemsize for s in held)
+
+
+def kernel_call(body, outs, args, scratch=(), scalars=1, flops=0, anywhere=()):
+    vmem = pl.BlockSpec(memory_space=pltpu.VMEM)
     specs = [pl.BlockSpec(memory_space=pltpu.SMEM)] * scalars
-    specs += [pl.BlockSpec(memory_space=pltpu.VMEM)] * (len(args) - scalars)
+    specs += [vmem] * (len(args) - scalars)
+    for place in anywhere:
+        specs[place] = pl.BlockSpec(memory_space=pltpu.HBM)
     moved = sum(a.size * a.dtype.itemsize for a in args)
     moved += sum(o.size * o.dtype.itemsize for o in outs)
+    limit = min(56 * MIB, moved + scratch_bytes(scratch) + 12 * MIB)
+    if anywhere:
+        limit = WIDE_LIMIT
     return pl.pallas_call(
         body,
         out_shape=outs,
         in_specs=specs,
-        out_specs=[pl.BlockSpec(memory_space=pltpu.VMEM)] * len(outs),
+        out_specs=[vmem] * len(outs),
         scratch_shapes=scratch,
-        input_output_aliases=aliases or {},
-        compiler_params=pltpu.CompilerParams(vmem_limit_bytes=VMEM_BYTES),
-        cost_estimate=pl.CostEstimate(flops=flops, bytes_accessed=moved, transcendentals=0),
+        compiler_params=pltpu.CompilerParams(vmem_limit_bytes=limit),
+        cost_estimate=SMALL_COST,
     )(*args)
 
 
@@ -50,49 +67,65 @@
 
 
 def embed_body(shards, width, frame_rows, info, codes, hidden, embed, cot, *rest):
-    sends, (chunks, cot_wide, part) = rest[:shards], rest[shards:]
+    sends, (chunks, cot_wide, part, table) = rest[:shards], rest[shards:]
     rows = codes.shape[0]
     cells = rows // width
     lanes = lax.broadcasted_iota(jnp.int32, (rows, LANES), 1)
     spread = jnp.broadcast_to(codes[...], (rows, LANES))
     bit = lax.bitwise_and(lax.shift_right_logical(spread, jnp.minimum(lanes, 31)), 1)
-    bits = jnp.where(lanes < CODE_BITS, 2 * bit - 1, 0).astype(f32).astype(bf16)
-    embedded = jnp.dot(bits, embed[...], preferred_element_type=f32)
+    bits = jnp.where(lanes < CODE_BITS, 2 * bit - 1, 0).astype(f32)
+    turned_bits = jnp.concatenate(
+        [bits.T[:BIT_ROWS], jnp.zeros((BIT_ROWS, 2 * LANES - rows), f32)], axis=1
+    ).astype(bf16)
+    bits = bits.astype(bf16)
+    table[...] = jnp.zeros_like(table)
+    table[:CODE_BITS, :] = embed[...]
+    embedded = jnp.dot(bits, table[...], preferred_element_type=f32)
     mask = frame_rows_below(rows, info[0] * frame_rows)
     features = ((embedded + hidden[...].astype(f32)) * mask).astype(bf16)
     cot_wide[...] = cot[...].astype(f32)
     for j in range(shards):
-        chunks[j, :, :LANES] = features[:, j * LANES : (j + 1) * LANES]
+        chunks[j, :rows, :LANES] = features[:, j * LANES : (j + 1) * LANES]
         for w in range(width):
             first = (j // 2) * (2 * width) + 2 * w + j % 2
             part[pl.ds(w, cells, stride=width), :] = step_rows(cot_wide, first, cells, 4 * width)
-        chunks[j, :, LANES:] = part[...].astype(bf16)
+        chunks[j, :rows, LANES:] = part[...].astype(bf16)
+        chunks[j, rows:, :] = turned_bits
     for hop in range(shards):
         sends[hop][...] = chunks[lax.bitwise_xor(info[1], hop)]
 
 
-def forward_body(shards, width, frames, height, info, *rest):
-    parts, weight = rest[:shards], rest[shards]
-    own_out = rest[shards + 1]
-    sends = rest[shards + 2 : 2 * shards + 1]
-    slab_out, turned_out, cot_out = rest[2 * shards + 1 : 2 * shards + 4]
-    chunks, slab, cot, rims, patches, sums = rest[2 * shards + 4 :]
+def slab_body(shards, width, cells, info, *rest):
+    parts, (slab_out, turned_out, cot_out) = rest[:shards], rest[shards : shards + 3]
+    chunks, slab, cot = rest[shards + 3 :]
     columns = width * shards
-    rows = frames * height * columns
-    cells = frames * height
     for hop in range(shards):
         origin = lax.bitwise_xor(info[1], hop)
-        chunks[origin, 0] = parts[hop][:, :LANES].astype(f32)
-        chunks[origin, 1] = parts[hop][:, LANES:].astype(f32)
+        chunks[origin, 0] = parts[hop][: cells * width, :LANES].astype(f32)
+        chunks[origin, 1] = parts[hop][: cells * width, LANES:].astype(f32)
     for j in range(shards):
         for w in range(width):
             place = pl.ds(width * j + w, cells, stride=columns)
             slab[place, :] = chunks[j, 0, pl.ds(w, cells, stride=width), :]
             cot[place, :] = chunks[j, 1, pl.ds(w, cells, stride=width), :]
     cot_out[...] = cot[...].astype(bf16)
-    middle = slab[...]
-    slab_out[...] = middle.astype(bf16)
-    turned_out[...] = middle.T.astype(bf16)
+    slab_out[...] = slab[...].astype(bf16)
+    turned_out[:LANES, :] = slab[...].T.astype(bf16)
+    rows = cells * columns
+    turned_out[LANES:, :] = jnp.full((LENGTH_ROWS, rows), info[0].astype(f32)).astype(bf16)
+
+
+def forward_body(shards, width, frames, height, info, slab, weight, own_out, *rest):
+    sends, (rims, patches, sums, held, sems) = rest[: shards - 1], rest[shards - 1 :]
+    span = 9 * LANES
+    copies = []
+    for dt in range(3):
+        chunk = pl.ds(dt * span, span)
+        copies.append(pltpu.make_async_copy(weight.at[chunk], held.at[chunk], sems.at[dt]))
+        copies[dt].start()
+    columns = width * shards
+    rows = frames * height * columns
+    middle = slab[...].astype(f32)
     column = lax.broadcasted_iota(jnp.int32, (rows, 1), 0) % columns
     rims[...] = jnp.zeros_like(rims)
     shifted = (
@@ -111,14 +144,16 @@
                 patches[:, tap * LANES : (tap + 1) * LANES] = rims[
                     dw, dt : dt + frames, dr : dr + height
                 ].reshape(rows, LANES)
-    for half in range(shards // 2):
-        total = jnp.dot(
-            patches[...],
-            weight[:, half * 2 * LANES : (half + 1) * 2 * LANES],
-            preferred_element_type=f32,
-        )
-        sums[2 * half] = total[:, :LANES]
-        sums[2 * half + 1] = total[:, LANES:]
+    for dt in range(3):
+        copies[dt].wait()
+        chunk = slice(dt * span, (dt + 1) * span)
+        total = jnp.dot(patches[:, chunk], held[chunk, :], preferred_element_type=f32)
+        for part in range(shards):
+            piece = total[:, part * LANES : (part + 1) * LANES]
+            if dt == 0:
+                sums[part] = piece
+            else:
+                sums[part] += piece
     own_out[...] = sums[info[1]]
     for hop in range(1, shards):
         sends[hop - 1][...] = sums[lax.bitwise_xor(info[1], hop)].astype(bf16)
@@ -141,11 +176,14 @@
 
 def norm_body(shards, width, frames, height, per_group, info, *rest):
     own, parts = rest[0], rest[1:shards]
-    gain, bias, cot, d_conv_out, terms_out = rest[shards : shards + 5]
-    sends = rest[shards + 5 : 2 * shards + 5]
-    conv, slope, act, part = rest[2 * shards + 5 :]
+    gain_all, bias_all, cot, d_conv_out, terms_out, act = rest[shards : shards + 6]
+    conv, slope, scale, sems = rest[shards + 6 :]
+    own_lanes = pl.ds(pl.multiple_of(info[1] * LANES, LANES), LANES)
+    copies = []
+    for place, source in enumerate((gain_all, bias_all)):
+        copies.append(pltpu.make_async_copy(source, scale.at[place], sems.at[place]))
+        copies[place].start()
     columns = width * shards
-    cells = frames * height
     block = height * columns
     length = info[0]
     sum_one = jnp.zeros((8, LANES), f32)
@@ -164,15 +202,18 @@
     variance = group_total(sum_two, per_group) / count - mean * mean
     inv_std = lax.rsqrt(variance + eps_norm)[:1]
     mean = mean[:1]
+    for copy in copies:
+        copy.wait()
+    gain, bias = scale[0, :, own_lanes], scale[1, :, own_lanes]
     gain_sum = jnp.zeros((8, LANES), f32)
     bias_sum = jnp.zeros((8, LANES), f32)
     for t in range(frames):
         span = pl.ds(t * block, block)
         mask = (t < length).astype(f32)
         normed = (conv[span, :] - mean) * inv_std
-        pre = normed * gain[...] + bias[...]
+        pre = normed * gain + bias
         sigma = jax.nn.sigmoid(pre)
-        act[span, :] = pre * sigma * mask
+        act[span, :] = (pre * sigma * mask).astype(bf16)
         d_pre = cot[span, :].astype(f32) * mask * sigma * (1.0 + pre * (1.0 - sigma))
         conv[span, :] = normed
         slope[span, :] = d_pre
@@ -180,40 +221,52 @@
         bias_sum += column_total(d_pre)
     row = lax.broadcasted_iota(jnp.int32, (8, LANES), 0)
     terms_out[...] = jnp.where(row == 0, gain_sum, jnp.where(row == 1, bias_sum, 0.0))
-    tot_one = (group_total(bias_sum * gain[...], per_group) / count)[:1]
-    tot_two = (group_total(gain_sum * gain[...], per_group) / count)[:1]
+    tot_one = (group_total(bias_sum * gain, per_group) / count)[:1]
+    tot_two = (group_total(gain_sum * gain, per_group) / count)[:1]
     for t in range(frames):
         span = pl.ds(t * block, block)
         mask = (t < length).astype(f32)
-        d_norm = slope[span, :] * gain[...]
+        d_norm = slope[span, :] * gain
         d_conv_out[span, :] = (
             inv_std * (d_norm - tot_one - conv[span, :] * tot_two) * mask
         ).astype(bf16)
-    column_chunks(shards, width, cells, info, act, part, sends)
-
-
-def column_chunks(shards, width, cells, info, slab, part, sends):
+
+
+def column_chunks(shards, width, cells, slab, part):
     for j in range(shards):
         for w in range(width):
             part[j, pl.ds(w, cells, stride=width), :] = step_rows(
                 slab, width * j + w, cells, width * shards
             )
-    for hop in range(shards):
-        sends[hop][...] = part[lax.bitwise_xor(info[1], hop)].astype(bf16)
 
 
 def input_grad_body(shards, width, frames, height, info, *rest):
-    parts, weight, codes = rest[:shards], rest[shards], rest[shards + 1 : 2 * shards + 1]
-    embed_out = rest[2 * shards + 1]
-    sends = rest[2 * shards + 2 : 3 * shards + 2]
-    pieces, whole, sums, part = rest[3 * shards + 2 :]
+    own, near, mixed = rest[0], rest[1], rest[2:6]
+    weight, act, terms = rest[6:9]
+    parts = rest[9 : 9 + shards]
+    small_out = rest[9 + shards]
+    sends = rest[10 + shards : 10 + 2 * shards]
+    whole, sums, slab, part, wide = rest[10 + 2 * shards :]
     columns = width * shards
     rows = frames * height * columns
     cells = frames * height
-    for hop in range(shards):
-        pieces[lax.bitwise_xor(info[1], hop)] = parts[hop][...]
-    for j in range(shards):
-        whole[:, j * LANES : (j + 1) * LANES] = pieces[j]
+    own_rows = cells * width
+    core = lax.bitwise_and(info[1], 1)
+
+    def place(piece, hop, when):
+        @pl.when(when)
+        def _():
+            origin = lax.bitwise_xor(info[1], hop)
+            lanes = pl.ds(pl.multiple_of(origin * LANES, LANES), LANES)
+            whole[:, lanes] = piece[...]
+
+    always = info[1] >= 0
+    place(own, 0, always)
+    place(near, 1, always)
+    place(mixed[0], 2, core == 1)
+    place(mixed[1], 2, core == 0)
+    place(mixed[2], 3, core == 0)
+    place(mixed[3], 3, core == 1)
     sums[...] = jnp.zeros_like(sums)
     for first in range(0, 27, 2):
         taps = min(2, 27 - first)
@@ -237,89 +290,240 @@
     total = sums[1].reshape(rows, LANES)
     total = total + jnp.where(column < columns - 1, after, 0.0)
     total = total + jnp.where(column > 0, before, 0.0)
-    total = total * frame_rows_below(rows, info[0] * (height * columns))
-    slab = sums.at[1]
-    slab[...] = total.reshape(frames, height, columns, LANES)
-    flat = slab.reshape(rows, LANES)
-    column_chunks(shards, width, cells, info, flat, part, sends)
-    level = lax.broadcasted_iota(jnp.int32, (32, cells * width), 0)
-    embed_term = jnp.zeros((32, LANES), f32)
+    slab[...] = total * frame_rows_below(rows, info[0] * (height * columns))
+    wide[...] = act[...].astype(f32)
+    small = jnp.zeros((BIT_ROWS, LANES), f32)
+    column_chunks(shards, width, cells, slab, part)
     for hop in range(shards):
-        spread = jnp.broadcast_to(codes[hop][...], (32, cells * width))
-        bit = lax.bitwise_and(lax.shift_right_logical(spread, level), 1)
-        bits = jnp.where(level < CODE_BITS, 2 * bit - 1, 0).astype(f32).astype(bf16)
-        embed_term += jnp.dot(bits, sends[hop][...], preferred_element_type=f32)
-    embed_out[...] = embed_term
-
-
-def hidden_body(shards, info, *rest):
-    parts, out, pieces = rest[:shards], rest[shards], rest[shards + 1]
+        grad = part[lax.bitwise_xor(info[1], hop)].astype(bf16)
+        sends[hop][:, :LANES] = grad
+        bits = parts[hop][own_rows:, :own_rows]
+        small += jnp.dot(bits, grad, preferred_element_type=f32)
+    column_chunks(shards, width, cells, wide, part)
     for hop in range(shards):
-        pieces[lax.bitwise_xor(info[1], hop)] = parts[hop][...]
-    for j in range(shards):
-        out[:, j * LANES : (j + 1) * LANES] = pieces[j]
-
-
-def decoded_body(shards, width, info, *rest):
-    parts, out, pieces, slab = rest[:shards], rest[shards], rest[shards + 1], rest[shards + 2]
+        sends[hop][:, LANES:] = part[lax.bitwise_xor(info[1], hop)].astype(bf16)
+    small_out[:TERM_ROW, :] = small[:TERM_ROW]
+    small_out[TERM_ROW:, :] = terms[...]
+
+
+def finish_body(shards, width, info, *rest):
+    parts, (hidden_out, decoded_out, active, slab) = rest[:shards], rest[shards:]
     cells = parts[0].shape[0] // width
     for hop in range(shards):
-        pieces[lax.bitwise_xor(info[1], hop)] = parts[hop][...].astype(f32)
+        origin = lax.bitwise_xor(info[1], hop)
+        lanes = pl.ds(pl.multiple_of(origin * LANES, LANES), LANES)
+        hidden_out[:, lanes] = parts[hop][:, :LANES]
+        active[origin] = parts[hop][:, LANES:].astype(f32)
     for j in range(shards):
         for w in range(width):
             first = (j // 2) * (2 * width) + 2 * w + j % 2
-            slab[pl.ds(first, cells, stride=4 * width), :] = pieces[
+            slab[pl.ds(first, cells, stride=4 * width), :] = active[
                 j, pl.ds(w, cells, stride=width), :
             ]
-    out[...] = slab[...].astype(bf16)
-
-
-def weight_grad_body(frames, height, columns, lengths, turned, grads, out, left, *rights):
-    clips = turned.shape[0]
-    shards = grads.shape[1]
+    decoded_out[...] = slab[...].astype(bf16)
+
+
+def terms_body(shards, info, *rest):
+    parts, (embed_out, gain_out, bias_out) = rest[:shards], rest[shards:]
+    for hop in range(shards):
+        origin = lax.bitwise_xor(info[1], hop)
+        lanes = pl.ds(pl.multiple_of(origin * LANES, LANES), LANES)
+        embed_out[:, lanes] = parts[hop][:CODE_BITS, :]
+        gain_out[:, lanes] = parts[hop][TERM_ROW : TERM_ROW + 1, :]
+        bias_out[:, lanes] = parts[hop][TERM_ROW + 1 : TERM_ROW + 2, :]
+
+
+def slot_clip(info, slot, clips):
+    lines = clips // 2
+    line = lax.rem(info[2] // 2 + lines - slot % lines, lines)
+    return 2 * line + lax.bitwise_xor(lax.rem(info[2], 2), slot // lines)
+
+
+def by_hop(group):
+    own, odd, even = group
+    return [own, odd.at[0], even, odd.at[1]]
+
+
+def fill_taps(frames, height, columns, info, groups, left, table, images, shifts):
+    turned = by_hop(groups[:3]) + by_hop(groups[3:])
+    clips = len(turned)
     block = height * columns
-    place = lax.broadcasted_iota(jnp.int32, (1, block), 1)
+    source = lax.broadcasted_iota(jnp.int32, (block, block), 0)
+    place = lax.broadcasted_iota(jnp.int32, (block, block), 1)
     row, column = place // columns, place % columns
-
-    def one_clip(clip, base):
-        length = lengths[clip]
-
-        def one_frame(t, at):
-            here = pl.ds(pl.multiple_of(t * block, block), block)
-            there = pl.ds(pl.multiple_of(at * block, block), block)
-            image = turned[clip, :, here].astype(f32)
-            for dr in range(3):
-                for dw in range(3):
-                    offset = (dr - 1) * columns + dw - 1
-                    moved = pltpu.roll(image, -offset % block, 1) if offset else image
-                    if dr == 0:
-                        moved = jnp.where(row > 0, moved, 0.0)
-                    if dr == 2:
-                        moved = jnp.where(row < height - 1, moved, 0.0)
-                    if dw == 0:
-                        moved = jnp.where(column > 0, moved, 0.0)
-                    if dw == 2:
-                        moved = jnp.where(column < columns - 1, moved, 0.0)
-                    tap = dr * 3 + dw
-                    left[tap * LANES : (tap + 1) * LANES, there] = moved.astype(bf16)
-            for j in range(shards):
-                lanes = slice(j * LANES, (j + 1) * LANES)
-                grad = grads[clip, j, here, :]
-                rights[2][there, lanes] = grad
-                rights[1][there, lanes] = jnp.where(t > 0, grad, jnp.zeros_like(grad))
-                rights[0][there, lanes] = jnp.where(t > 1, grad, jnp.zeros_like(grad))
-            return at + 1
-
-        return lax.fori_loop(0, length, one_frame, base)
-
-    lax.fori_loop(0, clips, one_clip, 0)
-    total = left.shape[1]
-    for dt in range(3):
-        skip = (2 - dt) * block
-        product = jnp.dot(
-            left[:, : total - skip], rights[dt][skip:, :], preferred_element_type=f32
+    for dr in range(3):
+        for dw in range(3):
+            tap = dr * 3 + dw
+            match = source == place + (dr - 1) * columns + dw - 1
+            if dr == 0:
+                match = jnp.logical_and(match, row > 0)
+            if dr == 2:
+                match = jnp.logical_and(match, row < height - 1)
+            if dw == 0:
+                match = jnp.logical_and(match, column > 0)
+            if dw == 2:
+                match = jnp.logical_and(match, column < columns - 1)
+            shifts[:, tap * block : (tap + 1) * block] = match.astype(f32).astype(bf16)
+
+    for slot in range(clips):
+        length = jnp.max(turned[slot][LANES:, :LANES].astype(f32)).astype(jnp.int32)
+        table[slot_clip(info, slot, clips)] = length
+    early = jnp.int32(0)
+    for clip in range(clips):
+        early = early + jnp.maximum(table[clip] - 2, 0)
+    first, middle = jnp.int32(0), early
+    for clip in range(clips):
+        length = table[clip]
+        for t in range(frames):
+            left_over = length - 1 - t
+            at = jnp.where(left_over == 1, middle, first + t)
+            table[clips + clip * frames + t] = jnp.where(left_over == 0, 2 * clips + clip, at)
+        first = first + jnp.maximum(length - 2, 0)
+        middle = middle + jnp.minimum(length - 1, 1)
+
+    for slot in range(clips):
+        clip = slot_clip(info, slot, clips)
+        for t in range(frames):
+
+            @pl.when(t < table[clip])
+            def _(slot=slot, clip=clip, t=t):
+                at = table[clips + clip * frames + t]
+                there = pl.ds(pl.multiple_of(at * LANES, LANES), LANES)
+                images[there, :] = turned[slot][:LANES, t * block : (t + 1) * block]
+
+    step = 4
+    for n in range(0, 3 * clips, step):
+        moved = jnp.dot(
+            images[n * LANES : (n + step) * LANES, :], shifts[...], preferred_element_type=f32
+        ).astype(bf16)
+        for frame in range(step):
+            lanes = slice((n + frame) * block, (n + frame + 1) * block)
+            for tap in range(9):
+                left[tap * LANES : (tap + 1) * LANES, lanes] = moved[
+                    frame * LANES : (frame + 1) * LANES, tap * block : (tap + 1) * block
+                ]
+
+
+def weight_grad_body(frames, height, columns, clips, info, *rest):
+    groups, pieces, out = rest[:6], rest[6:30], rest[30]
+    rights, (product, left, table, images, shifts, near, line) = rest[31:34], rest[34:41]
+    in_sems, sems = rest[41:]
+    block = height * columns
+    fetches = []
+    for kind in range(8):
+        targets = near.at[kind], line.at[kind, pl.ds(0, 2)], line.at[kind, 2]
+        for place, target in enumerate(targets):
+            source = pieces[3 * kind + place]
+            fetches.append(pltpu.make_async_copy(source, target, in_sems.at[3 * kind + place]))
+            fetches[-1].start()
+    fill_taps(frames, height, columns, info, groups, left, table, images, shifts)
+    for fetch in fetches:
+        fetch.wait()
+    held = []
+    for kind in range(8):
+        held.append([near.at[kind], line.at[kind, 0], line.at[kind, 2], line.at[kind, 1]])
+    lines = clips // 2
+    core = lax.bitwise_and(info[1], 1)
+    rights[2][clips * block :, :] = jnp.zeros_like(rights[2][clips * block :, :])
+
+    def place(slot, t, mine):
+        found = []
+        for hop in range(2):
+            same, side, chip, cross = (held[4 * hop + kind][slot % lines] for kind in range(4))
+            if hop != mine:
+                side, chip = chip, side
+            found += [(hop, same), (hop + 2, chip)] if slot < lines else [
+                (hop, side), (hop + 2, cross)
+            ]
+        clip = slot_clip(info, slot, clips)
+        for hop, image in found:
+            part = lax.bitwise_xor(info[1], hop)
+            lanes = pl.ds(pl.multiple_of(part * LANES, LANES), LANES)
+            value = image[t * block : (t + 1) * block, :]
+            for lag in range(min(t + 1, 3)):
+                at = table[clips + clip * frames + t - lag]
+                there = pl.ds(pl.multiple_of(at * block, block), block)
+                rights[lag][there, lanes] = value
+
+    for mine in range(2):
+
+        @pl.when(core == mine)
+        def _(mine=mine):
+            for slot in range(clips):
+                for t in range(frames):
+
+                    @pl.when(t < table[slot_clip(info, slot, clips)])
+                    def _(slot=slot, t=t):
+                        place(slot, t, mine)
+
+    copies = []
+    for lag in range(3):
+        used = rights[lag].shape[0]
+        product[2 - lag] = jnp.dot(
+            left[:, :used], rights[lag][...], preferred_element_type=f32
+        ).reshape(9, LANES, rights[lag].shape[1])
+        copy = pltpu.make_async_copy(
+            product.at[2 - lag], out.at[pl.ds((2 - lag) * 9, 9)], sems.at[lag]
         )
-        out[dt * 9 : (dt + 1) * 9] = product.reshape(9, LANES, product.shape[1])
+        copy.start()
+        copies.append(copy)
+    for copy in copies:
+        copy.wait()
+
+
+def pack(blocks):
+    def body(*refs):
+        for place, ref in enumerate(refs[:-1]):
+            refs[-1][place] = ref[...]
+
+    vmem = pl.BlockSpec(memory_space=pltpu.VMEM)
+    size = len(blocks) * blocks[0].size
+    return pl.pallas_call(
+        body,
+        out_shape=shaped((len(blocks), *blocks[0].shape), blocks[0].dtype),
+        in_specs=[vmem] * len(blocks),
+        out_specs=vmem,
+        compiler_params=pltpu.CompilerParams(vmem_limit_bytes=4 * MIB),
+        cost_estimate=SMALL_COST,
+    )(*blocks)
+
+
+def send(block, target):
+    lines, shards = lax.axis_size("dp") // 2, lax.axis_size("shard")
+    pairs = []
+    for line in range(lines):
+        for side in range(2):
+            for chip in range(shards // 2):
+                for core in range(2):
+                    to_line, to_side, to_chip, to_core = target(line, side, chip, core)
+                    source = (line * 2 + side) * shards + chip * 2 + core
+                    sink = (to_line % lines * 2 + to_side) * shards + to_chip * 2 + to_core
+                    pairs.append((source, sink))
+    return lax.ppermute(block, ("dp", "shard"), pairs)
+
+
+def to_side(line, side, chip, core):
+    return line, 1 - side, chip, core
+
+
+def to_chip(line, side, chip, core):
+    return line, side, 1 - chip, core
+
+
+def to_core(line, side, chip, core):
+    return line, side, chip, 1 - core
+
+
+def to_side_or_chip(line, side, chip, core):
+    return (line, 1 - side, chip, core) if core == 0 else (line, side, 1 - chip, core)
+
+
+def to_chip_or_side(line, side, chip, core):
+    return (line, 1 - side, chip, core) if core == 1 else (line, side, 1 - chip, core)
+
+
+def fence(*values):
+    return lax.optimization_barrier(values)
 
 
 def by_slices(codes, lengths, hidden, embed, conv_weight, gain, bias, cotangent):
@@ -334,11 +538,11 @@
     own_rows = cells * width
     block = height * columns
     here = lax.axis_index("shard")
-    info = jnp.stack([lengths[0], here.astype(jnp.int32)])
+    info = jnp.stack([lengths[0], here, lax.axis_index("dp")])
     hops = range(1, shards)
     flat_weight = conv_weight.transpose(1, 0, 2).reshape(27 * LANES, channels)
 
-    chunk = shaped((own_rows, 2 * LANES), bf16)
+    chunk = shaped((own_rows + BIT_ROWS, 2 * LANES), bf16)
     sent = kernel_call(
         lambda *refs: embed_body(shards, width, height * width, *refs),
         [chunk] * shards,
@@ -346,110 +550,195 @@
             info,
             codes.reshape(own_rows, 1),
             hidden.reshape(own_rows, channels),
-            jnp.pad(embed, ((0, LANES - CODE_BITS), (0, 0))),
+            embed,
             cotangent.reshape(rows, LANES),
         ],
         [
-            pltpu.VMEM((shards, own_rows, 2 * LANES), bf16),
+            pltpu.VMEM((shards, own_rows + BIT_ROWS, 2 * LANES), bf16),
             pltpu.VMEM((rows, LANES), f32),
             pltpu.VMEM((own_rows, LANES), f32),
+            pltpu.VMEM((LANES, channels), bf16),
         ],
         flops=2 * own_rows * LANES * channels,
     )
-    code_row = codes.reshape(1, own_rows)
-    all_codes = [code_row] + [swap(code_row, hop) for hop in hops]
     parts = [sent[0]] + [swap(sent[hop], hop) for hop in hops]
 
     slab = shaped((rows, LANES), bf16)
-    forward = kernel_call(
-        lambda *refs: forward_body(shards, width, frames, height, *refs),
-        [shaped((rows, LANES), f32)] + [slab] * (shards - 1)
-        + [slab, shaped((LANES, rows), bf16), slab],
-        [info, *parts, flat_weight],
+    features, turned, cot_slab = kernel_call(
+        lambda *refs: slab_body(shards, width, cells, *refs),
+        [slab, shaped((LANES + LENGTH_ROWS, rows), bf16), slab],
+        [info, *parts],
         [
             pltpu.VMEM((shards, 2, own_rows, LANES), f32),
             pltpu.VMEM((rows, LANES), f32),
             pltpu.VMEM((rows, LANES), f32),
+        ],
+    )
+    forward = kernel_call(
+        lambda *refs: forward_body(shards, width, frames, height, *refs),
+        [shaped((rows, LANES), f32)] + [slab] * (shards - 1),
+        [info, features, flat_weight],
+        [
             pltpu.VMEM((3, frames + 2, height + 2, columns, LANES), bf16),
             pltpu.VMEM((rows, 27 * LANES), bf16),
             pltpu.VMEM((shards, rows, LANES), f32),
+            pltpu.VMEM((27 * LANES, channels), bf16),
+            pltpu.SemaphoreType.DMA((3,)),
         ],
         flops=2 * rows * 27 * LANES * channels,
-    )
-    own_sum, sum_sends = forward[0], forward[1:shards]
-    turned, cot_slab = forward[shards + 1], forward[shards + 2]
-    all_turned = lax.all_gather(turned, "dp", axis=0)
-    all_lengths = lax.all_gather(lengths, "dp", axis=0, tiled=True)
+        anywhere=(2,),
+    )
+    own_sum, sum_sends = forward[0], forward[1:]
     sum_parts = [swap(sum_sends[hop - 1], hop) for hop in hops]
-
-    small = shaped((own_rows, LANES), bf16)
-    normed = kernel_call(
+    turned, _ = fence(turned, sum_parts[0])
+    line_one, line_three = along_line(turned, 1), along_line(turned, 3)
+    turned_side = send(turned, to_side)
+    own_sum, *sum_parts, turned, line_one, line_three, turned_side = fence(
+        own_sum, *sum_parts, turned, line_one, line_three, turned_side
+    )
+
+    d_conv, terms, act = kernel_call(
         lambda *refs: norm_body(shards, width, frames, height, per_group, *refs),
-        [slab, shaped((8, LANES), f32)] + [small] * shards,
+        [slab, shaped((8, LANES), f32), slab],
         [
             info,
             own_sum,
             *sum_parts,
-            lax.dynamic_slice_in_dim(gain, here * LANES, LANES).reshape(1, LANES),
-            lax.dynamic_slice_in_dim(bias, here * LANES, LANES).reshape(1, LANES),
+            gain.reshape(1, channels),
+            bias.reshape(1, channels),
             cot_slab,
         ],
-        [pltpu.VMEM((rows, LANES), f32)] * 3 + [pltpu.VMEM((shards, own_rows, LANES), f32)],
+        [pltpu.VMEM((rows, LANES), f32)] * 2
+        + [pltpu.VMEM((2, 1, channels), f32), pltpu.SemaphoreType.DMA((2,))],
         flops=rows * LANES * 40,
-    )
-    d_conv, terms, act_sends = normed[0], normed[1], normed[2:]
-    d_parts = [d_conv] + [swap(d_conv, hop) for hop in hops]
-    all_grads = lax.all_gather(d_conv, ("dp", "shard"), axis=0).reshape(
-        clips, shards, rows, LANES
-    )
-    act_parts = [act_sends[0]] + [swap(act_sends[hop], hop) for hop in hops]
-
-    back = kernel_call(
+        anywhere=(5, 6),
+    )
+    same_one, same_three = along_line(d_conv, 1), along_line(d_conv, 3)
+    side = send(d_conv, to_side_or_chip)
+    chip = send(d_conv, to_chip_or_side)
+    same_partner = send(d_conv, to_core)
+    turned_odd = pack([line_one, line_three])
+    turned_sides = send(turned_odd, to_side)
+    d_conv, same_one, same_three, side, chip, same_partner, turned, turned_sides = fence(
+        d_conv, same_one, same_three, side, chip, same_partner, turned, turned_sides
+    )
+
+    same_even = along_line(d_conv, 2)
+    same_odd = pack([same_one, same_three])
+    side_odd = send(same_odd, to_side_or_chip)
+    chip_odd = send(same_odd, to_chip_or_side)
+    cross = send(side, to_chip_or_side)
+    side_partner = send(side, to_core)
+    chip_partner = send(chip, to_core)
+    same_odd_partner = send(same_odd, to_core)
+    mixed = [side, chip, side_partner, chip_partner]
+    joint = shaped((own_rows, 2 * LANES), bf16)
+    small, *joint_sends = kernel_call(
         lambda *refs: input_grad_body(shards, width, frames, height, *refs),
-        [shaped((32, LANES), f32)] + [small] * shards,
-        [info, *d_parts, flat_weight, *all_codes],
+        [shaped((BIT_ROWS, LANES), f32)] + [joint] * shards,
+        [info, d_conv, same_partner, *mixed, flat_weight, act, terms, *parts],
         [
-            pltpu.VMEM((shards, rows, LANES), bf16),
             pltpu.VMEM((rows, channels), bf16),
             pltpu.VMEM((3, frames, height, columns, LANES), f32),
+            pltpu.VMEM((rows, LANES), f32),
             pltpu.VMEM((shards, own_rows, LANES), f32),
+            pltpu.VMEM((rows, LANES), f32),
         ],
         flops=2 * rows * 27 * LANES * channels,
     )
-    embed_term, hidden_sends = back[0], back[1:]
-    hidden_parts = [hidden_sends[0]] + [swap(hidden_sends[hop], hop) for hop in hops]
-    grad_hidden = kernel_call(
-        lambda *refs: hidden_body(shards, *refs),
-        [shaped((own_rows, channels), bf16)],
-        [info, *hidden_parts],
-        [pltpu.VMEM((shards, own_rows, LANES), bf16)],
-    )[0]
-    decoded = kernel_call(
-        lambda *refs: decoded_body(shards, width, *refs),
-        [slab],
-        [info, *act_parts],
+    same_even, side_odd, chip_odd, cross, same_odd_partner, small, turned, *joint_sends = fence(
+        same_even, side_odd, chip_odd, cross, same_odd_partner, small, turned, *joint_sends
+    )
+
+    side_even = send(same_even, to_side_or_chip)
+    chip_even = send(same_even, to_chip_or_side)
+    cross_odd = send(side_odd, to_chip_or_side)
+    turned_even = along_line(turned, 2)
+    joint_parts = [joint_sends[0]] + [swap(joint_sends[hop], hop) for hop in hops]
+    same_even_partner = send(same_even, to_core)
+    side_odd_partner = send(side_odd, to_core)
+    chip_odd_partner = send(chip_odd, to_core)
+    cross_partner = send(cross, to_core)
+    small = small + send(small, to_side)
+    side_even, chip_even, cross_odd, turned_even, small, *joint_parts = fence(
+        side_even, chip_even, cross_odd, turned_even, small, *joint_parts
+    )
+
+    cross_even = send(side_even, to_chip_or_side)
+    turned_side_even = send(turned_even, to_side)
+    side_even_partner = send(side_even, to_core)
+    chip_even_partner = send(chip_even, to_core)
+    cross_odd_partner = send(cross_odd, to_core)
+    small = small + send(small, lambda l, s, c, k: (l ^ 1, s, c, k))
+    grad_hidden, decoded = kernel_call(
+        lambda *refs: finish_body(shards, width, *refs),
+        [shaped((own_rows, channels), bf16), slab],
+        [info, *joint_parts],
         [pltpu.VMEM((shards, own_rows, LANES), f32), pltpu.VMEM((rows, LANES), f32)],
-    )[0]
-    valid = 3 * clips * block
-    grad_weight = kernel_call(
-        lambda *refs: weight_grad_body(frames, height, columns, *refs),
-        [shaped((27, LANES, channels), f32)],
-        [all_lengths, all_turned, all_grads],
-        [pltpu.VMEM((9 * LANES, valid), bf16)] + [pltpu.VMEM((valid, channels), bf16)] * 3,
-        flops=2 * valid * 27 * LANES * channels,
-    )[0]
-    grad_conv = grad_weight.transpose(1, 0, 2)
-
-    small_sum = lax.psum(jnp.concatenate([embed_term, terms], axis=0), "dp")
-    all_small = lax.all_gather(small_sum, "shard", axis=1, tiled=True)
+    )
+    cross_even, turned_side_even, small, _, _ = fence(
+        cross_even, turned_side_even, small, grad_hidden, decoded
+    )
+
+    cross_even_partner = send(cross_even, to_core)
+    small = small + send(small, lambda l, s, c, k: (l ^ 2, s, c, k))
+    small, cross_even_partner = fence(small, cross_even_partner)
+    pieces = [d_conv, same_odd, same_even, side, side_odd, side_even]
+    pieces += [chip, chip_odd, chip_even, cross, cross_odd, cross_even]
+    pieces += [same_partner, same_odd_partner, same_even_partner]
+    pieces += [side_partner, side_odd_partner, side_even_partner]
+    pieces += [chip_partner, chip_odd_partner, chip_even_partner]
+    pieces += [cross_partner, cross_odd_partner, cross_even_partner]
+    groups = [turned, turned_odd, turned_even, turned_side, turned_sides, turned_side_even]
+    grad_weight = weight_grad(info, groups, pieces, frames, height, channels)
+
+    small_parts = [small] + [swap(small, hop) for hop in hops]
+    grad_embed, grad_gain, grad_bias = kernel_call(
+        lambda *refs: terms_body(shards, *refs),
+        [shaped((CODE_BITS, channels), f32)] + [shaped((1, channels), f32)] * 2,
+        [info, *small_parts],
+    )
     return (
         decoded.reshape(1, frames, 2 * height, 2 * width, LANES),
         grad_hidden.reshape(1, frames, height, width, channels),
-        grad_conv,
-        all_small[:CODE_BITS],
-        all_small[32],
-        all_small[33],
-    )
+        grad_weight.transpose(1, 0, 2),
+        grad_embed,
+        grad_gain.reshape(channels),
+        grad_bias.reshape(channels),
+    )
+
+
+def along_line(block, hop):
+    return send(block, lambda l, s, c, k: (l + hop, s, c, k))
+
+
+def weight_grad(info, groups, pieces, frames, height, channels):
+    rows = pieces[0].shape[0]
+    clips = 2 * len(groups[:3]) + 2
+    vmem = pl.BlockSpec(memory_space=pltpu.VMEM)
+    smem = pl.BlockSpec(memory_space=pltpu.SMEM)
+    hbm = pl.BlockSpec(memory_space=pltpu.HBM)
+    counts = [3 * clips * LANES, 2 * clips * LANES, 3 * clips // 2 * LANES]
+    return pl.pallas_call(
+        lambda *refs: weight_grad_body(frames, height, LANES // height, clips, *refs),
+        out_shape=shaped((27, LANES, channels), f32),
+        in_specs=[smem] + [vmem] * len(groups) + [hbm] * len(pieces),
+        out_specs=hbm,
+        scratch_shapes=[pltpu.VMEM((count, channels), bf16) for count in counts]
+        + [
+            pltpu.VMEM((3, 9, LANES, channels), f32),
+            pltpu.VMEM((9 * LANES, counts[0]), bf16),
+            pltpu.SMEM((clips * (frames + 1),), jnp.int32),
+            pltpu.VMEM((counts[0], LANES), bf16),
+            pltpu.VMEM((LANES, 9 * LANES), bf16),
+            pltpu.VMEM((8, rows, LANES), bf16),
+            pltpu.VMEM((8, 3, rows, LANES), bf16),
+            pltpu.SemaphoreType.DMA((len(pieces),)),
+            pltpu.SemaphoreType.DMA((3,)),
+        ],
+        compiler_params=pltpu.CompilerParams(vmem_limit_bytes=WIDE_LIMIT),
+        cost_estimate=SMALL_COST,
+    )(info, *groups, *pieces)
 
 
 def extended(block, sides, width):
@@ -617,7 +906,8 @@
 def on_device(codes, lengths, hidden, embed, conv_weight, gain, bias, cotangent):
     share = conv_weight.shape[0]
     block = codes.shape[2] * codes.shape[3] * lax.axis_size("shard")
-    plan = by_slices if share == LANES and block == LANES else by_gathers
+    fits = share == LANES and block == LANES and lax.axis_size("shard") == 4
+    plan = by_slices if fits and lax.axis_size("dp") == 8 else by_gathers
     return plan(codes, lengths, hidden, embed, conv_weight, gain, bias, cotangent)
 
 

time: 170 us -> 119 us (0.70)
  blocking collectives: 52.4 us -> 0 us
  starting transfers between devices: 12.6 us -> 38 us
  between operations: 14.9 us -> 1.84 us
  Pallas kernels: 42.5 us -> 34.1 us
  local copies, waits for them, and re-layouts: 13.4 us -> 10.8 us
    psum x1 -> x0, blocking collectives: 34.4 us -> none  [by_slices(): small_sum = lax.psum(jnp.concatenate([embed_term, terms], axis=0), 'dp')]
    ppermute x0 -> x33, starting transfers between devices: none -> 30 us  [send(): return lax.ppermute(block, ('dp', 'shard'), pairs)]
    ppermute x0 -> x33, waiting for transfers between devices: none -> 14 us  [send(): return lax.ppermute(block, ('dp', 'shard'), pairs)]
    all_gather x2 -> x0, waiting for transfers between devices: 13.4 us -> none  [the longest x1 13.4 us: by_slices(): lax.all_gather(d_conv, ('dp', 'shard'), axis=0)]
    unnamed x1 -> x0, blocking collectives: 12.5 us -> none
    pallas_call x7 -> x10, Pallas kernels: 42.5 us -> 34.1 us  [the longest x7 17.2 us: kernel_call(): pl.pallas_call(body, out_shape=outs, in_specs=specs, out_specs=[vmem] * l...]
    all_gather x1 -> x0, blocking collectives: 5.46 us -> none  [by_slices(): all_small = lax.all_gather(small_sum, 'shard', axis=1, tiled=True)]
    ppermute x18 -> x12, starting transfers between devices: 12.5 us -> 7.97 us  [swap(): return lax.ppermute(block, 'shard', pairs)]
  transfers between devices with their start and end apart: 20 -> 45, of which waited for: 7 -> 15; matrix products, arithmetic and copies ran while one was open for 4% -> 1% of each run, Pallas kernels for 7% -> 21%
where the time goes in v3:
time: 119 us; the launch traced here: 118 us
  starting transfers between devices  38 us (32%)
  Pallas kernels  34.1 us (29%)
  waiting for transfers between devices  33.7 us (28%)
  local copies, waits for them, and re-layouts  10.8 us (9%)
  between operations  1.84 us (2%)
    ppermute x33, starting transfers between devices, send(): return lax.ppermute(block, ('dp', 'shard'), pairs)  30 us
    ppermute x12, waiting for transfers between devices, swap(): return lax.ppermute(block, 'shard', pairs)  19.7 us
    pallas_call x7, Pallas kernels, kernel_call(): pl.pallas_call(body, out_shape=outs, in_specs=specs, out_specs=[vmem] * l...  17.2 us
    pallas_call x1, Pallas kernels, weight_grad(): pl.pallas_call(lambda *refs: weight_grad_body(frames, height, LANES // he...  16.8 us
    ppermute x33, waiting for transfers between devices, send(): return lax.ppermute(block, ('dp', 'shard'), pairs)  14 us
    unnamed x79, local copies, waits for them, and re-layouts  9.08 us
    ppermute x12, starting transfers between devices, swap(): return lax.ppermute(block, 'shard', pairs)  7.97 us
  transfers between devices with their start and end apart: 45, of which 15 were waited for; matrix products, arithmetic and copies ran while one was open for 1% of the time, Pallas kernels for 21%

profile of v3, /device:TPU:0, one launch (start us, length us, event | category | flops | bytes accessed | tf_op | source)
XLA Modules:
  0.0 118.5 jit_solution(15573526522612353698)
XLA Ops:
  1.3 0.8 copy.15
  2.2 1.0 reshape.43.refs_2_
  3.2 0.9 copy-done.13
  4.9 0.9 shard_map.127
  6.3 2.6 %collective-permute-start.1 = (bf16[192,256]{1,0:T(8,128)(2,1)S(1)}, bf16[192,256]{1,0:T(8,128)(2,1)S(1)}, u32[]{:S(2)}, u32[]{:S(2)}) collective-permute-start(bf16[192,256]{1,0:T(8,128)(2,1)S(1)} %get-tuple-element.74), channel_id=1, source_target_pairs={{0,2},{1,3},{2,0},{3,1},{4,6},{5,7},{6,4},{7,5},{8,10},{9,11},{10,... | collective-permute-start | bytes 294920 | tf_op jit(solution)/shard_map/ppermute | solution.py:59
  9.0 3.6 %collective-permute-done.1.refs_3_.refs_12_ = bf16[192,256]{1,0:T(8,128)(2,1)S(1)} collective-permute-done((bf16[192,256]{1,0:T(8,128)(2,1)S(1)}, bf16[192,256]{1,0:T(8,128)(2,1)S(1)}, u32[]{:S(2)}, u32[]{:S(2)}) %collective-permute-start.1) | collective-permute-done | bytes 98336 | tf_op jit(solution)/shard_map/ppermute | solution.py:59
  12.5 1.6 %collective-permute-done.2.refs_4_.refs_13_ = bf16[192,256]{1,0:T(8,128)(2,1)S(1)} collective-permute-done((bf16[192,256]{1,0:T(8,128)(2,1)S(1)}, bf16[192,256]{1,0:T(8,128)(2,1)S(1)}, u32[]{:S(2)}, u32[]{:S(2)}) %collective-permute-start.2) | collective-permute-done | bytes 98336 | tf_op jit(solution)/shard_map/ppermute | solution.py:59
  14.1 0.9 shard_map.128
  16.4 6.0 %shard_map.129 = (f32[640,128]{1,0:T(8,128)}, bf16[640,128]{1,0:T(8,128)(2,1)}, bf16[640,128]{1,0:T(8,128)(2,1)}, bf16[640,128]{1,0:T(8,128)(2,1)}) custom-call(s32[3]{0:T(128)} %copy-done.14, bf16[640,128]{1,0:T(8,128)(2,1)} %copy-done.11, bf16[3456,512]{1,0:T(8,128)(2,1)} %bitcast.14), custom_call_target="tpu_custom_call" | custom-call | flops 1 | bytes 1 | tf_op jit(solution)/shard_map/pallas_call | solution.py:42
  22.6 1.5 %collective-permute-done.3.refs_2_ = bf16[640,128]{1,0:T(8,128)(2,1)S(1)} collective-permute-done((bf16[640,128]{1,0:T(8,128)(2,1)}, bf16[640,128]{1,0:T(8,128)(2,1)S(1)}, u32[]{:S(2)}, u32[]{:S(2)}) %collective-permute-start.3) | collective-permute-done | bytes 163872 | tf_op jit(solution)/shard_map/ppermute | solution.py:59
  24.0 1.6 %collective-permute-start.6 = (bf16[144,640]{1,0:T(8,128)(2,1)S(1)}, bf16[144,640]{1,0:T(8,128)(2,1)S(1)}, u32[]{:S(2)}, u32[]{:S(2)}) collective-permute-start(bf16[144,640]{1,0:T(8,128)(2,1)S(1)} %get-tuple-element.108.refs_1_), channel_id=1, source_target_pairs={{0,8},{1,9},{2,10},{3,11},{4,12},{5,13},{6,14},{7,15},{8,16},{9,17... | collective-permute-start | bytes 552968 | tf_op jit(solution)/shard_map/ppermute | solution.py:502
  25.7 2.2 %collective-permute-start.7 = (bf16[144,640]{1,0:T(8,128)(2,1)S(1)}, bf16[144,640]{1,0:T(8,128)(2,1)S(1)}, u32[]{:S(2)}, u32[]{:S(2)}) collective-permute-start(bf16[144,640]{1,0:T(8,128)(2,1)S(1)} %get-tuple-element.108.refs_1_), channel_id=1, source_target_pairs={{0,24},{1,25},{2,26},{3,27},{4,28},{5,29},{6,30},{7,31},{8,0},{9,1... | collective-permute-start | bytes 552968 | tf_op jit(solution)/shard_map/ppermute | solution.py:502
  27.9 1.5 %collective-permute-start.8 = (bf16[144,640]{1,0:T(8,128)(2,1)S(1)}, bf16[144,640]{1,0:T(8,128)(2,1)S(1)}, u32[]{:S(2)}, u32[]{:S(2)}) collective-permute-start(bf16[144,640]{1,0:T(8,128)(2,1)S(1)} %get-tuple-element.108.refs_1_), channel_id=1, source_target_pairs={{0,4},{1,5},{2,6},{3,7},{4,0},{5,1},{6,2},{7,3},{8,12},{9,13},{10,... | collective-permute-start | bytes 552968 | tf_op jit(solution)/shard_map/ppermute | solution.py:502
  29.4 1.5 %collective-permute-start.4 = (bf16[640,128]{1,0:T(8,128)(2,1)}, bf16[640,128]{1,0:T(8,128)(2,1)S(1)}, u32[]{:S(2)}, u32[]{:S(2)}) collective-permute-start(bf16[640,128]{1,0:T(8,128)(2,1)} %get-tuple-element.79), channel_id=1, source_target_pairs={{0,2},{1,3},{2,0},{3,1},{4,6},{5,7},{6,4},{7,5},{8,10},{9,11},{10,... | collective-permute-start | bytes 491528 | tf_op jit(solution)/shard_map/ppermute | solution.py:59
  30.9 5.4 %collective-permute-done.4.refs_3_ = bf16[640,128]{1,0:T(8,128)(2,1)S(1)} collective-permute-done((bf16[640,128]{1,0:T(8,128)(2,1)}, bf16[640,128]{1,0:T(8,128)(2,1)S(1)}, u32[]{:S(2)}, u32[]{:S(2)}) %collective-permute-start.4) | collective-permute-done | bytes 163872 | tf_op jit(solution)/shard_map/ppermute | solution.py:59
  36.3 1.6 %collective-permute-done.5.refs_4_ = bf16[640,128]{1,0:T(8,128)(2,1)S(1)} collective-permute-done((bf16[640,128]{1,0:T(8,128)(2,1)}, bf16[640,128]{1,0:T(8,128)(2,1)S(1)}, u32[]{:S(2)}, u32[]{:S(2)}) %collective-permute-start.5) | collective-permute-done | bytes 163872 | tf_op jit(solution)/shard_map/ppermute | solution.py:59
  38.6 3.2 %shard_map.130 = (bf16[640,128]{1,0:T(8,128)(2,1)}, f32[8,128]{1,0:T(8,128)}, bf16[640,128]{1,0:T(8,128)(2,1)}) custom-call(s32[3]{0:T(128)} %copy-done.14, f32[640,128]{1,0:T(8,128)} %get-tuple-element.83.refs_1_, bf16[640,128]{1,0:T(8,128)(2,1)} %copy-done.29, bf16[640,128]{1,0:T(8,128)(2,1)} %copy-done.30, bf16[640,128]{1,0:T(8,128)(2,1)} %copy-done.31, ...), custom_call_target="tpu_custom_call" | custom-call | flops 1 | bytes 1 | tf_op jit(solution)/shard_map/pallas_call | solution.py:42
  42.2 3.5 %collective-permute-start.10 = (bf16[640,128]{1,0:T(8,128)(2,1)}, bf16[640,128]{1,0:T(8,128)(2,1)S(1)}, u32[]{:S(2)}, u32[]{:S(2)}) collective-permute-start(bf16[640,128]{1,0:T(8,128)(2,1)} %get-tuple-element.92.refs_1_.refs_7_), channel_id=1, source_target_pairs={{0,24},{1,25},{2,26},{3,27},{4,28},{5,29},{6,30},{7,31},{8,0},{9,1... | collective-permute-start | bytes 491528 | tf_op jit(solution)/shard_map/ppermute | solution.py:502
  45.7 1.5 %collective-permute-start.11 = (bf16[640,128]{1,0:T(8,128)(2,1)}, bf16[640,128]{1,0:T(8,128)(2,1)S(1)}, u32[]{:S(2)}, u32[]{:S(2)}) collective-permute-start(bf16[640,128]{1,0:T(8,128)(2,1)} %get-tuple-element.92.refs_1_.refs_7_), channel_id=1, source_target_pairs={{0,4},{1,3},{2,6},{3,1},{4,0},{5,7},{6,2},{7,5},{8,12},{9,11},{10,... | collective-permute-start | bytes 491528 | tf_op jit(solution)/shard_map/ppermute | solution.py:502
  47.2 0.8 collective-permute-start.12
  48.0 3.0 %collective-permute-done.9.refs_0_ = bf16[640,128]{1,0:T(8,128)(2,1)S(1)} collective-permute-done((bf16[640,128]{1,0:T(8,128)(2,1)}, bf16[640,128]{1,0:T(8,128)(2,1)S(1)}, u32[]{:S(2)}, u32[]{:S(2)}) %collective-permute-start.9) | collective-permute-done | bytes 163872 | tf_op jit(solution)/shard_map/ppermute | solution.py:502
  51.0 1.4 %collective-permute-done.10.refs_1_ = bf16[640,128]{1,0:T(8,128)(2,1)S(1)} collective-permute-done((bf16[640,128]{1,0:T(8,128)(2,1)}, bf16[640,128]{1,0:T(8,128)(2,1)S(1)}, u32[]{:S(2)}, u32[]{:S(2)}) %collective-permute-start.10) | collective-permute-done | bytes 163872 | tf_op jit(solution)/shard_map/ppermute | solution.py:502
  53.4 1.7 %collective-permute-start.16 = (bf16[2,640,128]{2,1,0:T(8,128)(2,1)S(1)}, bf16[2,640,128]{2,1,0:T(8,128)(2,1)S(1)}, u32[]{:S(2)}, u32[]{:S(2)}) collective-permute-start(bf16[2,640,128]{2,1,0:T(8,128)(2,1)S(1)} %shard_map.132.refs_8_), channel_id=1, source_target_pairs={{0,4},{1,3},{2,6},{3,1},{4,0},{5,7},{6,2},{7,5},{8,12},{9,11},{10,... | collective-permute-start | bytes 983048 | tf_op jit(solution)/shard_map/ppermute | solution.py:502
  55.1 0.8 collective-permute-start.17
  55.8 2.3 %collective-permute-start.15 = (bf16[640,128]{1,0:T(8,128)(2,1)}, bf16[640,128]{1,0:T(8,128)(2,1)S(1)}, u32[]{:S(2)}, u32[]{:S(2)}) collective-permute-start(bf16[640,128]{1,0:T(8,128)(2,1)} %get-tuple-element.92.refs_1_.refs_7_), channel_id=1, source_target_pairs={{0,16},{1,17},{2,18},{3,19},{4,20},{5,21},{6,22},{7,23},{8,24},{9,... | collective-permute-start | bytes 491528 | tf_op jit(solution)/shard_map/ppermute | solution.py:502
  58.9 2.0 %copy-done = bf16[128,27,512]{2,0,1:T(8,128)(2,1)S(1)} copy-done((bf16[128,27,512]{2,0,1:T(8,128)(2,1)S(1)}, bf16[128,27,512]{2,0,1:T(8,128)(2,1)}, u32[]{:S(2)}) %copy-start) | copy-done | bytes 3538968
  60.9 0.9 copy-done.3
  61.8 0.9 copy-done.10
  64.0 3.6 %shard_map.133 = (f32[32,128]{1,0:T(8,128)S(1)}, bf16[160,256]{1,0:T(8,128)(2,1)S(1)}, bf16[160,256]{1,0:T(8,128)(2,1)S(1)}, bf16[160,256]{1,0:T(8,128)(2,1)S(1)}, bf16[160,256]{1,0:T(8,128)(2,1)S(1)}) custom-call(s32[3]{0:T(128)S(1)} %copy-done.15, bf16[640,128]{1,0:T(8,128)(2,1)S(1)} %copy-done.3, ...), custom_call_target="tpu_custom_call" | custom-call | flops 1 | bytes 1 | tf_op jit(solution)/shard_map/pallas_call | solution.py:42
  67.8 1.3 %collective-permute-start.24 = (bf16[2,640,128]{2,1,0:T(8,128)(2,1)S(1)}, bf16[2,640,128]{2,1,0:T(8,128)(2,1)S(1)}, u32[]{:S(2)}, u32[]{:S(2)}) collective-permute-start(bf16[2,640,128]{2,1,0:T(8,128)(2,1)S(1)} %collective-permute-done.16.refs_11_), channel_id=1, source_target_pairs={{0,2},{1,5},{2,0},{3,7},{4,6},{5,1},{6,4},{7,3},{8,10},{9,13},{10,... | collective-permute-start | bytes 983048 | tf_op jit(solution)/shard_map/ppermute | solution.py:502
  69.9 0.9 collective-permute-start.26
  70.8 0.8 collective-permute-start.28
  71.6 2.3 %collective-permute-done.26 = f32[32,128]{1,0:T(8,128)S(1)} collective-permute-done((f32[32,128]{1,0:T(8,128)S(1)}, f32[32,128]{1,0:T(8,128)S(1)}, u32[]{:S(2)}, u32[]{:S(2)}) %collective-permute-start.26) | collective-permute-done | bytes 16416 | tf_op jit(solution)/shard_map/ppermute | solution.py:502
  73.8 0.9 collective-permute-start.22
  74.7 0.8 collective-permute-start.23
  75.5 1.3 %collective-permute-done.28.refs_3_ = bf16[160,256]{1,0:T(8,128)(2,1)S(1)} collective-permute-done((bf16[160,256]{1,0:T(8,128)(2,1)S(1)}, bf16[160,256]{1,0:T(8,128)(2,1)S(1)}, u32[]{:S(2)}, u32[]{:S(2)}) %collective-permute-start.28) | collective-permute-done | bytes 81952 | tf_op jit(solution)/shard_map/ppermute | solution.py:59
  76.9 4.8 %collective-permute-done.29.refs_4_ = bf16[160,256]{1,0:T(8,128)(2,1)S(1)} collective-permute-done((bf16[160,256]{1,0:T(8,128)(2,1)S(1)}, bf16[160,256]{1,0:T(8,128)(2,1)S(1)}, u32[]{:S(2)}, u32[]{:S(2)}) %collective-permute-start.29) | collective-permute-done | bytes 81952 | tf_op jit(solution)/shard_map/ppermute | solution.py:59
  81.7 1.1 collective-permute-start.31
  83.5 0.8 collective-permute-start.32
  84.6 2.7 %collective-permute-done.32 = f32[32,128]{1,0:T(8,128)S(1)} collective-permute-done((f32[32,128]{1,0:T(8,128)S(1)}, f32[32,128]{1,0:T(8,128)S(1)}, u32[]{:S(2)}, u32[]{:S(2)}) %collective-permute-start.32) | collective-permute-done | bytes 16416 | tf_op jit(solution)/shard_map/ppermute | solution.py:502
  87.3 0.8 collective-permute-done.30.refs_18_
  88.1 1.9 %collective-permute-start.36 = (bf16[2,640,128]{2,1,0:T(8,128)(2,1)S(1)}, bf16[2,640,128]{2,1,0:T(8,128)(2,1)S(1)}, u32[]{:S(2)}, u32[]{:S(2)}) collective-permute-start(bf16[2,640,128]{2,1,0:T(8,128)(2,1)S(1)} %collective-permute-done.17.refs_14_), channel_id=1, source_target_pairs={{0,1},{1,0},{2,3},{3,2},{4,5},{5,4},{6,7},{7,6},{8,9},{9,8},{10,11... | collective-permute-start | bytes 983048 | tf_op jit(solution)/shard_map/ppermute | solution.py:502
  90.0 1.4 %shard_map.134 = (bf16[160,512]{1,0:T(8,128)(2,1)S(1)}, bf16[640,128]{1,0:T(8,128)(2,1)}) custom-call(s32[3]{0:T(128)S(1)} %copy-done.15, bf16[160,256]{1,0:T(8,128)(2,1)S(1)} %get-tuple-element.114.refs_1_, bf16[160,256]{1,0:T(8,128)(2,1)S(1)} %collective-permute-done.27.refs_2_, bf16[160,256]{1,0:T(8,128)(2,1)S(1)} %collective-permute-done.28.refs_3_, ...), custom_call_target="tpu_custom_call" | custom-call | flops 1 | bytes 1 | tf_op jit(solution)/shard_map/pallas_call | solution.py:42
  92.1 1.3 %collective-permute-start.40 = (f32[32,128]{1,0:T(8,128)S(1)}, f32[32,128]{1,0:T(8,128)S(1)}, u32[]{:S(2)}, u32[]{:S(2)}) collective-permute-start(f32[32,128]{1,0:T(8,128)S(1)} %add.10), channel_id=1, source_target_pairs={{0,16},{1,17},{2,18},{3,19},{4,20},{5,21},{6,22},{7,23},{8,24},{9,... | collective-permute-start | bytes 49160 | tf_op jit(solution)/shard_map/ppermute | solution.py:502
  93.4 3.3 %collective-permute-done.40 = f32[32,128]{1,0:T(8,128)S(1)} collective-permute-done((f32[32,128]{1,0:T(8,128)S(1)}, f32[32,128]{1,0:T(8,128)S(1)}, u32[]{:S(2)}, u32[]{:S(2)}) %collective-permute-start.40) | collective-permute-done | bytes 16416 | tf_op jit(solution)/shard_map/ppermute | solution.py:502
  97.4 1.5 %collective-permute-start.43 = (f32[32,128]{1,0:T(8,128)S(1)}, f32[32,128]{1,0:T(8,128)S(1)}, u32[]{:S(2)}, u32[]{:S(2)}) collective-permute-start(f32[32,128]{1,0:T(8,128)S(1)} %add.11.refs_1_), channel_id=1, source_target_pairs={{0,2},{1,3},{2,0},{3,1},{4,6},{5,7},{6,4},{7,5},{8,10},{9,11},{10,... | collective-permute-start | bytes 49160 | tf_op jit(solution)/shard_map/ppermute | solution.py:59
  100.5 16.8 %shard_map.135 = f32[27,128,512]{2,1,0:T(8,128)} custom-call(s32[3]{0:T(128)} %copy-done.14, bf16[144,640]{1,0:T(8,128)(2,1)} %copy-done.9, bf16[2,144,640]{2,1,0:T(8,128)(2,1)} %copy-done.1, bf16[144,640]{1,0:T(8,128)(2,1)} %copy-done.27, bf16[144,640]{1,0:T(8,128)(2,1)} %copy-done.26, bf16[2,144,640]{2,1,0:T(8,128)(2,1)} %copy-done.19, ...), custom_call_target="tpu_custom_call" | custom-call | flops 1 | bytes 1 | tf_op jit(solution)/shard_map/pallas_call | solution.py:722
  117.3 1.2 shard_map.136
  (138 shorter events, 11.6 us)
Async XLA Ops:
  5.8 3.2 %collective-permute-start = (bf16[192,256]{1,0:T(8,128)(2,1)S(1)}, bf16[192,256]{1,0:T(8,128)(2,1)S(1)}, u32[]{:S(2)}, u32[]{:S(2)}) collective-permute-start(bf16[192,256]{1,0:T(8,128)(2,1)S(1)} %get-tuple-element.73), channel_id=1, source_target_pairs={{0,1},{1,0},{2,3},{3,2},{4,5},{5,4},{6,7},{7,6},{8,9},{9,8},{10,11... | collective-permute-start | bytes 294920 | tf_op jit(solution)/shard_map/ppermute | solution.py:59
  6.3 6.2 %collective-permute-start.1 = (bf16[192,256]{1,0:T(8,128)(2,1)S(1)}, bf16[192,256]{1,0:T(8,128)(2,1)S(1)}, u32[]{:S(2)}, u32[]{:S(2)}) collective-permute-start(bf16[192,256]{1,0:T(8,128)(2,1)S(1)} %get-tuple-element.74), channel_id=1, source_target_pairs={{0,2},{1,3},{2,0},{3,1},{4,6},{5,7},{6,4},{7,5},{8,10},{9,11},{10,... | collective-permute-start | bytes 294920 | tf_op jit(solution)/shard_map/ppermute | solution.py:59
  8.9 5.2 %collective-permute-start.2 = (bf16[192,256]{1,0:T(8,128)(2,1)S(1)}, bf16[192,256]{1,0:T(8,128)(2,1)S(1)}, u32[]{:S(2)}, u32[]{:S(2)}) collective-permute-start(bf16[192,256]{1,0:T(8,128)(2,1)S(1)} %get-tuple-element.75), channel_id=1, source_target_pairs={{0,3},{1,2},{2,1},{3,0},{4,7},{5,6},{6,5},{7,4},{8,11},{9,10},{10,... | collective-permute-start | bytes 294920 | tf_op jit(solution)/shard_map/ppermute | solution.py:59
  16.4 84.0 %copy-start.9 = (bf16[144,640]{1,0:T(8,128)(2,1)}, bf16[144,640]{1,0:T(8,128)(2,1)S(1)}, u32[]{:S(2)}) copy-start(bf16[144,640]{1,0:T(8,128)(2,1)S(1)} %get-tuple-element.108.refs_1_) | copy-start | bytes 552964
  22.4 1.7 %collective-permute-start.3 = (bf16[640,128]{1,0:T(8,128)(2,1)}, bf16[640,128]{1,0:T(8,128)(2,1)S(1)}, u32[]{:S(2)}, u32[]{:S(2)}) collective-permute-start(bf16[640,128]{1,0:T(8,128)(2,1)} %get-tuple-element.78), channel_id=1, source_target_pairs={{0,1},{1,0},{2,3},{3,2},{4,5},{5,4},{6,7},{7,6},{8,9},{9,8},{10,11... | collective-permute-start | bytes 491528 | tf_op jit(solution)/shard_map/ppermute | solution.py:59
  24.0 13.8 %collective-permute-start.6 = (bf16[144,640]{1,0:T(8,128)(2,1)S(1)}, bf16[144,640]{1,0:T(8,128)(2,1)S(1)}, u32[]{:S(2)}, u32[]{:S(2)}) collective-permute-start(bf16[144,640]{1,0:T(8,128)(2,1)S(1)} %get-tuple-element.108.refs_1_), channel_id=1, source_target_pairs={{0,8},{1,9},{2,10},{3,11},{4,12},{5,13},{6,14},{7,15},{8,16},{9,17... | collective-permute-start | bytes 552968 | tf_op jit(solution)/shard_map/ppermute | solution.py:502
  25.7 12.2 %collective-permute-start.7 = (bf16[144,640]{1,0:T(8,128)(2,1)S(1)}, bf16[144,640]{1,0:T(8,128)(2,1)S(1)}, u32[]{:S(2)}, u32[]{:S(2)}) collective-permute-start(bf16[144,640]{1,0:T(8,128)(2,1)S(1)} %get-tuple-element.108.refs_1_), channel_id=1, source_target_pairs={{0,24},{1,25},{2,26},{3,27},{4,28},{5,29},{6,30},{7,31},{8,0},{9,1... | collective-permute-start | bytes 552968 | tf_op jit(solution)/shard_map/ppermute | solution.py:502
  27.9 10.0 %collective-permute-start.8 = (bf16[144,640]{1,0:T(8,128)(2,1)S(1)}, bf16[144,640]{1,0:T(8,128)(2,1)S(1)}, u32[]{:S(2)}, u32[]{:S(2)}) collective-permute-start(bf16[144,640]{1,0:T(8,128)(2,1)S(1)} %get-tuple-element.108.refs_1_), channel_id=1, source_target_pairs={{0,4},{1,5},{2,6},{3,7},{4,0},{5,1},{6,2},{7,3},{8,12},{9,13},{10,... | collective-permute-start | bytes 552968 | tf_op jit(solution)/shard_map/ppermute | solution.py:502
  29.4 6.9 %collective-permute-start.4 = (bf16[640,128]{1,0:T(8,128)(2,1)}, bf16[640,128]{1,0:T(8,128)(2,1)S(1)}, u32[]{:S(2)}, u32[]{:S(2)}) collective-permute-start(bf16[640,128]{1,0:T(8,128)(2,1)} %get-tuple-element.79), channel_id=1, source_target_pairs={{0,2},{1,3},{2,0},{3,1},{4,6},{5,7},{6,4},{7,5},{8,10},{9,11},{10,... | collective-permute-start | bytes 491528 | tf_op jit(solution)/shard_map/ppermute | solution.py:59
  30.9 6.9 %collective-permute-start.5 = (bf16[640,128]{1,0:T(8,128)(2,1)}, bf16[640,128]{1,0:T(8,128)(2,1)S(1)}, u32[]{:S(2)}, u32[]{:S(2)}) collective-permute-start(bf16[640,128]{1,0:T(8,128)(2,1)} %get-tuple-element.80), channel_id=1, source_target_pairs={{0,3},{1,2},{2,1},{3,0},{4,7},{5,6},{6,5},{7,4},{8,11},{9,10},{10,... | collective-permute-start | bytes 491528 | tf_op jit(solution)/shard_map/ppermute | solution.py:59
  37.9 62.5 %copy-start.26 = (bf16[144,640]{1,0:T(8,128)(2,1)}, bf16[144,640]{1,0:T(8,128)(2,1)S(1)}, u32[]{:S(2)}) copy-start(bf16[144,640]{1,0:T(8,128)(2,1)S(1)} %collective-permute-done.8.refs_4_) | copy-start | bytes 552964
  37.9 62.5 %copy-start.1 = (bf16[2,144,640]{2,1,0:T(8,128)(2,1)}, bf16[2,144,640]{2,1,0:T(8,128)(2,1)S(1)}, u32[]{:S(2)}) copy-start(bf16[2,144,640]{2,1,0:T(8,128)(2,1)S(1)} %shard_map.131.refs_2_) | copy-start | bytes 1105924
  37.9 14.8 %collective-permute-start.14 = (bf16[2,144,640]{2,1,0:T(8,128)(2,1)S(1)}, bf16[2,144,640]{2,1,0:T(8,128)(2,1)S(1)}, u32[]{:S(2)}, u32[]{:S(2)}) collective-permute-start(bf16[2,144,640]{2,1,0:T(8,128)(2,1)S(1)} %shard_map.131.refs_2_), channel_id=1, source_target_pairs={{0,4},{1,5},{2,6},{3,7},{4,0},{5,1},{6,2},{7,3},{8,12},{9,13},{10,... | collective-permute-start | bytes 1105928 | tf_op jit(solution)/shard_map/ppermute | solution.py:502
  41.8 9.2 %collective-permute-start.9 = (bf16[640,128]{1,0:T(8,128)(2,1)}, bf16[640,128]{1,0:T(8,128)(2,1)S(1)}, u32[]{:S(2)}, u32[]{:S(2)}) collective-permute-start(bf16[640,128]{1,0:T(8,128)(2,1)} %get-tuple-element.92.refs_1_.refs_7_), channel_id=1, source_target_pairs={{0,8},{1,9},{2,10},{3,11},{4,12},{5,13},{6,14},{7,15},{8,16},{9,17... | collective-permute-start | bytes 491528 | tf_op jit(solution)/shard_map/ppermute | solution.py:502
  42.2 10.2 %collective-permute-start.10 = (bf16[640,128]{1,0:T(8,128)(2,1)}, bf16[640,128]{1,0:T(8,128)(2,1)S(1)}, u32[]{:S(2)}, u32[]{:S(2)}) collective-permute-start(bf16[640,128]{1,0:T(8,128)(2,1)} %get-tuple-element.92.refs_1_.refs_7_), channel_id=1, source_target_pairs={{0,24},{1,25},{2,26},{3,27},{4,28},{5,29},{6,30},{7,31},{8,0},{9,1... | collective-permute-start | bytes 491528 | tf_op jit(solution)/shard_map/ppermute | solution.py:502
  45.7 7.0 %collective-permute-start.11 = (bf16[640,128]{1,0:T(8,128)(2,1)}, bf16[640,128]{1,0:T(8,128)(2,1)S(1)}, u32[]{:S(2)}, u32[]{:S(2)}) collective-permute-start(bf16[640,128]{1,0:T(8,128)(2,1)} %get-tuple-element.92.refs_1_.refs_7_), channel_id=1, source_target_pairs={{0,4},{1,3},{2,6},{3,1},{4,0},{5,7},{6,2},{7,5},{8,12},{9,11},{10,... | collective-permute-start | bytes 491528 | tf_op jit(solution)/shard_map/ppermute | solution.py:502
  47.2 5.6 %collective-permute-start.12 = (bf16[640,128]{1,0:T(8,128)(2,1)}, bf16[640,128]{1,0:T(8,128)(2,1)S(1)}, u32[]{:S(2)}, u32[]{:S(2)}) collective-permute-start(bf16[640,128]{1,0:T(8,128)(2,1)} %get-tuple-element.92.refs_1_.refs_7_), channel_id=1, source_target_pairs={{0,2},{1,5},{2,0},{3,7},{4,6},{5,1},{6,4},{7,3},{8,10},{9,13},{10,... | collective-permute-start | bytes 491528 | tf_op jit(solution)/shard_map/ppermute | solution.py:502
  51.0 1.7 %collective-permute-start.13 = (bf16[640,128]{1,0:T(8,128)(2,1)}, bf16[640,128]{1,0:T(8,128)(2,1)S(1)}, u32[]{:S(2)}, u32[]{:S(2)}) collective-permute-start(bf16[640,128]{1,0:T(8,128)(2,1)} %get-tuple-element.92.refs_1_.refs_7_), channel_id=1, source_target_pairs={{0,1},{1,0},{2,3},{3,2},{4,5},{5,4},{6,7},{7,6},{8,9},{9,8},{10,11... | collective-permute-start | bytes 491528 | tf_op jit(solution)/shard_map/ppermute | solution.py:502
  52.8 3.1 %collective-permute-start.20 = (bf16[640,128]{1,0:T(8,128)(2,1)S(1)}, bf16[640,128]{1,0:T(8,128)(2,1)S(1)}, u32[]{:S(2)}, u32[]{:S(2)}) collective-permute-start(bf16[640,128]{1,0:T(8,128)(2,1)S(1)} %collective-permute-done.11.refs_3_.refs_10_), channel_id=1, source_target_pairs={{0,1},{1,0},{2,3},{3,2},{4,5},{5,4},{6,7},{7,6},{8,9},{9,8},{10,11... | collective-permute-start | bytes 491528 | tf_op jit(solution)/shard_map/ppermute | solution.py:502
  52.9 5.2 %collective-permute-start.21 = (bf16[640,128]{1,0:T(8,128)(2,1)S(1)}, bf16[640,128]{1,0:T(8,128)(2,1)S(1)}, u32[]{:S(2)}, u32[]{:S(2)}) collective-permute-start(bf16[640,128]{1,0:T(8,128)(2,1)S(1)} %collective-permute-done.12.refs_4_.refs_13_), channel_id=1, source_target_pairs={{0,1},{1,0},{2,3},{3,2},{4,5},{5,4},{6,7},{7,6},{8,9},{9,8},{10,11... | collective-permute-start | bytes 491528 | tf_op jit(solution)/shard_map/ppermute | solution.py:502
  53.4 14.4 %collective-permute-start.16 = (bf16[2,640,128]{2,1,0:T(8,128)(2,1)S(1)}, bf16[2,640,128]{2,1,0:T(8,128)(2,1)S(1)}, u32[]{:S(2)}, u32[]{:S(2)}) collective-permute-start(bf16[2,640,128]{2,1,0:T(8,128)(2,1)S(1)} %shard_map.132.refs_8_), channel_id=1, source_target_pairs={{0,4},{1,3},{2,6},{3,1},{4,0},{5,7},{6,2},{7,5},{8,12},{9,11},{10,... | collective-permute-start | bytes 983048 | tf_op jit(solution)/shard_map/ppermute | solution.py:502
  55.1 12.7 %collective-permute-start.17 = (bf16[2,640,128]{2,1,0:T(8,128)(2,1)S(1)}, bf16[2,640,128]{2,1,0:T(8,128)(2,1)S(1)}, u32[]{:S(2)}, u32[]{:S(2)}) collective-permute-start(bf16[2,640,128]{2,1,0:T(8,128)(2,1)S(1)} %shard_map.132.refs_8_), channel_id=1, source_target_pairs={{0,2},{1,5},{2,0},{3,7},{4,6},{5,1},{6,4},{7,3},{8,10},{9,13},{10,... | collective-permute-start | bytes 983048 | tf_op jit(solution)/shard_map/ppermute | solution.py:502
  55.8 12.0 %collective-permute-start.19 = (bf16[2,640,128]{2,1,0:T(8,128)(2,1)S(1)}, bf16[2,640,128]{2,1,0:T(8,128)(2,1)S(1)}, u32[]{:S(2)}, u32[]{:S(2)}) collective-permute-start(bf16[2,640,128]{2,1,0:T(8,128)(2,1)S(1)} %shard_map.132.refs_8_), channel_id=1, source_target_pairs={{0,1},{1,0},{2,3},{3,2},{4,5},{5,4},{6,7},{7,6},{8,9},{9,8},{10,11... | collective-permute-start | bytes 983048 | tf_op jit(solution)/shard_map/ppermute | solution.py:502
  55.8 11.9 %collective-permute-start.15 = (bf16[640,128]{1,0:T(8,128)(2,1)}, bf16[640,128]{1,0:T(8,128)(2,1)S(1)}, u32[]{:S(2)}, u32[]{:S(2)}) collective-permute-start(bf16[640,128]{1,0:T(8,128)(2,1)} %get-tuple-element.92.refs_1_.refs_7_), channel_id=1, source_target_pairs={{0,16},{1,17},{2,18},{3,19},{4,20},{5,21},{6,22},{7,23},{8,24},{9,... | collective-permute-start | bytes 491528 | tf_op jit(solution)/shard_map/ppermute | solution.py:502
  58.1 9.6 %collective-permute-start.18 = (bf16[640,128]{1,0:T(8,128)(2,1)S(1)}, bf16[640,128]{1,0:T(8,128)(2,1)S(1)}, u32[]{:S(2)}, u32[]{:S(2)}) collective-permute-start(bf16[640,128]{1,0:T(8,128)(2,1)S(1)} %collective-permute-done.11.refs_3_.refs_10_), channel_id=1, source_target_pairs={{0,2},{1,5},{2,0},{3,7},{4,6},{5,1},{6,4},{7,3},{8,10},{9,13},{10,... | collective-permute-start | bytes 491528 | tf_op jit(solution)/shard_map/ppermute | solution.py:502
  67.8 13.9 %collective-permute-start.24 = (bf16[2,640,128]{2,1,0:T(8,128)(2,1)S(1)}, bf16[2,640,128]{2,1,0:T(8,128)(2,1)S(1)}, u32[]{:S(2)}, u32[]{:S(2)}) collective-permute-start(bf16[2,640,128]{2,1,0:T(8,128)(2,1)S(1)} %collective-permute-done.16.refs_11_), channel_id=1, source_target_pairs={{0,2},{1,5},{2,0},{3,7},{4,6},{5,1},{6,4},{7,3},{8,10},{9,13},{10,... | collective-permute-start | bytes 983048 | tf_op jit(solution)/shard_map/ppermute | solution.py:502
  69.2 5.6 %collective-permute-start.27 = (bf16[160,256]{1,0:T(8,128)(2,1)S(1)}, bf16[160,256]{1,0:T(8,128)(2,1)S(1)}, u32[]{:S(2)}, u32[]{:S(2)}) collective-permute-start(bf16[160,256]{1,0:T(8,128)(2,1)S(1)} %get-tuple-element.111), channel_id=1, source_target_pairs={{0,1},{1,0},{2,3},{3,2},{4,5},{5,4},{6,7},{7,6},{8,9},{9,8},{10,11... | collective-permute-start | bytes 245768 | tf_op jit(solution)/shard_map/ppermute | solution.py:59
  69.2 12.5 %collective-permute-start.25 = (bf16[144,640]{1,0:T(8,128)(2,1)S(1)}, bf16[144,640]{1,0:T(8,128)(2,1)S(1)}, u32[]{:S(2)}, u32[]{:S(2)}) collective-permute-start(bf16[144,640]{1,0:T(8,128)(2,1)S(1)} %get-tuple-element.108.refs_1_), channel_id=1, source_target_pairs={{0,16},{1,17},{2,18},{3,19},{4,20},{5,21},{6,22},{7,23},{8,24},{9,... | collective-permute-start | bytes 552968 | tf_op jit(solution)/shard_map/ppermute | solution.py:502
  69.9 3.9 %collective-permute-start.26 = (f32[32,128]{1,0:T(8,128)S(1)}, f32[32,128]{1,0:T(8,128)S(1)}, u32[]{:S(2)}, u32[]{:S(2)}) collective-permute-start(f32[32,128]{1,0:T(8,128)S(1)} %get-tuple-element.109), channel_id=1, source_target_pairs={{0,4},{1,5},{2,6},{3,7},{4,0},{5,1},{6,2},{7,3},{8,12},{9,13},{10,... | collective-permute-start | bytes 49160 | tf_op jit(solution)/shard_map/ppermute | solution.py:502
  70.8 6.1 %collective-permute-start.28 = (bf16[160,256]{1,0:T(8,128)(2,1)S(1)}, bf16[160,256]{1,0:T(8,128)(2,1)S(1)}, u32[]{:S(2)}, u32[]{:S(2)}) collective-permute-start(bf16[160,256]{1,0:T(8,128)(2,1)S(1)} %get-tuple-element.112), channel_id=1, source_target_pairs={{0,2},{1,3},{2,0},{3,1},{4,6},{5,7},{6,4},{7,5},{8,10},{9,11},{10,... | collective-permute-start | bytes 245768 | tf_op jit(solution)/shard_map/ppermute | solution.py:59
  73.8 7.8 %collective-permute-start.22 = (bf16[640,128]{1,0:T(8,128)(2,1)S(1)}, bf16[640,128]{1,0:T(8,128)(2,1)S(1)}, u32[]{:S(2)}, u32[]{:S(2)}) collective-permute-start(bf16[640,128]{1,0:T(8,128)(2,1)S(1)} %collective-permute-done.15.refs_9_), channel_id=1, source_target_pairs={{0,4},{1,3},{2,6},{3,1},{4,0},{5,7},{6,2},{7,5},{8,12},{9,11},{10,... | collective-permute-start | bytes 491528 | tf_op jit(solution)/shard_map/ppermute | solution.py:502
  74.7 6.9 %collective-permute-start.23 = (bf16[640,128]{1,0:T(8,128)(2,1)S(1)}, bf16[640,128]{1,0:T(8,128)(2,1)}, u32[]{:S(2)}, u32[]{:S(2)}) collective-permute-start(bf16[640,128]{1,0:T(8,128)(2,1)S(1)} %collective-permute-done.15.refs_9_), channel_id=1, source_target_pairs={{0,2},{1,5},{2,0},{3,7},{4,6},{5,1},{6,4},{7,3},{8,10},{9,13},{10,... | collective-permute-start | bytes 491528 | tf_op jit(solution)/shard_map/ppermute | solution.py:502
  76.9 4.8 %collective-permute-start.29 = (bf16[160,256]{1,0:T(8,128)(2,1)S(1)}, bf16[160,256]{1,0:T(8,128)(2,1)S(1)}, u32[]{:S(2)}, u32[]{:S(2)}) collective-permute-start(bf16[160,256]{1,0:T(8,128)(2,1)S(1)} %get-tuple-element.113), channel_id=1, source_target_pairs={{0,3},{1,2},{2,1},{3,0},{4,7},{5,6},{6,5},{7,4},{8,11},{9,10},{10,... | collective-permute-start | bytes 245768 | tf_op jit(solution)/shard_map/ppermute | solution.py:59
  81.7 9.8 %collective-permute-start.31 = (bf16[144,640]{1,0:T(8,128)(2,1)S(1)}, bf16[144,640]{1,0:T(8,128)(2,1)S(1)}, u32[]{:S(2)}, u32[]{:S(2)}) collective-permute-start(bf16[144,640]{1,0:T(8,128)(2,1)S(1)} %collective-permute-done.25.refs_3_), channel_id=1, source_target_pairs={{0,4},{1,5},{2,6},{3,7},{4,0},{5,1},{6,2},{7,3},{8,12},{9,13},{10,... | collective-permute-start | bytes 552968 | tf_op jit(solution)/shard_map/ppermute | solution.py:502
  82.8 5.3 %collective-permute-start.30 = (bf16[640,128]{1,0:T(8,128)(2,1)S(1)}, bf16[640,128]{1,0:T(8,128)(2,1)S(1)}, u32[]{:S(2)}, u32[]{:S(2)}) collective-permute-start(bf16[640,128]{1,0:T(8,128)(2,1)S(1)} %collective-permute-done.22.refs_12_), channel_id=1, source_target_pairs={{0,2},{1,5},{2,0},{3,7},{4,6},{5,1},{6,4},{7,3},{8,10},{9,13},{10,... | collective-permute-start | bytes 491528 | tf_op jit(solution)/shard_map/ppermute | solution.py:502
  83.5 8.1 %collective-permute-start.33 = (bf16[640,128]{1,0:T(8,128)(2,1)S(1)}, bf16[640,128]{1,0:T(8,128)(2,1)S(1)}, u32[]{:S(2)}, u32[]{:S(2)}) collective-permute-start(bf16[640,128]{1,0:T(8,128)(2,1)S(1)} %collective-permute-done.15.refs_9_), channel_id=1, source_target_pairs={{0,1},{1,0},{2,3},{3,2},{4,5},{5,4},{6,7},{7,6},{8,9},{9,8},{10,11... | collective-permute-start | bytes 491528 | tf_op jit(solution)/shard_map/ppermute | solution.py:502
  83.5 3.7 %collective-permute-start.32 = (f32[32,128]{1,0:T(8,128)S(1)}, f32[32,128]{1,0:T(8,128)S(1)}, u32[]{:S(2)}, u32[]{:S(2)}) collective-permute-start(f32[32,128]{1,0:T(8,128)S(1)} %add.9), channel_id=1, source_target_pairs={{0,8},{1,9},{2,10},{3,11},{4,12},{5,13},{6,14},{7,15},{8,0},{9,1},... | collective-permute-start | bytes 49160 | tf_op jit(solution)/shard_map/ppermute | solution.py:502
  84.3 7.8 %collective-permute-start.38 = (bf16[640,128]{1,0:T(8,128)(2,1)S(1)}, bf16[640,128]{1,0:T(8,128)(2,1)S(1)}, u32[]{:S(2)}, u32[]{:S(2)}) collective-permute-start(bf16[640,128]{1,0:T(8,128)(2,1)S(1)} %collective-permute-done.18.refs_16_), channel_id=1, source_target_pairs={{0,1},{1,0},{2,3},{3,2},{4,5},{5,4},{6,7},{7,6},{8,9},{9,8},{10,11... | collective-permute-start | bytes 491528 | tf_op jit(solution)/shard_map/ppermute | solution.py:502
  87.3 10.0 %collective-permute-start.34 = (bf16[2,640,128]{2,1,0:T(8,128)(2,1)S(1)}, bf16[2,640,128]{2,1,0:T(8,128)(2,1)S(1)}, u32[]{:S(2)}, u32[]{:S(2)}) collective-permute-start(bf16[2,640,128]{2,1,0:T(8,128)(2,1)S(1)} %collective-permute-done.16.refs_11_), channel_id=1, source_target_pairs={{0,1},{1,0},{2,3},{3,2},{4,5},{5,4},{6,7},{7,6},{8,9},{9,8},{10,11... | collective-permute-start | bytes 983048 | tf_op jit(solution)/shard_map/ppermute | solution.py:502
  88.1 9.3 %collective-permute-start.36 = (bf16[2,640,128]{2,1,0:T(8,128)(2,1)S(1)}, bf16[2,640,128]{2,1,0:T(8,128)(2,1)S(1)}, u32[]{:S(2)}, u32[]{:S(2)}) collective-permute-start(bf16[2,640,128]{2,1,0:T(8,128)(2,1)S(1)} %collective-permute-done.17.refs_14_), channel_id=1, source_target_pairs={{0,1},{1,0},{2,3},{3,2},{4,5},{5,4},{6,7},{7,6},{8,9},{9,8},{10,11... | collective-permute-start | bytes 983048 | tf_op jit(solution)/shard_map/ppermute | solution.py:502
  91.5 5.2 %collective-permute-start.41 = (bf16[640,128]{1,0:T(8,128)(2,1)S(1)}, bf16[640,128]{1,0:T(8,128)(2,1)S(1)}, u32[]{:S(2)}, u32[]{:S(2)}) collective-permute-start(bf16[640,128]{1,0:T(8,128)(2,1)S(1)} %collective-permute-done.30.refs_18_), channel_id=1, source_target_pairs={{0,1},{1,0},{2,3},{3,2},{4,5},{5,4},{6,7},{7,6},{8,9},{9,8},{10,11... | collective-permute-start | bytes 491528 | tf_op jit(solution)/shard_map/ppermute | solution.py:502
  91.6 8.8 %collective-permute-start.39 = (bf16[2,640,128]{2,1,0:T(8,128)(2,1)S(1)}, bf16[2,640,128]{2,1,0:T(8,128)(2,1)}, u32[]{:S(2)}, u32[]{:S(2)}) collective-permute-start(bf16[2,640,128]{2,1,0:T(8,128)(2,1)S(1)} %collective-permute-done.24.refs_17_), channel_id=1, source_target_pairs={{0,1},{1,0},{2,3},{3,2},{4,5},{5,4},{6,7},{7,6},{8,9},{9,8},{10,11... | collective-permute-start | bytes 983048 | tf_op jit(solution)/shard_map/ppermute | solution.py:502
  92.1 4.6 %collective-permute-start.40 = (f32[32,128]{1,0:T(8,128)S(1)}, f32[32,128]{1,0:T(8,128)S(1)}, u32[]{:S(2)}, u32[]{:S(2)}) collective-permute-start(f32[32,128]{1,0:T(8,128)S(1)} %add.10), channel_id=1, source_target_pairs={{0,16},{1,17},{2,18},{3,19},{4,20},{5,21},{6,22},{7,23},{8,24},{9,... | collective-permute-start | bytes 49160 | tf_op jit(solution)/shard_map/ppermute | solution.py:502
  96.7 2.2 %collective-permute-start.35 = (bf16[640,128]{1,0:T(8,128)(2,1)S(1)}, bf16[640,128]{1,0:T(8,128)(2,1)}, u32[]{:S(2)}, u32[]{:S(2)}) collective-permute-start(bf16[640,128]{1,0:T(8,128)(2,1)S(1)} %collective-permute-done.22.refs_12_), channel_id=1, source_target_pairs={{0,1},{1,0},{2,3},{3,2},{4,5},{5,4},{6,7},{7,6},{8,9},{9,8},{10,11... | collective-permute-start | bytes 491528 | tf_op jit(solution)/shard_map/ppermute | solution.py:502
  96.7 3.6 %collective-permute-start.37 = (bf16[640,128]{1,0:T(8,128)(2,1)}, bf16[640,128]{1,0:T(8,128)(2,1)}, u32[]{:S(2)}, u32[]{:S(2)}) collective-permute-start(bf16[640,128]{1,0:T(8,128)(2,1)} %collective-permute-done.23.refs_15_), channel_id=1, source_target_pairs={{0,1},{1,0},{2,3},{3,2},{4,5},{5,4},{6,7},{7,6},{8,9},{9,8},{10,11... | collective-permute-start | bytes 491528 | tf_op jit(solution)/shard_map/ppermute | solution.py:502
  97.3 20.0 %collective-permute-start.42 = (f32[32,128]{1,0:T(8,128)S(1)}, f32[32,128]{1,0:T(8,128)S(1)}, u32[]{:S(2)}, u32[]{:S(2)}) collective-permute-start(f32[32,128]{1,0:T(8,128)S(1)} %add.11.refs_1_), channel_id=1, source_target_pairs={{0,1},{1,0},{2,3},{3,2},{4,5},{5,4},{6,7},{7,6},{8,9},{9,8},{10,11... | collective-permute-start | bytes 49160 | tf_op jit(solution)/shard_map/ppermute | solution.py:59
  97.4 19.9 %collective-permute-start.43 = (f32[32,128]{1,0:T(8,128)S(1)}, f32[32,128]{1,0:T(8,128)S(1)}, u32[]{:S(2)}, u32[]{:S(2)}) collective-permute-start(f32[32,128]{1,0:T(8,128)S(1)} %add.11.refs_1_), channel_id=1, source_target_pairs={{0,2},{1,3},{2,0},{3,1},{4,6},{5,7},{6,4},{7,5},{8,10},{9,11},{10,... | collective-permute-start | bytes 49160 | tf_op jit(solution)/shard_map/ppermute | solution.py:59
  99.0 18.3 %collective-permute-start.44 = (f32[32,128]{1,0:T(8,128)S(1)}, f32[32,128]{1,0:T(8,128)S(1)}, u32[]{:S(2)}, u32[]{:S(2)}) collective-permute-start(f32[32,128]{1,0:T(8,128)S(1)} %add.11.refs_1_), channel_id=1, source_target_pairs={{0,3},{1,2},{2,1},{3,0},{4,7},{5,6},{6,5},{7,4},{8,11},{9,10},{10,... | collective-permute-start | bytes 49160 | tf_op jit(solution)/shard_map/ppermute | solution.py:59
  (36 other events, 630.9 us)

commit v4 on v3

--- a/solution.py
+++ b/solution.py
@@ -95,6 +95,15 @@
         sends[hop][...] = chunks[lax.bitwise_xor(info[1], hop)]
 
 
+def stage_body(weight, gain, bias, weight_out, scale_out, sem):
+    copy = pltpu.make_async_copy(weight, weight_out, sem.at[0])
+    copy.start()
+    scale_out[...] = jnp.zeros_like(scale_out)
+    scale_out[0:1, :] = gain[...]
+    scale_out[1:2, :] = bias[...]
+    copy.wait()
+
+
 def slab_body(shards, width, cells, info, *rest):
     parts, (slab_out, turned_out, cot_out) = rest[:shards], rest[shards : shards + 3]
     chunks, slab, cot = rest[shards + 3 :]
@@ -115,14 +124,8 @@
     turned_out[LANES:, :] = jnp.full((LENGTH_ROWS, rows), info[0].astype(f32)).astype(bf16)
 
 
-def forward_body(shards, width, frames, height, info, slab, weight, own_out, *rest):
-    sends, (rims, patches, sums, held, sems) = rest[: shards - 1], rest[shards - 1 :]
-    span = 9 * LANES
-    copies = []
-    for dt in range(3):
-        chunk = pl.ds(dt * span, span)
-        copies.append(pltpu.make_async_copy(weight.at[chunk], held.at[chunk], sems.at[dt]))
-        copies[dt].start()
+def forward_body(shards, width, frames, height, far, info, slab, weight, *rest):
+    outs, (rims, patches, sums) = rest[:2], rest[2:]
     columns = width * shards
     rows = frames * height * columns
     middle = slab[...].astype(f32)
@@ -144,19 +147,14 @@
                 patches[:, tap * LANES : (tap + 1) * LANES] = rims[
                     dw, dt : dt + frames, dr : dr + height
                 ].reshape(rows, LANES)
-    for dt in range(3):
-        copies[dt].wait()
-        chunk = slice(dt * span, (dt + 1) * span)
-        total = jnp.dot(patches[:, chunk], held[chunk, :], preferred_element_type=f32)
-        for part in range(shards):
-            piece = total[:, part * LANES : (part + 1) * LANES]
-            if dt == 0:
-                sums[part] = piece
-            else:
-                sums[part] += piece
-    own_out[...] = sums[info[1]]
-    for hop in range(1, shards):
-        sends[hop - 1][...] = sums[lax.bitwise_xor(info[1], hop)].astype(bf16)
+    chip = lax.bitwise_xor(info[1] // 2, far)
+    lanes = pl.ds(pl.multiple_of(chip * 2 * LANES, 2 * LANES), 2 * LANES)
+    total = jnp.dot(patches[...], weight[:, lanes], preferred_element_type=f32)
+    sums[0] = total[:, :LANES]
+    sums[1] = total[:, LANES:]
+    core = lax.bitwise_and(info[1], 1)
+    outs[0][...] = sums[core].astype(outs[0].dtype)
+    outs[1][...] = sums[1 - core].astype(bf16)
 
 
 def group_total(values, per_group):
@@ -176,13 +174,10 @@
 
 def norm_body(shards, width, frames, height, per_group, info, *rest):
     own, parts = rest[0], rest[1:shards]
-    gain_all, bias_all, cot, d_conv_out, terms_out, act = rest[shards : shards + 6]
-    conv, slope, scale, sems = rest[shards + 6 :]
+    scale, cot, d_conv_out, terms_out, act = rest[shards : shards + 5]
+    conv, slope = rest[shards + 5 :]
     own_lanes = pl.ds(pl.multiple_of(info[1] * LANES, LANES), LANES)
-    copies = []
-    for place, source in enumerate((gain_all, bias_all)):
-        copies.append(pltpu.make_async_copy(source, scale.at[place], sems.at[place]))
-        copies[place].start()
+    gain, bias = scale[0:1, own_lanes], scale[1:2, own_lanes]
     columns = width * shards
     block = height * columns
     length = info[0]
@@ -202,9 +197,6 @@
     variance = group_total(sum_two, per_group) / count - mean * mean
     inv_std = lax.rsqrt(variance + eps_norm)[:1]
     mean = mean[:1]
-    for copy in copies:
-        copy.wait()
-    gain, bias = scale[0, :, own_lanes], scale[1, :, own_lanes]
     gain_sum = jnp.zeros((8, LANES), f32)
     bias_sum = jnp.zeros((8, LANES), f32)
     for t in range(frames):
@@ -562,6 +554,17 @@
         flops=2 * own_rows * LANES * channels,
     )
     parts = [sent[0]] + [swap(sent[hop], hop) for hop in hops]
+    vmem = pl.BlockSpec(memory_space=pltpu.VMEM)
+    held_weight, scale = pl.pallas_call(
+        stage_body,
+        out_shape=[shaped(flat_weight.shape, bf16), shaped((8, channels), f32)],
+        in_specs=[pl.BlockSpec(memory_space=pltpu.HBM), vmem, vmem],
+        out_specs=[vmem, vmem],
+        scratch_shapes=[pltpu.SemaphoreType.DMA((1,))],
+        compiler_params=pltpu.CompilerParams(vmem_limit_bytes=8 * MIB),
+        cost_estimate=SMALL_COST,
+    )(flat_weight, gain.reshape(1, channels), bias.reshape(1, channels))
+    held_weight, scale, *parts = fence(held_weight, scale, *parts)
 
     slab = shaped((rows, LANES), bf16)
     features, turned, cot_slab = kernel_call(
@@ -574,28 +577,28 @@
             pltpu.VMEM((rows, LANES), f32),
         ],
     )
-    forward = kernel_call(
-        lambda *refs: forward_body(shards, width, frames, height, *refs),
-        [shaped((rows, LANES), f32)] + [slab] * (shards - 1),
-        [info, features, flat_weight],
-        [
-            pltpu.VMEM((3, frames + 2, height + 2, columns, LANES), bf16),
-            pltpu.VMEM((rows, 27 * LANES), bf16),
-            pltpu.VMEM((shards, rows, LANES), f32),
-            pltpu.VMEM((27 * LANES, channels), bf16),
-            pltpu.SemaphoreType.DMA((3,)),
-        ],
-        flops=2 * rows * 27 * LANES * channels,
-        anywhere=(2,),
-    )
-    own_sum, sum_sends = forward[0], forward[1:]
-    sum_parts = [swap(sum_sends[hop - 1], hop) for hop in hops]
-    turned, _ = fence(turned, sum_parts[0])
     line_one, line_three = along_line(turned, 1), along_line(turned, 3)
     turned_side = send(turned, to_side)
-    own_sum, *sum_parts, turned, line_one, line_three, turned_side = fence(
-        own_sum, *sum_parts, turned, line_one, line_three, turned_side
-    )
+
+    def forward_half(image, far, own_type):
+        return kernel_call(
+            lambda *refs: forward_body(shards, width, frames, height, far, *refs),
+            [shaped((rows, LANES), own_type), slab],
+            [info, image, held_weight],
+            [
+                pltpu.VMEM((3, frames + 2, height + 2, columns, LANES), bf16),
+                pltpu.VMEM((rows, 27 * LANES), bf16),
+                pltpu.VMEM((2, rows, LANES), f32),
+            ],
+            flops=rows * 27 * LANES * channels,
+        )
+
+    far_sends = forward_half(features, 1, bf16)
+    features, turned, line_one, line_three, turned_side, _ = fence(
+        features, turned, line_one, line_three, turned_side, far_sends[0]
+    )
+    own_sum, near_send = forward_half(features, 0, f32)
+    sum_parts = [swap(near_send, 1), swap(far_sends[0], 2), swap(far_sends[1], 3)]
 
     d_conv, terms, act = kernel_call(
         lambda *refs: norm_body(shards, width, frames, height, per_group, *refs),
@@ -604,14 +607,11 @@
             info,
             own_sum,
             *sum_parts,
-            gain.reshape(1, channels),
-            bias.reshape(1, channels),
+            scale,
             cot_slab,
         ],
-        [pltpu.VMEM((rows, LANES), f32)] * 2
-        + [pltpu.VMEM((2, 1, channels), f32), pltpu.SemaphoreType.DMA((2,))],
+        [pltpu.VMEM((rows, LANES), f32)] * 2,
         flops=rows * LANES * 40,
-        anywhere=(5, 6),
     )
     same_one, same_three = along_line(d_conv, 1), along_line(d_conv, 3)
     side = send(d_conv, to_side_or_chip)
@@ -636,7 +636,7 @@
     small, *joint_sends = kernel_call(
         lambda *refs: input_grad_body(shards, width, frames, height, *refs),
         [shaped((BIT_ROWS, LANES), f32)] + [joint] * shards,
-        [info, d_conv, same_partner, *mixed, flat_weight, act, terms, *parts],
+        [info, d_conv, same_partner, *mixed, held_weight, act, terms, *parts],
         [
             pltpu.VMEM((rows, channels), bf16),
             pltpu.VMEM((3, frames, height, columns, LANES), f32),
@@ -681,8 +681,6 @@
     )
 
     cross_even_partner = send(cross_even, to_core)
-    small = small + send(small, lambda l, s, c, k: (l ^ 2, s, c, k))
-    small, cross_even_partner = fence(small, cross_even_partner)
     pieces = [d_conv, same_odd, same_even, side, side_odd, side_even]
     pieces += [chip, chip_odd, chip_even, cross, cross_odd, cross_even]
     pieces += [same_partner, same_odd_partner, same_even_partner]
@@ -692,6 +690,7 @@
     groups = [turned, turned_odd, turned_even, turned_side, turned_sides, turned_side_even]
     grad_weight = weight_grad(info, groups, pieces, frames, height, channels)
 
+    small = small + send(small, lambda l, s, c, k: (l ^ 2, s, c, k))
     small_parts = [small] + [swap(small, hop) for hop in hops]
     grad_embed, grad_gain, grad_bias = kernel_call(
         lambda *refs: terms_body(shards, *refs),

time: 119 us -> 110 us (0.924)
  Pallas kernels: 34.1 us -> 31.2 us
  local copies, waits for them, and re-layouts: 10.8 us -> 8.22 us
  waiting for transfers between devices: 33.7 us -> 31.5 us
    ppermute x12, waiting for transfers between devices: 19.7 us -> 10.2 us  [swap(): return lax.ppermute(block, 'shard', pairs)]
    ppermute x33, waiting for transfers between devices: 14 us -> 21.3 us  [send(): return lax.ppermute(block, ('dp', 'shard'), pairs)]
    pallas_call x7 -> x8, Pallas kernels: 17.2 us -> 14 us  [kernel_call(): pl.pallas_call(body, out_shape=outs, in_specs=specs, out_specs=[vmem] * l...]
    unnamed x79 -> x57, local copies, waits for them, and re-layouts: 9.08 us -> 6.47 us
  transfers between devices with their start and end apart: 45 -> 45, of which waited for: 15 -> 15; matrix products, arithmetic and copies ran while one was open for 1% -> 1% of each run, Pallas kernels for 21% -> 12%
where the time goes in v4:
time: 110 us
  starting transfers between devices  36.9 us (34%)
  waiting for transfers between devices  31.5 us (29%)
  Pallas kernels  31.2 us (28%)
  local copies, waits for them, and re-layouts  8.22 us (7%)
  between operations  2.01 us (2%)
    ppermute x33, starting transfers between devices, send(): return lax.ppermute(block, ('dp', 'shard'), pairs)  29.2 us
    ppermute x33, waiting for transfers between devices, send(): return lax.ppermute(block, ('dp', 'shard'), pairs)  21.3 us
    pallas_call x1, Pallas kernels, weight_grad(): pl.pallas_call(lambda *refs: weight_grad_body(frames, height, LANES // he...  16.7 us
    pallas_call x8, Pallas kernels, kernel_call(): pl.pallas_call(body, out_shape=outs, in_specs=specs, out_specs=[vmem] * l...  14 us
    ppermute x12, waiting for transfers between devices, swap(): return lax.ppermute(block, 'shard', pairs)  10.2 us
    ppermute x12, starting transfers between devices, swap(): return lax.ppermute(block, 'shard', pairs)  7.7 us
    unnamed x57, local copies, waits for them, and re-layouts  6.47 us
  transfers between devices with their start and end apart: 45, of which 15 were waited for; matrix products, arithmetic and copies ran while one was open for 1% of the time, Pallas kernels for 12%

profile of v4, /device:TPU:0, one launch (start us, length us, event | category | flops | bytes accessed | tf_op | source)
XLA Modules:
  0.0 109.9 jit_solution(9553148621944790760)
XLA Ops:
  1.3 0.8 copy.15
  2.2 1.0 reshape.46.refs_2_
  3.2 0.9 copy-done.10
  4.1 0.7 copy-done.12
  4.9 0.9 shard_map.128
  6.3 2.6 %collective-permute-start.1 = (bf16[192,256]{1,0:T(8,128)(2,1)S(1)}, bf16[192,256]{1,0:T(8,128)(2,1)S(1)}, u32[]{:S(2)}, u32[]{:S(2)}) collective-permute-start(bf16[192,256]{1,0:T(8,128)(2,1)S(1)} %get-tuple-element.78), channel_id=1, source_target_pairs={{0,2},{1,3},{2,0},{3,1},{4,6},{5,7},{6,4},{7,5},{8,10},{9,11},{10,... | collective-permute-start | bytes 294920 | tf_op jit(solution)/shard_map/ppermute | solution.py:59
  9.0 2.0 %copy-done = bf16[128,27,512]{2,0,1:T(8,128)(2,1)S(1)} copy-done((bf16[128,27,512]{2,0,1:T(8,128)(2,1)S(1)}, bf16[128,27,512]{2,0,1:T(8,128)(2,1)}, u32[]{:S(2)}) %copy-start) | copy-done | bytes 3538968
  12.8 1.4 %collective-permute-done.2.refs_4_.refs_13_ = bf16[192,256]{1,0:T(8,128)(2,1)S(1)} collective-permute-done((bf16[192,256]{1,0:T(8,128)(2,1)S(1)}, bf16[192,256]{1,0:T(8,128)(2,1)S(1)}, u32[]{:S(2)}, u32[]{:S(2)}) %collective-permute-start.2) | collective-permute-done | bytes 98336 | tf_op jit(solution)/shard_map/ppermute | solution.py:59
  14.1 0.9 shard_map.129
  15.1 1.7 %collective-permute-start.3 = (bf16[144,640]{1,0:T(8,128)(2,1)S(1)}, bf16[144,640]{1,0:T(8,128)(2,1)S(1)}, u32[]{:S(2)}, u32[]{:S(2)}) collective-permute-start(bf16[144,640]{1,0:T(8,128)(2,1)S(1)} %get-tuple-element.114.refs_1_), channel_id=1, source_target_pairs={{0,8},{1,9},{2,10},{3,11},{4,12},{5,13},{6,14},{7,15},{8,16},{9,17... | collective-permute-start | bytes 552968 | tf_op jit(solution)/shard_map/ppermute | solution.py:494
  16.7 2.2 %collective-permute-start.4 = (bf16[144,640]{1,0:T(8,128)(2,1)S(1)}, bf16[144,640]{1,0:T(8,128)(2,1)S(1)}, u32[]{:S(2)}, u32[]{:S(2)}) collective-permute-start(bf16[144,640]{1,0:T(8,128)(2,1)S(1)} %get-tuple-element.114.refs_1_), channel_id=1, source_target_pairs={{0,24},{1,25},{2,26},{3,27},{4,28},{5,29},{6,30},{7,31},{8,0},{9,1... | collective-permute-start | bytes 552968 | tf_op jit(solution)/shard_map/ppermute | solution.py:494
  18.9 1.5 %collective-permute-start.5 = (bf16[144,640]{1,0:T(8,128)(2,1)S(1)}, bf16[144,640]{1,0:T(8,128)(2,1)S(1)}, u32[]{:S(2)}, u32[]{:S(2)}) collective-permute-start(bf16[144,640]{1,0:T(8,128)(2,1)S(1)} %get-tuple-element.114.refs_1_), channel_id=1, source_target_pairs={{0,4},{1,5},{2,6},{3,7},{4,0},{5,1},{6,2},{7,3},{8,12},{9,13},{10,... | collective-permute-start | bytes 552968 | tf_op jit(solution)/shard_map/ppermute | solution.py:494
  20.5 2.3 %shard_map.130 = (bf16[640,128]{1,0:T(8,128)(2,1)S(1)}, bf16[640,128]{1,0:T(8,128)(2,1)S(1)}) custom-call(s32[3]{0:T(128)S(1)} %pad_add_fusion.refs_0_, bf16[640,128]{1,0:T(8,128)(2,1)S(1)} %get-tuple-element.88.refs_1_, bf16[3456,512]{1,0:T(8,128)(2,1)S(1)} %get-tuple-element.86.refs_2_.refs_7_), custom_call_target="tpu_custom_call" | custom-call | flops 1 | bytes 1 | tf_op jit(solution)/shard_map/pallas_call | solution.py:42
  22.8 1.5 %collective-permute-start.7 = (bf16[640,128]{1,0:T(8,128)(2,1)S(1)}, bf16[640,128]{1,0:T(8,128)(2,1)S(1)}, u32[]{:S(2)}, u32[]{:S(2)}) collective-permute-start(bf16[640,128]{1,0:T(8,128)(2,1)S(1)} %get-tuple-element.87), channel_id=1, source_target_pairs={{0,2},{1,3},{2,0},{3,1},{4,6},{5,7},{6,4},{7,5},{8,10},{9,11},{10,... | collective-permute-start | bytes 491528 | tf_op jit(solution)/shard_map/ppermute | solution.py:59
  24.4 2.8 %collective-permute-done.4.refs_1_ = bf16[144,640]{1,0:T(8,128)(2,1)S(1)} collective-permute-done((bf16[144,640]{1,0:T(8,128)(2,1)S(1)}, bf16[144,640]{1,0:T(8,128)(2,1)S(1)}, u32[]{:S(2)}, u32[]{:S(2)}) %collective-permute-start.4) | collective-permute-done | bytes 184352 | tf_op jit(solution)/shard_map/ppermute | solution.py:494
  27.2 2.2 %shard_map.131 = (f32[640,128]{1,0:T(8,128)S(1)}, bf16[640,128]{1,0:T(8,128)(2,1)S(1)}) custom-call(s32[3]{0:T(128)S(1)} %pad_add_fusion.refs_0_, bf16[640,128]{1,0:T(8,128)(2,1)S(1)} %get-tuple-element.88.refs_1_, bf16[3456,512]{1,0:T(8,128)(2,1)S(1)} %get-tuple-element.86.refs_2_.refs_7_), custom_call_target="tpu_custom_call" | custom-call | flops 1 | bytes 1 | tf_op jit(solution)/shard_map/pallas_call | solution.py:42
  29.6 1.6 %collective-permute-start.14 = (bf16[2,144,640]{2,1,0:T(8,128)(2,1)S(1)}, bf16[2,144,640]{2,1,0:T(8,128)(2,1)S(1)}, u32[]{:S(2)}, u32[]{:S(2)}) collective-permute-start(bf16[2,144,640]{2,1,0:T(8,128)(2,1)S(1)} %shard_map.133.refs_2_), channel_id=1, source_target_pairs={{0,4},{1,5},{2,6},{3,7},{4,0},{5,1},{6,2},{7,3},{8,12},{9,13},{10,... | collective-permute-start | bytes 1105928 | tf_op jit(solution)/shard_map/ppermute | solution.py:494
  31.1 1.5 %shard_map.132 = (bf16[640,128]{1,0:T(8,128)(2,1)S(1)}, f32[8,128]{1,0:T(8,128)S(1)}, bf16[640,128]{1,0:T(8,128)(2,1)S(1)}) custom-call(s32[3]{0:T(128)S(1)} %pad_add_fusion.refs_0_, f32[640,128]{1,0:T(8,128)S(1)} %get-tuple-element.89.refs_1_, bf16[640,128]{1,0:T(8,128)(2,1)S(1)} %collective-permute-done.6.refs_2_, ...), custom_call_target="tpu_custom_call" | custom-call | flops 1 | bytes 1 | tf_op jit(solution)/shard_map/pallas_call | solution.py:42
  32.7 1.2 %collective-permute-start.9 = (bf16[640,128]{1,0:T(8,128)(2,1)S(1)}, bf16[640,128]{1,0:T(8,128)(2,1)S(1)}, u32[]{:S(2)}, u32[]{:S(2)}) collective-permute-start(bf16[640,128]{1,0:T(8,128)(2,1)S(1)} %get-tuple-element.98.refs_1_.refs_7_), channel_id=1, source_target_pairs={{0,8},{1,9},{2,10},{3,11},{4,12},{5,13},{6,14},{7,15},{8,16},{9,17... | collective-permute-start | bytes 491528 | tf_op jit(solution)/shard_map/ppermute | solution.py:494
  33.9 2.7 %collective-permute-start.10 = (bf16[640,128]{1,0:T(8,128)(2,1)S(1)}, bf16[640,128]{1,0:T(8,128)(2,1)S(1)}, u32[]{:S(2)}, u32[]{:S(2)}) collective-permute-start(bf16[640,128]{1,0:T(8,128)(2,1)S(1)} %get-tuple-element.98.refs_1_.refs_7_), channel_id=1, source_target_pairs={{0,24},{1,25},{2,26},{3,27},{4,28},{5,29},{6,30},{7,31},{8,0},{9,1... | collective-permute-start | bytes 491528 | tf_op jit(solution)/shard_map/ppermute | solution.py:494
  36.6 1.3 %collective-permute-start.11 = (bf16[640,128]{1,0:T(8,128)(2,1)S(1)}, bf16[640,128]{1,0:T(8,128)(2,1)S(1)}, u32[]{:S(2)}, u32[]{:S(2)}) collective-permute-start(bf16[640,128]{1,0:T(8,128)(2,1)S(1)} %get-tuple-element.98.refs_1_.refs_7_), channel_id=1, source_target_pairs={{0,4},{1,3},{2,6},{3,1},{4,0},{5,7},{6,2},{7,5},{8,12},{9,11},{10,... | collective-permute-start | bytes 491528 | tf_op jit(solution)/shard_map/ppermute | solution.py:494
  37.8 1.6 %collective-permute-start.12 = (bf16[640,128]{1,0:T(8,128)(2,1)S(1)}, bf16[640,128]{1,0:T(8,128)(2,1)S(1)}, u32[]{:S(2)}, u32[]{:S(2)}) collective-permute-start(bf16[640,128]{1,0:T(8,128)(2,1)S(1)} %get-tuple-element.98.refs_1_.refs_7_), channel_id=1, source_target_pairs={{0,2},{1,5},{2,0},{3,7},{4,6},{5,1},{6,4},{7,3},{8,10},{9,13},{10,... | collective-permute-start | bytes 491528 | tf_op jit(solution)/shard_map/ppermute | solution.py:494
  39.4 2.3 %collective-permute-done.9.refs_0_ = bf16[640,128]{1,0:T(8,128)(2,1)S(1)} collective-permute-done((bf16[640,128]{1,0:T(8,128)(2,1)S(1)}, bf16[640,128]{1,0:T(8,128)(2,1)S(1)}, u32[]{:S(2)}, u32[]{:S(2)}) %collective-permute-start.9) | collective-permute-done | bytes 163872 | tf_op jit(solution)/shard_map/ppermute | solution.py:494
  41.7 1.8 %collective-permute-done.10.refs_1_ = bf16[640,128]{1,0:T(8,128)(2,1)S(1)} collective-permute-done((bf16[640,128]{1,0:T(8,128)(2,1)S(1)}, bf16[640,128]{1,0:T(8,128)(2,1)S(1)}, u32[]{:S(2)}, u32[]{:S(2)}) %collective-permute-start.10) | collective-permute-done | bytes 163872 | tf_op jit(solution)/shard_map/ppermute | solution.py:494
  43.4 0.7 collective-permute-done.11.refs_3_.refs_10_
  44.8 1.6 %collective-permute-start.16 = (bf16[2,640,128]{2,1,0:T(8,128)(2,1)S(1)}, bf16[2,640,128]{2,1,0:T(8,128)(2,1)S(1)}, u32[]{:S(2)}, u32[]{:S(2)}) collective-permute-start(bf16[2,640,128]{2,1,0:T(8,128)(2,1)S(1)} %shard_map.134.refs_8_), channel_id=1, source_target_pairs={{0,4},{1,3},{2,6},{3,1},{4,0},{5,7},{6,2},{7,5},{8,12},{9,11},{10,... | collective-permute-start | bytes 983048 | tf_op jit(solution)/shard_map/ppermute | solution.py:494
  46.3 1.6 %collective-permute-start.17 = (bf16[2,640,128]{2,1,0:T(8,128)(2,1)S(1)}, bf16[2,640,128]{2,1,0:T(8,128)(2,1)S(1)}, u32[]{:S(2)}, u32[]{:S(2)}) collective-permute-start(bf16[2,640,128]{2,1,0:T(8,128)(2,1)S(1)} %shard_map.134.refs_8_), channel_id=1, source_target_pairs={{0,2},{1,5},{2,0},{3,7},{4,6},{5,1},{6,4},{7,3},{8,10},{9,13},{10,... | collective-permute-start | bytes 983048 | tf_op jit(solution)/shard_map/ppermute | solution.py:494
  47.9 1.4 %collective-permute-start.15 = (bf16[640,128]{1,0:T(8,128)(2,1)S(1)}, bf16[640,128]{1,0:T(8,128)(2,1)S(1)}, u32[]{:S(2)}, u32[]{:S(2)}) collective-permute-start(bf16[640,128]{1,0:T(8,128)(2,1)S(1)} %get-tuple-element.98.refs_1_.refs_7_), channel_id=1, source_target_pairs={{0,16},{1,17},{2,18},{3,19},{4,20},{5,21},{6,22},{7,23},{8,24},{9,... | collective-permute-start | bytes 491528 | tf_op jit(solution)/shard_map/ppermute | solution.py:494
  49.8 3.6 %shard_map.135 = (f32[32,128]{1,0:T(8,128)S(1)}, bf16[160,256]{1,0:T(8,128)(2,1)S(1)}, bf16[160,256]{1,0:T(8,128)(2,1)S(1)}, bf16[160,256]{1,0:T(8,128)(2,1)S(1)}, bf16[160,256]{1,0:T(8,128)(2,1)S(1)}) custom-call(s32[3]{0:T(128)S(1)} %pad_add_fusion.refs_0_, bf16[640,128]{1,0:T(8,128)(2,1)S(1)} %get-tuple-element.98.refs_1_.refs_7_, ...), custom_call_target="tpu_custom_call" | custom-call | flops 1 | bytes 1 | tf_op jit(solution)/shard_map/pallas_call | solution.py:42
  53.4 5.6 %collective-permute-done.15.refs_9_ = bf16[640,128]{1,0:T(8,128)(2,1)S(1)} collective-permute-done((bf16[640,128]{1,0:T(8,128)(2,1)S(1)}, bf16[640,128]{1,0:T(8,128)(2,1)S(1)}, u32[]{:S(2)}, u32[]{:S(2)}) %collective-permute-start.15) | collective-permute-done | bytes 163872 | tf_op jit(solution)/shard_map/ppermute | solution.py:494
  59.6 1.1 %collective-permute-start.26 = (f32[32,128]{1,0:T(8,128)S(1)}, f32[32,128]{1,0:T(8,128)S(1)}, u32[]{:S(2)}, u32[]{:S(2)}) collective-permute-start(f32[32,128]{1,0:T(8,128)S(1)} %get-tuple-element.115), channel_id=1, source_target_pairs={{0,4},{1,5},{2,6},{3,7},{4,0},{5,1},{6,2},{7,3},{8,12},{9,13},{10,... | collective-permute-start | bytes 49160 | tf_op jit(solution)/shard_map/ppermute | solution.py:494
  60.8 0.9 collective-permute-start.28
  61.7 1.9 %collective-permute-done.26 = f32[32,128]{1,0:T(8,128)S(1)} collective-permute-done((f32[32,128]{1,0:T(8,128)S(1)}, f32[32,128]{1,0:T(8,128)S(1)}, u32[]{:S(2)}, u32[]{:S(2)}) %collective-permute-start.26) | collective-permute-done | bytes 16416 | tf_op jit(solution)/shard_map/ppermute | solution.py:494
  63.6 1.1 %collective-permute-start.22 = (bf16[640,128]{1,0:T(8,128)(2,1)S(1)}, bf16[640,128]{1,0:T(8,128)(2,1)}, u32[]{:S(2)}, u32[]{:S(2)}) collective-permute-start(bf16[640,128]{1,0:T(8,128)(2,1)S(1)} %collective-permute-done.15.refs_9_), channel_id=1, source_target_pairs={{0,4},{1,3},{2,6},{3,1},{4,0},{5,7},{6,2},{7,5},{8,12},{9,11},{10,... | collective-permute-start | bytes 491528 | tf_op jit(solution)/shard_map/ppermute | solution.py:494
  64.8 0.9 collective-permute-start.23
  65.7 2.2 %collective-permute-done.28.refs_3_ = bf16[160,256]{1,0:T(8,128)(2,1)S(1)} collective-permute-done((bf16[160,256]{1,0:T(8,128)(2,1)S(1)}, bf16[160,256]{1,0:T(8,128)(2,1)S(1)}, u32[]{:S(2)}, u32[]{:S(2)}) %collective-permute-start.28) | collective-permute-done | bytes 81952 | tf_op jit(solution)/shard_map/ppermute | solution.py:59
  67.9 5.0 %collective-permute-done.29.refs_4_ = bf16[160,256]{1,0:T(8,128)(2,1)S(1)} collective-permute-done((bf16[160,256]{1,0:T(8,128)(2,1)S(1)}, bf16[160,256]{1,0:T(8,128)(2,1)S(1)}, u32[]{:S(2)}, u32[]{:S(2)}) %collective-permute-start.29) | collective-permute-done | bytes 81952 | tf_op jit(solution)/shard_map/ppermute | solution.py:59
  73.8 0.9 collective-permute-start.34
  74.7 1.4 %collective-permute-start.32 = (f32[32,128]{1,0:T(8,128)S(1)}, f32[32,128]{1,0:T(8,128)S(1)}, u32[]{:S(2)}, u32[]{:S(2)}) collective-permute-start(f32[32,128]{1,0:T(8,128)S(1)} %add.9), channel_id=1, source_target_pairs={{0,8},{1,9},{2,10},{3,11},{4,12},{5,13},{6,14},{7,15},{8,0},{9,1},... | collective-permute-start | bytes 49160 | tf_op jit(solution)/shard_map/ppermute | solution.py:494
  76.3 1.4 %shard_map.136 = (bf16[160,512]{1,0:T(8,128)(2,1)S(1)}, bf16[640,128]{1,0:T(8,128)(2,1)}) custom-call(s32[3]{0:T(128)S(1)} %pad_add_fusion.refs_0_, bf16[160,256]{1,0:T(8,128)(2,1)S(1)} %get-tuple-element.120.refs_1_, bf16[160,256]{1,0:T(8,128)(2,1)S(1)} %collective-permute-done.27.refs_2_, bf16[160,256]{1,0:T(8,128)(2,1)S(1)} %collective-permute-done.28.refs_3_, ...), custom_call_target="tpu_custom_call" | custom-call | flops 1 | bytes 1 | tf_op jit(solution)/shard_map/pallas_call | solution.py:42
  79.0 1.5 %collective-permute-done.31.refs_6_ = bf16[144,640]{1,0:T(8,128)(2,1)S(1)} collective-permute-done((bf16[144,640]{1,0:T(8,128)(2,1)S(1)}, bf16[144,640]{1,0:T(8,128)(2,1)S(1)}, u32[]{:S(2)}, u32[]{:S(2)}) %collective-permute-start.31) | collective-permute-done | bytes 184352 | tf_op jit(solution)/shard_map/ppermute | solution.py:494
  81.0 1.1 %collective-permute-start.36 = (bf16[2,640,128]{2,1,0:T(8,128)(2,1)S(1)}, bf16[2,640,128]{2,1,0:T(8,128)(2,1)S(1)}, u32[]{:S(2)}, u32[]{:S(2)}) collective-permute-start(bf16[2,640,128]{2,1,0:T(8,128)(2,1)S(1)} %collective-permute-done.17.refs_14_), channel_id=1, source_target_pairs={{0,1},{1,0},{2,3},{3,2},{4,5},{5,4},{6,7},{7,6},{8,9},{9,8},{10,11... | collective-permute-start | bytes 983048 | tf_op jit(solution)/shard_map/ppermute | solution.py:494
  82.1 3.3 %collective-permute-done.41 = f32[32,128]{1,0:T(8,128)S(1)} collective-permute-done((f32[32,128]{1,0:T(8,128)S(1)}, f32[32,128]{1,0:T(8,128)S(1)}, u32[]{:S(2)}, u32[]{:S(2)}) %collective-permute-start.41) | collective-permute-done | bytes 16416 | tf_op jit(solution)/shard_map/ppermute | solution.py:494
  86.1 1.4 %collective-permute-start.44 = (f32[32,128]{1,0:T(8,128)S(1)}, f32[32,128]{1,0:T(8,128)S(1)}, u32[]{:S(2)}, u32[]{:S(2)}) collective-permute-start(f32[32,128]{1,0:T(8,128)S(1)} %add.11.refs_1_), channel_id=1, source_target_pairs={{0,3},{1,2},{2,1},{3,0},{4,7},{5,6},{6,5},{7,4},{8,11},{9,10},{10,... | collective-permute-start | bytes 49160 | tf_op jit(solution)/shard_map/ppermute | solution.py:59
  88.2 1.6 %collective-permute-done.43.refs_3_ = f32[32,128]{1,0:T(8,128)S(1)} collective-permute-done((f32[32,128]{1,0:T(8,128)S(1)}, f32[32,128]{1,0:T(8,128)S(1)}, u32[]{:S(2)}, u32[]{:S(2)}) %collective-permute-start.43) | collective-permute-done | bytes 16416 | tf_op jit(solution)/shard_map/ppermute | solution.py:59
  90.4 0.7 reshape.49
  91.1 1.2 %shard_map.138 = (f32[18,512]{1,0:T(8,128)}, f32[1,512]{1,0:T(1,128)}, f32[1,512]{1,0:T(1,128)}) custom-call(s32[3]{0:T(128)S(1)} %pad_add_fusion.refs_0_, f32[32,128]{1,0:T(8,128)S(1)} %add.11.refs_1_, f32[32,128]{1,0:T(8,128)S(1)} %collective-permute-done.42.refs_2_, f32[32,128]{1,0:T(8,128)S(1)} %collective-permute-done.43.refs_3_, ...), custom_call_target="tpu_custom_call" | custom-call | flops 1 | bytes 1 | tf_op jit(solution)/shard_map/pallas_call | solution.py:42
  93.0 16.7 %shard_map.137 = f32[27,128,512]{2,1,0:T(8,128)} custom-call(s32[3]{0:T(128)} %copy-done.11, bf16[144,640]{1,0:T(8,128)(2,1)} %copy-done.9, bf16[2,144,640]{2,1,0:T(8,128)(2,1)} %copy-done.1, bf16[144,640]{1,0:T(8,128)(2,1)} %copy-done.22, bf16[144,640]{1,0:T(8,128)(2,1)} %copy-done.21, bf16[2,144,640]{2,1,0:T(8,128)(2,1)} %copy-done.15, ...), custom_call_target="tpu_custom_call" | custom-call | flops 1 | bytes 1 | tf_op jit(solution)/shard_map/pallas_call | solution.py:721
  (118 shorter events, 9.7 us)
Async XLA Ops:
  3.2 87.9 %copy-start.11 = (s32[3]{0:T(128)}, s32[3]{0:T(128)S(1)}, u32[]{:S(2)}) copy-start(s32[3]{0:T(128)S(1)} %pad_add_fusion.refs_0_) | copy-start | bytes 40
  5.8 7.0 %collective-permute-start = (bf16[192,256]{1,0:T(8,128)(2,1)S(1)}, bf16[192,256]{1,0:T(8,128)(2,1)S(1)}, u32[]{:S(2)}, u32[]{:S(2)}) collective-permute-start(bf16[192,256]{1,0:T(8,128)(2,1)S(1)} %get-tuple-element.77), channel_id=1, source_target_pairs={{0,1},{1,0},{2,3},{3,2},{4,5},{5,4},{6,7},{7,6},{8,9},{9,8},{10,11... | collective-permute-start | bytes 294920 | tf_op jit(solution)/shard_map/ppermute | solution.py:59
  6.3 6.5 %collective-permute-start.1 = (bf16[192,256]{1,0:T(8,128)(2,1)S(1)}, bf16[192,256]{1,0:T(8,128)(2,1)S(1)}, u32[]{:S(2)}, u32[]{:S(2)}) collective-permute-start(bf16[192,256]{1,0:T(8,128)(2,1)S(1)} %get-tuple-element.78), channel_id=1, source_target_pairs={{0,2},{1,3},{2,0},{3,1},{4,6},{5,7},{6,4},{7,5},{8,10},{9,11},{10,... | collective-permute-start | bytes 294920 | tf_op jit(solution)/shard_map/ppermute | solution.py:59
  8.9 5.2 %collective-permute-start.2 = (bf16[192,256]{1,0:T(8,128)(2,1)S(1)}, bf16[192,256]{1,0:T(8,128)(2,1)S(1)}, u32[]{:S(2)}, u32[]{:S(2)}) collective-permute-start(bf16[192,256]{1,0:T(8,128)(2,1)S(1)} %get-tuple-element.79), channel_id=1, source_target_pairs={{0,3},{1,2},{2,1},{3,0},{4,7},{5,6},{6,5},{7,4},{8,11},{9,10},{10,... | collective-permute-start | bytes 294920 | tf_op jit(solution)/shard_map/ppermute | solution.py:59
  15.1 9.3 %collective-permute-start.3 = (bf16[144,640]{1,0:T(8,128)(2,1)S(1)}, bf16[144,640]{1,0:T(8,128)(2,1)S(1)}, u32[]{:S(2)}, u32[]{:S(2)}) collective-permute-start(bf16[144,640]{1,0:T(8,128)(2,1)S(1)} %get-tuple-element.114.refs_1_), channel_id=1, source_target_pairs={{0,8},{1,9},{2,10},{3,11},{4,12},{5,13},{6,14},{7,15},{8,16},{9,17... | collective-permute-start | bytes 552968 | tf_op jit(solution)/shard_map/ppermute | solution.py:494
  16.7 10.5 %collective-permute-start.4 = (bf16[144,640]{1,0:T(8,128)(2,1)S(1)}, bf16[144,640]{1,0:T(8,128)(2,1)S(1)}, u32[]{:S(2)}, u32[]{:S(2)}) collective-permute-start(bf16[144,640]{1,0:T(8,128)(2,1)S(1)} %get-tuple-element.114.refs_1_), channel_id=1, source_target_pairs={{0,24},{1,25},{2,26},{3,27},{4,28},{5,29},{6,30},{7,31},{8,0},{9,1... | collective-permute-start | bytes 552968 | tf_op jit(solution)/shard_map/ppermute | solution.py:494
  18.9 8.3 %collective-permute-start.5 = (bf16[144,640]{1,0:T(8,128)(2,1)S(1)}, bf16[144,640]{1,0:T(8,128)(2,1)S(1)}, u32[]{:S(2)}, u32[]{:S(2)}) collective-permute-start(bf16[144,640]{1,0:T(8,128)(2,1)S(1)} %get-tuple-element.114.refs_1_), channel_id=1, source_target_pairs={{0,4},{1,5},{2,6},{3,7},{4,0},{5,1},{6,2},{7,3},{8,12},{9,13},{10,... | collective-permute-start | bytes 552968 | tf_op jit(solution)/shard_map/ppermute | solution.py:494
  22.8 8.4 %collective-permute-start.7 = (bf16[640,128]{1,0:T(8,128)(2,1)S(1)}, bf16[640,128]{1,0:T(8,128)(2,1)S(1)}, u32[]{:S(2)}, u32[]{:S(2)}) collective-permute-start(bf16[640,128]{1,0:T(8,128)(2,1)S(1)} %get-tuple-element.87), channel_id=1, source_target_pairs={{0,2},{1,3},{2,0},{3,1},{4,6},{5,7},{6,4},{7,5},{8,10},{9,11},{10,... | collective-permute-start | bytes 491528 | tf_op jit(solution)/shard_map/ppermute | solution.py:59
  24.3 6.9 %collective-permute-start.8 = (bf16[640,128]{1,0:T(8,128)(2,1)S(1)}, bf16[640,128]{1,0:T(8,128)(2,1)S(1)}, u32[]{:S(2)}, u32[]{:S(2)}) collective-permute-start(bf16[640,128]{1,0:T(8,128)(2,1)S(1)} %get-tuple-element.91), channel_id=1, source_target_pairs={{0,3},{1,2},{2,1},{3,0},{4,7},{5,6},{6,5},{7,4},{8,11},{9,10},{10,... | collective-permute-start | bytes 491528 | tf_op jit(solution)/shard_map/ppermute | solution.py:59
  29.4 1.7 %collective-permute-start.6 = (bf16[640,128]{1,0:T(8,128)(2,1)S(1)}, bf16[640,128]{1,0:T(8,128)(2,1)S(1)}, u32[]{:S(2)}, u32[]{:S(2)}) collective-permute-start(bf16[640,128]{1,0:T(8,128)(2,1)S(1)} %get-tuple-element.90), channel_id=1, source_target_pairs={{0,1},{1,0},{2,3},{3,2},{4,5},{5,4},{6,7},{7,6},{8,9},{9,8},{10,11... | collective-permute-start | bytes 491528 | tf_op jit(solution)/shard_map/ppermute | solution.py:59
  29.6 14.6 %collective-permute-start.14 = (bf16[2,144,640]{2,1,0:T(8,128)(2,1)S(1)}, bf16[2,144,640]{2,1,0:T(8,128)(2,1)S(1)}, u32[]{:S(2)}, u32[]{:S(2)}) collective-permute-start(bf16[2,144,640]{2,1,0:T(8,128)(2,1)S(1)} %shard_map.133.refs_2_), channel_id=1, source_target_pairs={{0,4},{1,5},{2,6},{3,7},{4,0},{5,1},{6,2},{7,3},{8,12},{9,13},{10,... | collective-permute-start | bytes 1105928 | tf_op jit(solution)/shard_map/ppermute | solution.py:494
  32.7 59.7 %copy-start.3 = (bf16[640,128]{1,0:T(8,128)(2,1)}, bf16[640,128]{1,0:T(8,128)(2,1)S(1)}, u32[]{:S(2)}) copy-start(bf16[640,128]{1,0:T(8,128)(2,1)S(1)} %get-tuple-element.98.refs_1_.refs_7_) | copy-start | bytes 491524
  32.7 9.0 %collective-permute-start.9 = (bf16[640,128]{1,0:T(8,128)(2,1)S(1)}, bf16[640,128]{1,0:T(8,128)(2,1)S(1)}, u32[]{:S(2)}, u32[]{:S(2)}) collective-permute-start(bf16[640,128]{1,0:T(8,128)(2,1)S(1)} %get-tuple-element.98.refs_1_.refs_7_), channel_id=1, source_target_pairs={{0,8},{1,9},{2,10},{3,11},{4,12},{5,13},{6,14},{7,15},{8,16},{9,17... | collective-permute-start | bytes 491528 | tf_op jit(solution)/shard_map/ppermute | solution.py:494
  33.9 9.5 %collective-permute-start.10 = (bf16[640,128]{1,0:T(8,128)(2,1)S(1)}, bf16[640,128]{1,0:T(8,128)(2,1)S(1)}, u32[]{:S(2)}, u32[]{:S(2)}) collective-permute-start(bf16[640,128]{1,0:T(8,128)(2,1)S(1)} %get-tuple-element.98.refs_1_.refs_7_), channel_id=1, source_target_pairs={{0,24},{1,25},{2,26},{3,27},{4,28},{5,29},{6,30},{7,31},{8,0},{9,1... | collective-permute-start | bytes 491528 | tf_op jit(solution)/shard_map/ppermute | solution.py:494
  36.6 7.6 %collective-permute-start.11 = (bf16[640,128]{1,0:T(8,128)(2,1)S(1)}, bf16[640,128]{1,0:T(8,128)(2,1)S(1)}, u32[]{:S(2)}, u32[]{:S(2)}) collective-permute-start(bf16[640,128]{1,0:T(8,128)(2,1)S(1)} %get-tuple-element.98.refs_1_.refs_7_), channel_id=1, source_target_pairs={{0,4},{1,3},{2,6},{3,1},{4,0},{5,7},{6,2},{7,5},{8,12},{9,11},{10,... | collective-permute-start | bytes 491528 | tf_op jit(solution)/shard_map/ppermute | solution.py:494
  37.8 6.3 %collective-permute-start.12 = (bf16[640,128]{1,0:T(8,128)(2,1)S(1)}, bf16[640,128]{1,0:T(8,128)(2,1)S(1)}, u32[]{:S(2)}, u32[]{:S(2)}) collective-permute-start(bf16[640,128]{1,0:T(8,128)(2,1)S(1)} %get-tuple-element.98.refs_1_.refs_7_), channel_id=1, source_target_pairs={{0,2},{1,5},{2,0},{3,7},{4,6},{5,1},{6,4},{7,3},{8,10},{9,13},{10,... | collective-permute-start | bytes 491528 | tf_op jit(solution)/shard_map/ppermute | solution.py:494
  41.7 2.5 %collective-permute-start.13 = (bf16[640,128]{1,0:T(8,128)(2,1)S(1)}, bf16[640,128]{1,0:T(8,128)(2,1)S(1)}, u32[]{:S(2)}, u32[]{:S(2)}) collective-permute-start(bf16[640,128]{1,0:T(8,128)(2,1)S(1)} %get-tuple-element.98.refs_1_.refs_7_), channel_id=1, source_target_pairs={{0,1},{1,0},{2,3},{3,2},{4,5},{5,4},{6,7},{7,6},{8,9},{9,8},{10,11... | collective-permute-start | bytes 491528 | tf_op jit(solution)/shard_map/ppermute | solution.py:494
  44.1 48.2 %copy-start.6 = (bf16[640,128]{1,0:T(8,128)(2,1)}, bf16[640,128]{1,0:T(8,128)(2,1)S(1)}, u32[]{:S(2)}) copy-start(bf16[640,128]{1,0:T(8,128)(2,1)S(1)} %collective-permute-done.13.refs_2_.refs_19_) | copy-start | bytes 491524
  44.2 3.7 %collective-permute-start.20 = (bf16[640,128]{1,0:T(8,128)(2,1)S(1)}, bf16[640,128]{1,0:T(8,128)(2,1)S(1)}, u32[]{:S(2)}, u32[]{:S(2)}) collective-permute-start(bf16[640,128]{1,0:T(8,128)(2,1)S(1)} %collective-permute-done.11.refs_3_.refs_10_), channel_id=1, source_target_pairs={{0,1},{1,0},{2,3},{3,2},{4,5},{5,4},{6,7},{7,6},{8,9},{9,8},{10,11... | collective-permute-start | bytes 491528 | tf_op jit(solution)/shard_map/ppermute | solution.py:494
  44.3 5.0 %collective-permute-start.21 = (bf16[640,128]{1,0:T(8,128)(2,1)S(1)}, bf16[640,128]{1,0:T(8,128)(2,1)S(1)}, u32[]{:S(2)}, u32[]{:S(2)}) collective-permute-start(bf16[640,128]{1,0:T(8,128)(2,1)S(1)} %collective-permute-done.12.refs_4_.refs_13_), channel_id=1, source_target_pairs={{0,1},{1,0},{2,3},{3,2},{4,5},{5,4},{6,7},{7,6},{8,9},{9,8},{10,11... | collective-permute-start | bytes 491528 | tf_op jit(solution)/shard_map/ppermute | solution.py:494
  44.8 14.2 %collective-permute-start.16 = (bf16[2,640,128]{2,1,0:T(8,128)(2,1)S(1)}, bf16[2,640,128]{2,1,0:T(8,128)(2,1)S(1)}, u32[]{:S(2)}, u32[]{:S(2)}) collective-permute-start(bf16[2,640,128]{2,1,0:T(8,128)(2,1)S(1)} %shard_map.134.refs_8_), channel_id=1, source_target_pairs={{0,4},{1,3},{2,6},{3,1},{4,0},{5,7},{6,2},{7,5},{8,12},{9,11},{10,... | collective-permute-start | bytes 983048 | tf_op jit(solution)/shard_map/ppermute | solution.py:494
  46.3 12.6 %collective-permute-start.17 = (bf16[2,640,128]{2,1,0:T(8,128)(2,1)S(1)}, bf16[2,640,128]{2,1,0:T(8,128)(2,1)S(1)}, u32[]{:S(2)}, u32[]{:S(2)}) collective-permute-start(bf16[2,640,128]{2,1,0:T(8,128)(2,1)S(1)} %shard_map.134.refs_8_), channel_id=1, source_target_pairs={{0,2},{1,5},{2,0},{3,7},{4,6},{5,1},{6,4},{7,3},{8,10},{9,13},{10,... | collective-permute-start | bytes 983048 | tf_op jit(solution)/shard_map/ppermute | solution.py:494
  47.9 11.1 %collective-permute-start.19 = (bf16[2,640,128]{2,1,0:T(8,128)(2,1)S(1)}, bf16[2,640,128]{2,1,0:T(8,128)(2,1)S(1)}, u32[]{:S(2)}, u32[]{:S(2)}) collective-permute-start(bf16[2,640,128]{2,1,0:T(8,128)(2,1)S(1)} %shard_map.134.refs_8_), channel_id=1, source_target_pairs={{0,1},{1,0},{2,3},{3,2},{4,5},{5,4},{6,7},{7,6},{8,9},{9,8},{10,11... | collective-permute-start | bytes 983048 | tf_op jit(solution)/shard_map/ppermute | solution.py:494
  47.9 11.0 %collective-permute-start.15 = (bf16[640,128]{1,0:T(8,128)(2,1)S(1)}, bf16[640,128]{1,0:T(8,128)(2,1)S(1)}, u32[]{:S(2)}, u32[]{:S(2)}) collective-permute-start(bf16[640,128]{1,0:T(8,128)(2,1)S(1)} %get-tuple-element.98.refs_1_.refs_7_), channel_id=1, source_target_pairs={{0,16},{1,17},{2,18},{3,19},{4,20},{5,21},{6,22},{7,23},{8,24},{9,... | collective-permute-start | bytes 491528 | tf_op jit(solution)/shard_map/ppermute | solution.py:494
  49.3 9.7 %collective-permute-start.18 = (bf16[640,128]{1,0:T(8,128)(2,1)S(1)}, bf16[640,128]{1,0:T(8,128)(2,1)S(1)}, u32[]{:S(2)}, u32[]{:S(2)}) collective-permute-start(bf16[640,128]{1,0:T(8,128)(2,1)S(1)} %collective-permute-done.11.refs_3_.refs_10_), channel_id=1, source_target_pairs={{0,2},{1,5},{2,0},{3,7},{4,6},{5,1},{6,4},{7,3},{8,10},{9,13},{10,... | collective-permute-start | bytes 491528 | tf_op jit(solution)/shard_map/ppermute | solution.py:494
  59.0 13.9 %collective-permute-start.24 = (bf16[2,640,128]{2,1,0:T(8,128)(2,1)S(1)}, bf16[2,640,128]{2,1,0:T(8,128)(2,1)}, u32[]{:S(2)}, u32[]{:S(2)}) collective-permute-start(bf16[2,640,128]{2,1,0:T(8,128)(2,1)S(1)} %collective-permute-done.16.refs_11_), channel_id=1, source_target_pairs={{0,2},{1,5},{2,0},{3,7},{4,6},{5,1},{6,4},{7,3},{8,10},{9,13},{10,... | collective-permute-start | bytes 983048 | tf_op jit(solution)/shard_map/ppermute | solution.py:494
  59.5 5.2 %collective-permute-start.27 = (bf16[160,256]{1,0:T(8,128)(2,1)S(1)}, bf16[160,256]{1,0:T(8,128)(2,1)S(1)}, u32[]{:S(2)}, u32[]{:S(2)}) collective-permute-start(bf16[160,256]{1,0:T(8,128)(2,1)S(1)} %get-tuple-element.117), channel_id=1, source_target_pairs={{0,1},{1,0},{2,3},{3,2},{4,5},{5,4},{6,7},{7,6},{8,9},{9,8},{10,11... | collective-permute-start | bytes 245768 | tf_op jit(solution)/shard_map/ppermute | solution.py:59
  59.5 13.4 %collective-permute-start.25 = (bf16[144,640]{1,0:T(8,128)(2,1)S(1)}, bf16[144,640]{1,0:T(8,128)(2,1)S(1)}, u32[]{:S(2)}, u32[]{:S(2)}) collective-permute-start(bf16[144,640]{1,0:T(8,128)(2,1)S(1)} %get-tuple-element.114.refs_1_), channel_id=1, source_target_pairs={{0,16},{1,17},{2,18},{3,19},{4,20},{5,21},{6,22},{7,23},{8,24},{9,... | collective-permute-start | bytes 552968 | tf_op jit(solution)/shard_map/ppermute | solution.py:494
  59.6 4.0 %collective-permute-start.26 = (f32[32,128]{1,0:T(8,128)S(1)}, f32[32,128]{1,0:T(8,128)S(1)}, u32[]{:S(2)}, u32[]{:S(2)}) collective-permute-start(f32[32,128]{1,0:T(8,128)S(1)} %get-tuple-element.115), channel_id=1, source_target_pairs={{0,4},{1,5},{2,6},{3,7},{4,0},{5,1},{6,2},{7,3},{8,12},{9,13},{10,... | collective-permute-start | bytes 49160 | tf_op jit(solution)/shard_map/ppermute | solution.py:494
  60.8 7.1 %collective-permute-start.28 = (bf16[160,256]{1,0:T(8,128)(2,1)S(1)}, bf16[160,256]{1,0:T(8,128)(2,1)S(1)}, u32[]{:S(2)}, u32[]{:S(2)}) collective-permute-start(bf16[160,256]{1,0:T(8,128)(2,1)S(1)} %get-tuple-element.118), channel_id=1, source_target_pairs={{0,2},{1,3},{2,0},{3,1},{4,6},{5,7},{6,4},{7,5},{8,10},{9,11},{10,... | collective-permute-start | bytes 245768 | tf_op jit(solution)/shard_map/ppermute | solution.py:59
  63.6 9.3 %collective-permute-start.22 = (bf16[640,128]{1,0:T(8,128)(2,1)S(1)}, bf16[640,128]{1,0:T(8,128)(2,1)}, u32[]{:S(2)}, u32[]{:S(2)}) collective-permute-start(bf16[640,128]{1,0:T(8,128)(2,1)S(1)} %collective-permute-done.15.refs_9_), channel_id=1, source_target_pairs={{0,4},{1,3},{2,6},{3,1},{4,0},{5,7},{6,2},{7,5},{8,12},{9,11},{10,... | collective-permute-start | bytes 491528 | tf_op jit(solution)/shard_map/ppermute | solution.py:494
  64.8 8.2 %collective-permute-start.23 = (bf16[640,128]{1,0:T(8,128)(2,1)S(1)}, bf16[640,128]{1,0:T(8,128)(2,1)}, u32[]{:S(2)}, u32[]{:S(2)}) collective-permute-start(bf16[640,128]{1,0:T(8,128)(2,1)S(1)} %collective-permute-done.15.refs_9_), channel_id=1, source_target_pairs={{0,2},{1,5},{2,0},{3,7},{4,6},{5,1},{6,4},{7,3},{8,10},{9,13},{10,... | collective-permute-start | bytes 491528 | tf_op jit(solution)/shard_map/ppermute | solution.py:494
  67.9 5.0 %collective-permute-start.29 = (bf16[160,256]{1,0:T(8,128)(2,1)S(1)}, bf16[160,256]{1,0:T(8,128)(2,1)S(1)}, u32[]{:S(2)}, u32[]{:S(2)}) collective-permute-start(bf16[160,256]{1,0:T(8,128)(2,1)S(1)} %get-tuple-element.119), channel_id=1, source_target_pairs={{0,3},{1,2},{2,1},{3,0},{4,7},{5,6},{6,5},{7,4},{8,11},{9,10},{10,... | collective-permute-start | bytes 245768 | tf_op jit(solution)/shard_map/ppermute | solution.py:59
  73.0 7.5 %collective-permute-start.31 = (bf16[144,640]{1,0:T(8,128)(2,1)S(1)}, bf16[144,640]{1,0:T(8,128)(2,1)S(1)}, u32[]{:S(2)}, u32[]{:S(2)}) collective-permute-start(bf16[144,640]{1,0:T(8,128)(2,1)S(1)} %collective-permute-done.25.refs_3_), channel_id=1, source_target_pairs={{0,4},{1,5},{2,6},{3,7},{4,0},{5,1},{6,2},{7,3},{8,12},{9,13},{10,... | collective-permute-start | bytes 552968 | tf_op jit(solution)/shard_map/ppermute | solution.py:494
  73.4 5.6 %collective-permute-start.30 = (bf16[640,128]{1,0:T(8,128)(2,1)}, bf16[640,128]{1,0:T(8,128)(2,1)}, u32[]{:S(2)}, u32[]{:S(2)}) collective-permute-start(bf16[640,128]{1,0:T(8,128)(2,1)} %collective-permute-done.22.refs_12_), channel_id=1, source_target_pairs={{0,2},{1,5},{2,0},{3,7},{4,6},{5,1},{6,4},{7,3},{8,10},{9,13},{10,... | collective-permute-start | bytes 491528 | tf_op jit(solution)/shard_map/ppermute | solution.py:494
  73.8 12.3 %collective-permute-start.34 = (bf16[2,640,128]{2,1,0:T(8,128)(2,1)S(1)}, bf16[2,640,128]{2,1,0:T(8,128)(2,1)S(1)}, u32[]{:S(2)}, u32[]{:S(2)}) collective-permute-start(bf16[2,640,128]{2,1,0:T(8,128)(2,1)S(1)} %collective-permute-done.16.refs_11_), channel_id=1, source_target_pairs={{0,1},{1,0},{2,3},{3,2},{4,5},{5,4},{6,7},{7,6},{8,9},{9,8},{10,11... | collective-permute-start | bytes 983048 | tf_op jit(solution)/shard_map/ppermute | solution.py:494
  74.7 3.7 %collective-permute-start.32 = (f32[32,128]{1,0:T(8,128)S(1)}, f32[32,128]{1,0:T(8,128)S(1)}, u32[]{:S(2)}, u32[]{:S(2)}) collective-permute-start(f32[32,128]{1,0:T(8,128)S(1)} %add.9), channel_id=1, source_target_pairs={{0,8},{1,9},{2,10},{3,11},{4,12},{5,13},{6,14},{7,15},{8,0},{9,1},... | collective-permute-start | bytes 49160 | tf_op jit(solution)/shard_map/ppermute | solution.py:494
  76.0 9.4 %collective-permute-start.33 = (bf16[640,128]{1,0:T(8,128)(2,1)S(1)}, bf16[640,128]{1,0:T(8,128)(2,1)S(1)}, u32[]{:S(2)}, u32[]{:S(2)}) collective-permute-start(bf16[640,128]{1,0:T(8,128)(2,1)S(1)} %collective-permute-done.15.refs_9_), channel_id=1, source_target_pairs={{0,1},{1,0},{2,3},{3,2},{4,5},{5,4},{6,7},{7,6},{8,9},{9,8},{10,11... | collective-permute-start | bytes 491528 | tf_op jit(solution)/shard_map/ppermute | solution.py:494
  78.4 7.6 %collective-permute-start.38 = (bf16[640,128]{1,0:T(8,128)(2,1)S(1)}, bf16[640,128]{1,0:T(8,128)(2,1)S(1)}, u32[]{:S(2)}, u32[]{:S(2)}) collective-permute-start(bf16[640,128]{1,0:T(8,128)(2,1)S(1)} %collective-permute-done.18.refs_16_), channel_id=1, source_target_pairs={{0,1},{1,0},{2,3},{3,2},{4,5},{5,4},{6,7},{7,6},{8,9},{9,8},{10,11... | collective-permute-start | bytes 491528 | tf_op jit(solution)/shard_map/ppermute | solution.py:494
  80.5 4.9 %collective-permute-start.41 = (f32[32,128]{1,0:T(8,128)S(1)}, f32[32,128]{1,0:T(8,128)S(1)}, u32[]{:S(2)}, u32[]{:S(2)}) collective-permute-start(f32[32,128]{1,0:T(8,128)S(1)} %add.10), channel_id=1, source_target_pairs={{0,16},{1,17},{2,18},{3,19},{4,20},{5,21},{6,22},{7,23},{8,24},{9,... | collective-permute-start | bytes 49160 | tf_op jit(solution)/shard_map/ppermute | solution.py:494
  81.0 11.3 %collective-permute-start.36 = (bf16[2,640,128]{2,1,0:T(8,128)(2,1)S(1)}, bf16[2,640,128]{2,1,0:T(8,128)(2,1)S(1)}, u32[]{:S(2)}, u32[]{:S(2)}) collective-permute-start(bf16[2,640,128]{2,1,0:T(8,128)(2,1)S(1)} %collective-permute-done.17.refs_14_), channel_id=1, source_target_pairs={{0,1},{1,0},{2,3},{3,2},{4,5},{5,4},{6,7},{7,6},{8,9},{9,8},{10,11... | collective-permute-start | bytes 983048 | tf_op jit(solution)/shard_map/ppermute | solution.py:494
  85.4 6.9 %collective-permute-start.39 = (bf16[2,640,128]{2,1,0:T(8,128)(2,1)}, bf16[2,640,128]{2,1,0:T(8,128)(2,1)}, u32[]{:S(2)}, u32[]{:S(2)}) collective-permute-start(bf16[2,640,128]{2,1,0:T(8,128)(2,1)} %collective-permute-done.24.refs_17_), channel_id=1, source_target_pairs={{0,1},{1,0},{2,3},{3,2},{4,5},{5,4},{6,7},{7,6},{8,9},{9,8},{10,11... | collective-permute-start | bytes 983048 | tf_op jit(solution)/shard_map/ppermute | solution.py:494
  85.5 2.0 %collective-permute-start.42 = (f32[32,128]{1,0:T(8,128)S(1)}, f32[32,128]{1,0:T(8,128)S(1)}, u32[]{:S(2)}, u32[]{:S(2)}) collective-permute-start(f32[32,128]{1,0:T(8,128)S(1)} %add.11.refs_1_), channel_id=1, source_target_pairs={{0,1},{1,0},{2,3},{3,2},{4,5},{5,4},{6,7},{7,6},{8,9},{9,8},{10,11... | collective-permute-start | bytes 49160 | tf_op jit(solution)/shard_map/ppermute | solution.py:59
  86.0 3.7 %collective-permute-start.43 = (f32[32,128]{1,0:T(8,128)S(1)}, f32[32,128]{1,0:T(8,128)S(1)}, u32[]{:S(2)}, u32[]{:S(2)}) collective-permute-start(f32[32,128]{1,0:T(8,128)S(1)} %add.11.refs_1_), channel_id=1, source_target_pairs={{0,2},{1,3},{2,0},{3,1},{4,6},{5,7},{6,4},{7,5},{8,10},{9,11},{10,... | collective-permute-start | bytes 49160 | tf_op jit(solution)/shard_map/ppermute | solution.py:59
  86.1 3.7 %collective-permute-start.44 = (f32[32,128]{1,0:T(8,128)S(1)}, f32[32,128]{1,0:T(8,128)S(1)}, u32[]{:S(2)}, u32[]{:S(2)}) collective-permute-start(f32[32,128]{1,0:T(8,128)S(1)} %add.11.refs_1_), channel_id=1, source_target_pairs={{0,3},{1,2},{2,1},{3,0},{4,7},{5,6},{6,5},{7,4},{8,11},{9,10},{10,... | collective-permute-start | bytes 49160 | tf_op jit(solution)/shard_map/ppermute | solution.py:59
  87.5 4.8 %collective-permute-start.35 = (bf16[640,128]{1,0:T(8,128)(2,1)}, bf16[640,128]{1,0:T(8,128)(2,1)}, u32[]{:S(2)}, u32[]{:S(2)}) collective-permute-start(bf16[640,128]{1,0:T(8,128)(2,1)} %collective-permute-done.22.refs_12_), channel_id=1, source_target_pairs={{0,1},{1,0},{2,3},{3,2},{4,5},{5,4},{6,7},{7,6},{8,9},{9,8},{10,11... | collective-permute-start | bytes 491528 | tf_op jit(solution)/shard_map/ppermute | solution.py:494
  89.8 2.5 %collective-permute-start.37 = (bf16[640,128]{1,0:T(8,128)(2,1)}, bf16[640,128]{1,0:T(8,128)(2,1)}, u32[]{:S(2)}, u32[]{:S(2)}) collective-permute-start(bf16[640,128]{1,0:T(8,128)(2,1)} %collective-permute-done.23.refs_15_), channel_id=1, source_target_pairs={{0,1},{1,0},{2,3},{3,2},{4,5},{5,4},{6,7},{7,6},{8,9},{9,8},{10,11... | collective-permute-start | bytes 491528 | tf_op jit(solution)/shard_map/ppermute | solution.py:494
  89.8 2.5 %collective-permute-start.40 = (bf16[640,128]{1,0:T(8,128)(2,1)}, bf16[640,128]{1,0:T(8,128)(2,1)}, u32[]{:S(2)}, u32[]{:S(2)}) collective-permute-start(bf16[640,128]{1,0:T(8,128)(2,1)} %collective-permute-done.30.refs_18_), channel_id=1, source_target_pairs={{0,1},{1,0},{2,3},{3,2},{4,5},{5,4},{6,7},{7,6},{8,9},{9,8},{10,11... | collective-permute-start | bytes 491528 | tf_op jit(solution)/shard_map/ppermute | solution.py:494
  (25 other events, 602.5 us)

commit v5 on v4

--- a/solution.py
+++ b/solution.py
@@ -383,7 +383,7 @@
                 there = pl.ds(pl.multiple_of(at * LANES, LANES), LANES)
                 images[there, :] = turned[slot][:LANES, t * block : (t + 1) * block]
 
-    step = 4
+    step = 8
     for n in range(0, 3 * clips, step):
         moved = jnp.dot(
             images[n * LANES : (n + step) * LANES, :], shifts[...], preferred_element_type=f32
@@ -442,7 +442,8 @@
         @pl.when(core == mine)
         def _(mine=mine):
             for slot in range(clips):
-                for t in range(frames):
+                place(slot, 0, mine)
+                for t in range(1, frames):
 
                     @pl.when(t < table[slot_clip(info, slot, clips)])
                     def _(slot=slot, t=t):

time: 110 us -> 110 us (level)
  no operation moved by 1% of the time
where the time goes in v5:
time: 110 us
  starting transfers between devices  36.9 us (34%)
  waiting for transfers between devices  31.5 us (29%)
  Pallas kernels  30.8 us (28%)
  local copies, waits for them, and re-layouts  8.22 us (7%)
  between operations  2.01 us (2%)
    ppermute x33, starting transfers between devices, send(): return lax.ppermute(block, ('dp', 'shard'), pairs)  29.2 us
    ppermute x33, waiting for transfers between devices, send(): return lax.ppermute(block, ('dp', 'shard'), pairs)  21.3 us
    pallas_call x1, Pallas kernels, weight_grad(): pl.pallas_call(lambda *refs: weight_grad_body(frames, height, LANES // he...  16.3 us
    pallas_call x8, Pallas kernels, kernel_call(): pl.pallas_call(body, out_shape=outs, in_specs=specs, out_specs=[vmem] * l...  14 us
    ppermute x12, waiting for transfers between devices, swap(): return lax.ppermute(block, 'shard', pairs)  10.2 us
    ppermute x12, starting transfers between devices, swap(): return lax.ppermute(block, 'shard', pairs)  7.7 us
    unnamed x57, local copies, waits for them, and re-layouts  6.47 us
  transfers between devices with their start and end apart: 45, of which 15 were waited for; matrix products, arithmetic and copies ran while one was open for 1% of the time, Pallas kernels for 12%

profile of v5, /device:TPU:0, one launch (start us, length us, event | category | flops | bytes accessed | tf_op | source)
XLA Modules:
  0.0 109.5 jit_solution(3926113123248495304)
XLA Ops:
  1.3 0.8 copy.15
  2.2 1.0 reshape.46.refs_2_
  3.2 0.9 copy-done.10
  4.1 0.7 copy-done.12
  4.9 0.9 shard_map.128
  6.3 2.6 %collective-permute-start.1 = (bf16[192,256]{1,0:T(8,128)(2,1)S(1)}, bf16[192,256]{1,0:T(8,128)(2,1)S(1)}, u32[]{:S(2)}, u32[]{:S(2)}) collective-permute-start(bf16[192,256]{1,0:T(8,128)(2,1)S(1)} %get-tuple-element.78), channel_id=1, source_target_pairs={{0,2},{1,3},{2,0},{3,1},{4,6},{5,7},{6,4},{7,5},{8,10},{9,11},{10,... | collective-permute-start | bytes 294920 | tf_op jit(solution)/shard_map/ppermute | solution.py:59
  9.0 2.0 %copy-done = bf16[128,27,512]{2,0,1:T(8,128)(2,1)S(1)} copy-done((bf16[128,27,512]{2,0,1:T(8,128)(2,1)S(1)}, bf16[128,27,512]{2,0,1:T(8,128)(2,1)}, u32[]{:S(2)}) %copy-start) | copy-done | bytes 3538968
  12.8 1.4 %collective-permute-done.2.refs_4_.refs_13_ = bf16[192,256]{1,0:T(8,128)(2,1)S(1)} collective-permute-done((bf16[192,256]{1,0:T(8,128)(2,1)S(1)}, bf16[192,256]{1,0:T(8,128)(2,1)S(1)}, u32[]{:S(2)}, u32[]{:S(2)}) %collective-permute-start.2) | collective-permute-done | bytes 98336 | tf_op jit(solution)/shard_map/ppermute | solution.py:59
  14.1 0.9 shard_map.129
  15.1 1.7 %collective-permute-start.3 = (bf16[144,640]{1,0:T(8,128)(2,1)S(1)}, bf16[144,640]{1,0:T(8,128)(2,1)S(1)}, u32[]{:S(2)}, u32[]{:S(2)}) collective-permute-start(bf16[144,640]{1,0:T(8,128)(2,1)S(1)} %get-tuple-element.114.refs_1_), channel_id=1, source_target_pairs={{0,8},{1,9},{2,10},{3,11},{4,12},{5,13},{6,14},{7,15},{8,16},{9,17... | collective-permute-start | bytes 552968 | tf_op jit(solution)/shard_map/ppermute | solution.py:495
  16.7 2.2 %collective-permute-start.4 = (bf16[144,640]{1,0:T(8,128)(2,1)S(1)}, bf16[144,640]{1,0:T(8,128)(2,1)S(1)}, u32[]{:S(2)}, u32[]{:S(2)}) collective-permute-start(bf16[144,640]{1,0:T(8,128)(2,1)S(1)} %get-tuple-element.114.refs_1_), channel_id=1, source_target_pairs={{0,24},{1,25},{2,26},{3,27},{4,28},{5,29},{6,30},{7,31},{8,0},{9,1... | collective-permute-start | bytes 552968 | tf_op jit(solution)/shard_map/ppermute | solution.py:495
  18.9 1.5 %collective-permute-start.5 = (bf16[144,640]{1,0:T(8,128)(2,1)S(1)}, bf16[144,640]{1,0:T(8,128)(2,1)S(1)}, u32[]{:S(2)}, u32[]{:S(2)}) collective-permute-start(bf16[144,640]{1,0:T(8,128)(2,1)S(1)} %get-tuple-element.114.refs_1_), channel_id=1, source_target_pairs={{0,4},{1,5},{2,6},{3,7},{4,0},{5,1},{6,2},{7,3},{8,12},{9,13},{10,... | collective-permute-start | bytes 552968 | tf_op jit(solution)/shard_map/ppermute | solution.py:495
  20.5 2.3 %shard_map.130 = (bf16[640,128]{1,0:T(8,128)(2,1)S(1)}, bf16[640,128]{1,0:T(8,128)(2,1)S(1)}) custom-call(s32[3]{0:T(128)S(1)} %pad_add_fusion.refs_0_, bf16[640,128]{1,0:T(8,128)(2,1)S(1)} %get-tuple-element.88.refs_1_, bf16[3456,512]{1,0:T(8,128)(2,1)S(1)} %get-tuple-element.86.refs_2_.refs_7_), custom_call_target="tpu_custom_call" | custom-call | flops 1 | bytes 1 | tf_op jit(solution)/shard_map/pallas_call | solution.py:42
  22.8 1.5 %collective-permute-start.7 = (bf16[640,128]{1,0:T(8,128)(2,1)S(1)}, bf16[640,128]{1,0:T(8,128)(2,1)S(1)}, u32[]{:S(2)}, u32[]{:S(2)}) collective-permute-start(bf16[640,128]{1,0:T(8,128)(2,1)S(1)} %get-tuple-element.87), channel_id=1, source_target_pairs={{0,2},{1,3},{2,0},{3,1},{4,6},{5,7},{6,4},{7,5},{8,10},{9,11},{10,... | collective-permute-start | bytes 491528 | tf_op jit(solution)/shard_map/ppermute | solution.py:59
  24.4 2.8 %collective-permute-done.4.refs_1_ = bf16[144,640]{1,0:T(8,128)(2,1)S(1)} collective-permute-done((bf16[144,640]{1,0:T(8,128)(2,1)S(1)}, bf16[144,640]{1,0:T(8,128)(2,1)S(1)}, u32[]{:S(2)}, u32[]{:S(2)}) %collective-permute-start.4) | collective-permute-done | bytes 184352 | tf_op jit(solution)/shard_map/ppermute | solution.py:495
  27.2 2.2 %shard_map.131 = (f32[640,128]{1,0:T(8,128)S(1)}, bf16[640,128]{1,0:T(8,128)(2,1)S(1)}) custom-call(s32[3]{0:T(128)S(1)} %pad_add_fusion.refs_0_, bf16[640,128]{1,0:T(8,128)(2,1)S(1)} %get-tuple-element.88.refs_1_, bf16[3456,512]{1,0:T(8,128)(2,1)S(1)} %get-tuple-element.86.refs_2_.refs_7_), custom_call_target="tpu_custom_call" | custom-call | flops 1 | bytes 1 | tf_op jit(solution)/shard_map/pallas_call | solution.py:42
  29.6 1.6 %collective-permute-start.14 = (bf16[2,144,640]{2,1,0:T(8,128)(2,1)S(1)}, bf16[2,144,640]{2,1,0:T(8,128)(2,1)S(1)}, u32[]{:S(2)}, u32[]{:S(2)}) collective-permute-start(bf16[2,144,640]{2,1,0:T(8,128)(2,1)S(1)} %shard_map.133.refs_2_), channel_id=1, source_target_pairs={{0,4},{1,5},{2,6},{3,7},{4,0},{5,1},{6,2},{7,3},{8,12},{9,13},{10,... | collective-permute-start | bytes 1105928 | tf_op jit(solution)/shard_map/ppermute | solution.py:495
  31.1 1.5 %shard_map.132 = (bf16[640,128]{1,0:T(8,128)(2,1)S(1)}, f32[8,128]{1,0:T(8,128)S(1)}, bf16[640,128]{1,0:T(8,128)(2,1)S(1)}) custom-call(s32[3]{0:T(128)S(1)} %pad_add_fusion.refs_0_, f32[640,128]{1,0:T(8,128)S(1)} %get-tuple-element.89.refs_1_, bf16[640,128]{1,0:T(8,128)(2,1)S(1)} %collective-permute-done.6.refs_2_, ...), custom_call_target="tpu_custom_call" | custom-call | flops 1 | bytes 1 | tf_op jit(solution)/shard_map/pallas_call | solution.py:42
  32.7 1.2 %collective-permute-start.9 = (bf16[640,128]{1,0:T(8,128)(2,1)S(1)}, bf16[640,128]{1,0:T(8,128)(2,1)S(1)}, u32[]{:S(2)}, u32[]{:S(2)}) collective-permute-start(bf16[640,128]{1,0:T(8,128)(2,1)S(1)} %get-tuple-element.98.refs_1_.refs_7_), channel_id=1, source_target_pairs={{0,8},{1,9},{2,10},{3,11},{4,12},{5,13},{6,14},{7,15},{8,16},{9,17... | collective-permute-start | bytes 491528 | tf_op jit(solution)/shard_map/ppermute | solution.py:495
  33.9 2.7 %collective-permute-start.10 = (bf16[640,128]{1,0:T(8,128)(2,1)S(1)}, bf16[640,128]{1,0:T(8,128)(2,1)S(1)}, u32[]{:S(2)}, u32[]{:S(2)}) collective-permute-start(bf16[640,128]{1,0:T(8,128)(2,1)S(1)} %get-tuple-element.98.refs_1_.refs_7_), channel_id=1, source_target_pairs={{0,24},{1,25},{2,26},{3,27},{4,28},{5,29},{6,30},{7,31},{8,0},{9,1... | collective-permute-start | bytes 491528 | tf_op jit(solution)/shard_map/ppermute | solution.py:495
  36.6 1.3 %collective-permute-start.11 = (bf16[640,128]{1,0:T(8,128)(2,1)S(1)}, bf16[640,128]{1,0:T(8,128)(2,1)S(1)}, u32[]{:S(2)}, u32[]{:S(2)}) collective-permute-start(bf16[640,128]{1,0:T(8,128)(2,1)S(1)} %get-tuple-element.98.refs_1_.refs_7_), channel_id=1, source_target_pairs={{0,4},{1,3},{2,6},{3,1},{4,0},{5,7},{6,2},{7,5},{8,12},{9,11},{10,... | collective-permute-start | bytes 491528 | tf_op jit(solution)/shard_map/ppermute | solution.py:495
  37.8 1.6 %collective-permute-start.12 = (bf16[640,128]{1,0:T(8,128)(2,1)S(1)}, bf16[640,128]{1,0:T(8,128)(2,1)S(1)}, u32[]{:S(2)}, u32[]{:S(2)}) collective-permute-start(bf16[640,128]{1,0:T(8,128)(2,1)S(1)} %get-tuple-element.98.refs_1_.refs_7_), channel_id=1, source_target_pairs={{0,2},{1,5},{2,0},{3,7},{4,6},{5,1},{6,4},{7,3},{8,10},{9,13},{10,... | collective-permute-start | bytes 491528 | tf_op jit(solution)/shard_map/ppermute | solution.py:495
  39.4 2.3 %collective-permute-done.9.refs_0_ = bf16[640,128]{1,0:T(8,128)(2,1)S(1)} collective-permute-done((bf16[640,128]{1,0:T(8,128)(2,1)S(1)}, bf16[640,128]{1,0:T(8,128)(2,1)S(1)}, u32[]{:S(2)}, u32[]{:S(2)}) %collective-permute-start.9) | collective-permute-done | bytes 163872 | tf_op jit(solution)/shard_map/ppermute | solution.py:495
  41.7 1.8 %collective-permute-done.10.refs_1_ = bf16[640,128]{1,0:T(8,128)(2,1)S(1)} collective-permute-done((bf16[640,128]{1,0:T(8,128)(2,1)S(1)}, bf16[640,128]{1,0:T(8,128)(2,1)S(1)}, u32[]{:S(2)}, u32[]{:S(2)}) %collective-permute-start.10) | collective-permute-done | bytes 163872 | tf_op jit(solution)/shard_map/ppermute | solution.py:495
  43.4 0.7 collective-permute-done.11.refs_3_.refs_10_
  44.8 1.6 %collective-permute-start.16 = (bf16[2,640,128]{2,1,0:T(8,128)(2,1)S(1)}, bf16[2,640,128]{2,1,0:T(8,128)(2,1)S(1)}, u32[]{:S(2)}, u32[]{:S(2)}) collective-permute-start(bf16[2,640,128]{2,1,0:T(8,128)(2,1)S(1)} %shard_map.134.refs_8_), channel_id=1, source_target_pairs={{0,4},{1,3},{2,6},{3,1},{4,0},{5,7},{6,2},{7,5},{8,12},{9,11},{10,... | collective-permute-start | bytes 983048 | tf_op jit(solution)/shard_map/ppermute | solution.py:495
  46.3 1.6 %collective-permute-start.17 = (bf16[2,640,128]{2,1,0:T(8,128)(2,1)S(1)}, bf16[2,640,128]{2,1,0:T(8,128)(2,1)S(1)}, u32[]{:S(2)}, u32[]{:S(2)}) collective-permute-start(bf16[2,640,128]{2,1,0:T(8,128)(2,1)S(1)} %shard_map.134.refs_8_), channel_id=1, source_target_pairs={{0,2},{1,5},{2,0},{3,7},{4,6},{5,1},{6,4},{7,3},{8,10},{9,13},{10,... | collective-permute-start | bytes 983048 | tf_op jit(solution)/shard_map/ppermute | solution.py:495
  47.9 1.4 %collective-permute-start.15 = (bf16[640,128]{1,0:T(8,128)(2,1)S(1)}, bf16[640,128]{1,0:T(8,128)(2,1)S(1)}, u32[]{:S(2)}, u32[]{:S(2)}) collective-permute-start(bf16[640,128]{1,0:T(8,128)(2,1)S(1)} %get-tuple-element.98.refs_1_.refs_7_), channel_id=1, source_target_pairs={{0,16},{1,17},{2,18},{3,19},{4,20},{5,21},{6,22},{7,23},{8,24},{9,... | collective-permute-start | bytes 491528 | tf_op jit(solution)/shard_map/ppermute | solution.py:495
  49.8 3.6 %shard_map.135 = (f32[32,128]{1,0:T(8,128)S(1)}, bf16[160,256]{1,0:T(8,128)(2,1)S(1)}, bf16[160,256]{1,0:T(8,128)(2,1)S(1)}, bf16[160,256]{1,0:T(8,128)(2,1)S(1)}, bf16[160,256]{1,0:T(8,128)(2,1)S(1)}) custom-call(s32[3]{0:T(128)S(1)} %pad_add_fusion.refs_0_, bf16[640,128]{1,0:T(8,128)(2,1)S(1)} %get-tuple-element.98.refs_1_.refs_7_, ...), custom_call_target="tpu_custom_call" | custom-call | flops 1 | bytes 1 | tf_op jit(solution)/shard_map/pallas_call | solution.py:42
  53.4 5.6 %collective-permute-done.15.refs_9_ = bf16[640,128]{1,0:T(8,128)(2,1)S(1)} collective-permute-done((bf16[640,128]{1,0:T(8,128)(2,1)S(1)}, bf16[640,128]{1,0:T(8,128)(2,1)S(1)}, u32[]{:S(2)}, u32[]{:S(2)}) %collective-permute-start.15) | collective-permute-done | bytes 163872 | tf_op jit(solution)/shard_map/ppermute | solution.py:495
  59.6 1.1 %collective-permute-start.26 = (f32[32,128]{1,0:T(8,128)S(1)}, f32[32,128]{1,0:T(8,128)S(1)}, u32[]{:S(2)}, u32[]{:S(2)}) collective-permute-start(f32[32,128]{1,0:T(8,128)S(1)} %get-tuple-element.115), channel_id=1, source_target_pairs={{0,4},{1,5},{2,6},{3,7},{4,0},{5,1},{6,2},{7,3},{8,12},{9,13},{10,... | collective-permute-start | bytes 49160 | tf_op jit(solution)/shard_map/ppermute | solution.py:495
  60.8 0.9 collective-permute-start.28
  61.7 1.9 %collective-permute-done.26 = f32[32,128]{1,0:T(8,128)S(1)} collective-permute-done((f32[32,128]{1,0:T(8,128)S(1)}, f32[32,128]{1,0:T(8,128)S(1)}, u32[]{:S(2)}, u32[]{:S(2)}) %collective-permute-start.26) | collective-permute-done | bytes 16416 | tf_op jit(solution)/shard_map/ppermute | solution.py:495
  63.6 1.1 %collective-permute-start.22 = (bf16[640,128]{1,0:T(8,128)(2,1)S(1)}, bf16[640,128]{1,0:T(8,128)(2,1)}, u32[]{:S(2)}, u32[]{:S(2)}) collective-permute-start(bf16[640,128]{1,0:T(8,128)(2,1)S(1)} %collective-permute-done.15.refs_9_), channel_id=1, source_target_pairs={{0,4},{1,3},{2,6},{3,1},{4,0},{5,7},{6,2},{7,5},{8,12},{9,11},{10,... | collective-permute-start | bytes 491528 | tf_op jit(solution)/shard_map/ppermute | solution.py:495
  64.8 0.9 collective-permute-start.23
  65.7 2.2 %collective-permute-done.28.refs_3_ = bf16[160,256]{1,0:T(8,128)(2,1)S(1)} collective-permute-done((bf16[160,256]{1,0:T(8,128)(2,1)S(1)}, bf16[160,256]{1,0:T(8,128)(2,1)S(1)}, u32[]{:S(2)}, u32[]{:S(2)}) %collective-permute-start.28) | collective-permute-done | bytes 81952 | tf_op jit(solution)/shard_map/ppermute | solution.py:59
  67.9 5.0 %collective-permute-done.29.refs_4_ = bf16[160,256]{1,0:T(8,128)(2,1)S(1)} collective-permute-done((bf16[160,256]{1,0:T(8,128)(2,1)S(1)}, bf16[160,256]{1,0:T(8,128)(2,1)S(1)}, u32[]{:S(2)}, u32[]{:S(2)}) %collective-permute-start.29) | collective-permute-done | bytes 81952 | tf_op jit(solution)/shard_map/ppermute | solution.py:59
  73.8 0.9 collective-permute-start.34
  74.7 1.4 %collective-permute-start.32 = (f32[32,128]{1,0:T(8,128)S(1)}, f32[32,128]{1,0:T(8,128)S(1)}, u32[]{:S(2)}, u32[]{:S(2)}) collective-permute-start(f32[32,128]{1,0:T(8,128)S(1)} %add.9), channel_id=1, source_target_pairs={{0,8},{1,9},{2,10},{3,11},{4,12},{5,13},{6,14},{7,15},{8,0},{9,1},... | collective-permute-start | bytes 49160 | tf_op jit(solution)/shard_map/ppermute | solution.py:495
  76.3 1.4 %shard_map.136 = (bf16[160,512]{1,0:T(8,128)(2,1)S(1)}, bf16[640,128]{1,0:T(8,128)(2,1)}) custom-call(s32[3]{0:T(128)S(1)} %pad_add_fusion.refs_0_, bf16[160,256]{1,0:T(8,128)(2,1)S(1)} %get-tuple-element.120.refs_1_, bf16[160,256]{1,0:T(8,128)(2,1)S(1)} %collective-permute-done.27.refs_2_, bf16[160,256]{1,0:T(8,128)(2,1)S(1)} %collective-permute-done.28.refs_3_, ...), custom_call_target="tpu_custom_call" | custom-call | flops 1 | bytes 1 | tf_op jit(solution)/shard_map/pallas_call | solution.py:42
  79.0 1.5 %collective-permute-done.31.refs_6_ = bf16[144,640]{1,0:T(8,128)(2,1)S(1)} collective-permute-done((bf16[144,640]{1,0:T(8,128)(2,1)S(1)}, bf16[144,640]{1,0:T(8,128)(2,1)S(1)}, u32[]{:S(2)}, u32[]{:S(2)}) %collective-permute-start.31) | collective-permute-done | bytes 184352 | tf_op jit(solution)/shard_map/ppermute | solution.py:495
  81.0 1.1 %collective-permute-start.36 = (bf16[2,640,128]{2,1,0:T(8,128)(2,1)S(1)}, bf16[2,640,128]{2,1,0:T(8,128)(2,1)S(1)}, u32[]{:S(2)}, u32[]{:S(2)}) collective-permute-start(bf16[2,640,128]{2,1,0:T(8,128)(2,1)S(1)} %collective-permute-done.17.refs_14_), channel_id=1, source_target_pairs={{0,1},{1,0},{2,3},{3,2},{4,5},{5,4},{6,7},{7,6},{8,9},{9,8},{10,11... | collective-permute-start | bytes 983048 | tf_op jit(solution)/shard_map/ppermute | solution.py:495
  82.1 3.3 %collective-permute-done.41 = f32[32,128]{1,0:T(8,128)S(1)} collective-permute-done((f32[32,128]{1,0:T(8,128)S(1)}, f32[32,128]{1,0:T(8,128)S(1)}, u32[]{:S(2)}, u32[]{:S(2)}) %collective-permute-start.41) | collective-permute-done | bytes 16416 | tf_op jit(solution)/shard_map/ppermute | solution.py:495
  86.1 1.4 %collective-permute-start.44 = (f32[32,128]{1,0:T(8,128)S(1)}, f32[32,128]{1,0:T(8,128)S(1)}, u32[]{:S(2)}, u32[]{:S(2)}) collective-permute-start(f32[32,128]{1,0:T(8,128)S(1)} %add.11.refs_1_), channel_id=1, source_target_pairs={{0,3},{1,2},{2,1},{3,0},{4,7},{5,6},{6,5},{7,4},{8,11},{9,10},{10,... | collective-permute-start | bytes 49160 | tf_op jit(solution)/shard_map/ppermute | solution.py:59
  88.2 1.6 %collective-permute-done.43.refs_3_ = f32[32,128]{1,0:T(8,128)S(1)} collective-permute-done((f32[32,128]{1,0:T(8,128)S(1)}, f32[32,128]{1,0:T(8,128)S(1)}, u32[]{:S(2)}, u32[]{:S(2)}) %collective-permute-start.43) | collective-permute-done | bytes 16416 | tf_op jit(solution)/shard_map/ppermute | solution.py:59
  90.4 0.7 reshape.49
  91.1 1.2 %shard_map.138 = (f32[18,512]{1,0:T(8,128)}, f32[1,512]{1,0:T(1,128)}, f32[1,512]{1,0:T(1,128)}) custom-call(s32[3]{0:T(128)S(1)} %pad_add_fusion.refs_0_, f32[32,128]{1,0:T(8,128)S(1)} %add.11.refs_1_, f32[32,128]{1,0:T(8,128)S(1)} %collective-permute-done.42.refs_2_, f32[32,128]{1,0:T(8,128)S(1)} %collective-permute-done.43.refs_3_, ...), custom_call_target="tpu_custom_call" | custom-call | flops 1 | bytes 1 | tf_op jit(solution)/shard_map/pallas_call | solution.py:42
  93.0 16.3 %shard_map.137 = f32[27,128,512]{2,1,0:T(8,128)} custom-call(s32[3]{0:T(128)} %copy-done.11, bf16[144,640]{1,0:T(8,128)(2,1)} %copy-done.9, bf16[2,144,640]{2,1,0:T(8,128)(2,1)} %copy-done.1, bf16[144,640]{1,0:T(8,128)(2,1)} %copy-done.22, bf16[144,640]{1,0:T(8,128)(2,1)} %copy-done.21, bf16[2,144,640]{2,1,0:T(8,128)(2,1)} %copy-done.15, ...), custom_call_target="tpu_custom_call" | custom-call | flops 1 | bytes 1 | tf_op jit(solution)/shard_map/pallas_call | solution.py:722
  (118 shorter events, 9.7 us)
Async XLA Ops:
  3.2 87.9 %copy-start.11 = (s32[3]{0:T(128)}, s32[3]{0:T(128)S(1)}, u32[]{:S(2)}) copy-start(s32[3]{0:T(128)S(1)} %pad_add_fusion.refs_0_) | copy-start | bytes 40
  5.8 7.0 %collective-permute-start = (bf16[192,256]{1,0:T(8,128)(2,1)S(1)}, bf16[192,256]{1,0:T(8,128)(2,1)S(1)}, u32[]{:S(2)}, u32[]{:S(2)}) collective-permute-start(bf16[192,256]{1,0:T(8,128)(2,1)S(1)} %get-tuple-element.77), channel_id=1, source_target_pairs={{0,1},{1,0},{2,3},{3,2},{4,5},{5,4},{6,7},{7,6},{8,9},{9,8},{10,11... | collective-permute-start | bytes 294920 | tf_op jit(solution)/shard_map/ppermute | solution.py:59
  6.3 6.5 %collective-permute-start.1 = (bf16[192,256]{1,0:T(8,128)(2,1)S(1)}, bf16[192,256]{1,0:T(8,128)(2,1)S(1)}, u32[]{:S(2)}, u32[]{:S(2)}) collective-permute-start(bf16[192,256]{1,0:T(8,128)(2,1)S(1)} %get-tuple-element.78), channel_id=1, source_target_pairs={{0,2},{1,3},{2,0},{3,1},{4,6},{5,7},{6,4},{7,5},{8,10},{9,11},{10,... | collective-permute-start | bytes 294920 | tf_op jit(solution)/shard_map/ppermute | solution.py:59
  8.9 5.2 %collective-permute-start.2 = (bf16[192,256]{1,0:T(8,128)(2,1)S(1)}, bf16[192,256]{1,0:T(8,128)(2,1)S(1)}, u32[]{:S(2)}, u32[]{:S(2)}) collective-permute-start(bf16[192,256]{1,0:T(8,128)(2,1)S(1)} %get-tuple-element.79), channel_id=1, source_target_pairs={{0,3},{1,2},{2,1},{3,0},{4,7},{5,6},{6,5},{7,4},{8,11},{9,10},{10,... | collective-permute-start | bytes 294920 | tf_op jit(solution)/shard_map/ppermute | solution.py:59
  15.1 9.3 %collective-permute-start.3 = (bf16[144,640]{1,0:T(8,128)(2,1)S(1)}, bf16[144,640]{1,0:T(8,128)(2,1)S(1)}, u32[]{:S(2)}, u32[]{:S(2)}) collective-permute-start(bf16[144,640]{1,0:T(8,128)(2,1)S(1)} %get-tuple-element.114.refs_1_), channel_id=1, source_target_pairs={{0,8},{1,9},{2,10},{3,11},{4,12},{5,13},{6,14},{7,15},{8,16},{9,17... | collective-permute-start | bytes 552968 | tf_op jit(solution)/shard_map/ppermute | solution.py:495
  16.7 10.5 %collective-permute-start.4 = (bf16[144,640]{1,0:T(8,128)(2,1)S(1)}, bf16[144,640]{1,0:T(8,128)(2,1)S(1)}, u32[]{:S(2)}, u32[]{:S(2)}) collective-permute-start(bf16[144,640]{1,0:T(8,128)(2,1)S(1)} %get-tuple-element.114.refs_1_), channel_id=1, source_target_pairs={{0,24},{1,25},{2,26},{3,27},{4,28},{5,29},{6,30},{7,31},{8,0},{9,1... | collective-permute-start | bytes 552968 | tf_op jit(solution)/shard_map/ppermute | solution.py:495
  18.9 8.3 %collective-permute-start.5 = (bf16[144,640]{1,0:T(8,128)(2,1)S(1)}, bf16[144,640]{1,0:T(8,128)(2,1)S(1)}, u32[]{:S(2)}, u32[]{:S(2)}) collective-permute-start(bf16[144,640]{1,0:T(8,128)(2,1)S(1)} %get-tuple-element.114.refs_1_), channel_id=1, source_target_pairs={{0,4},{1,5},{2,6},{3,7},{4,0},{5,1},{6,2},{7,3},{8,12},{9,13},{10,... | collective-permute-start | bytes 552968 | tf_op jit(solution)/shard_map/ppermute | solution.py:495
  22.8 8.4 %collective-permute-start.7 = (bf16[640,128]{1,0:T(8,128)(2,1)S(1)}, bf16[640,128]{1,0:T(8,128)(2,1)S(1)}, u32[]{:S(2)}, u32[]{:S(2)}) collective-permute-start(bf16[640,128]{1,0:T(8,128)(2,1)S(1)} %get-tuple-element.87), channel_id=1, source_target_pairs={{0,2},{1,3},{2,0},{3,1},{4,6},{5,7},{6,4},{7,5},{8,10},{9,11},{10,... | collective-permute-start | bytes 491528 | tf_op jit(solution)/shard_map/ppermute | solution.py:59
  24.3 6.9 %collective-permute-start.8 = (bf16[640,128]{1,0:T(8,128)(2,1)S(1)}, bf16[640,128]{1,0:T(8,128)(2,1)S(1)}, u32[]{:S(2)}, u32[]{:S(2)}) collective-permute-start(bf16[640,128]{1,0:T(8,128)(2,1)S(1)} %get-tuple-element.91), channel_id=1, source_target_pairs={{0,3},{1,2},{2,1},{3,0},{4,7},{5,6},{6,5},{7,4},{8,11},{9,10},{10,... | collective-permute-start | bytes 491528 | tf_op jit(solution)/shard_map/ppermute | solution.py:59
  29.4 1.7 %collective-permute-start.6 = (bf16[640,128]{1,0:T(8,128)(2,1)S(1)}, bf16[640,128]{1,0:T(8,128)(2,1)S(1)}, u32[]{:S(2)}, u32[]{:S(2)}) collective-permute-start(bf16[640,128]{1,0:T(8,128)(2,1)S(1)} %get-tuple-element.90), channel_id=1, source_target_pairs={{0,1},{1,0},{2,3},{3,2},{4,5},{5,4},{6,7},{7,6},{8,9},{9,8},{10,11... | collective-permute-start | bytes 491528 | tf_op jit(solution)/shard_map/ppermute | solution.py:59
  29.6 14.6 %collective-permute-start.14 = (bf16[2,144,640]{2,1,0:T(8,128)(2,1)S(1)}, bf16[2,144,640]{2,1,0:T(8,128)(2,1)S(1)}, u32[]{:S(2)}, u32[]{:S(2)}) collective-permute-start(bf16[2,144,640]{2,1,0:T(8,128)(2,1)S(1)} %shard_map.133.refs_2_), channel_id=1, source_target_pairs={{0,4},{1,5},{2,6},{3,7},{4,0},{5,1},{6,2},{7,3},{8,12},{9,13},{10,... | collective-permute-start | bytes 1105928 | tf_op jit(solution)/shard_map/ppermute | solution.py:495
  32.7 59.7 %copy-start.3 = (bf16[640,128]{1,0:T(8,128)(2,1)}, bf16[640,128]{1,0:T(8,128)(2,1)S(1)}, u32[]{:S(2)}) copy-start(bf16[640,128]{1,0:T(8,128)(2,1)S(1)} %get-tuple-element.98.refs_1_.refs_7_) | copy-start | bytes 491524
  32.7 9.0 %collective-permute-start.9 = (bf16[640,128]{1,0:T(8,128)(2,1)S(1)}, bf16[640,128]{1,0:T(8,128)(2,1)S(1)}, u32[]{:S(2)}, u32[]{:S(2)}) collective-permute-start(bf16[640,128]{1,0:T(8,128)(2,1)S(1)} %get-tuple-element.98.refs_1_.refs_7_), channel_id=1, source_target_pairs={{0,8},{1,9},{2,10},{3,11},{4,12},{5,13},{6,14},{7,15},{8,16},{9,17... | collective-permute-start | bytes 491528 | tf_op jit(solution)/shard_map/ppermute | solution.py:495
  33.9 9.5 %collective-permute-start.10 = (bf16[640,128]{1,0:T(8,128)(2,1)S(1)}, bf16[640,128]{1,0:T(8,128)(2,1)S(1)}, u32[]{:S(2)}, u32[]{:S(2)}) collective-permute-start(bf16[640,128]{1,0:T(8,128)(2,1)S(1)} %get-tuple-element.98.refs_1_.refs_7_), channel_id=1, source_target_pairs={{0,24},{1,25},{2,26},{3,27},{4,28},{5,29},{6,30},{7,31},{8,0},{9,1... | collective-permute-start | bytes 491528 | tf_op jit(solution)/shard_map/ppermute | solution.py:495
  36.6 7.6 %collective-permute-start.11 = (bf16[640,128]{1,0:T(8,128)(2,1)S(1)}, bf16[640,128]{1,0:T(8,128)(2,1)S(1)}, u32[]{:S(2)}, u32[]{:S(2)}) collective-permute-start(bf16[640,128]{1,0:T(8,128)(2,1)S(1)} %get-tuple-element.98.refs_1_.refs_7_), channel_id=1, source_target_pairs={{0,4},{1,3},{2,6},{3,1},{4,0},{5,7},{6,2},{7,5},{8,12},{9,11},{10,... | collective-permute-start | bytes 491528 | tf_op jit(solution)/shard_map/ppermute | solution.py:495
  37.8 6.3 %collective-permute-start.12 = (bf16[640,128]{1,0:T(8,128)(2,1)S(1)}, bf16[640,128]{1,0:T(8,128)(2,1)S(1)}, u32[]{:S(2)}, u32[]{:S(2)}) collective-permute-start(bf16[640,128]{1,0:T(8,128)(2,1)S(1)} %get-tuple-element.98.refs_1_.refs_7_), channel_id=1, source_target_pairs={{0,2},{1,5},{2,0},{3,7},{4,6},{5,1},{6,4},{7,3},{8,10},{9,13},{10,... | collective-permute-start | bytes 491528 | tf_op jit(solution)/shard_map/ppermute | solution.py:495
  41.7 2.5 %collective-permute-start.13 = (bf16[640,128]{1,0:T(8,128)(2,1)S(1)}, bf16[640,128]{1,0:T(8,128)(2,1)S(1)}, u32[]{:S(2)}, u32[]{:S(2)}) collective-permute-start(bf16[640,128]{1,0:T(8,128)(2,1)S(1)} %get-tuple-element.98.refs_1_.refs_7_), channel_id=1, source_target_pairs={{0,1},{1,0},{2,3},{3,2},{4,5},{5,4},{6,7},{7,6},{8,9},{9,8},{10,11... | collective-permute-start | bytes 491528 | tf_op jit(solution)/shard_map/ppermute | solution.py:495
  44.1 48.2 %copy-start.6 = (bf16[640,128]{1,0:T(8,128)(2,1)}, bf16[640,128]{1,0:T(8,128)(2,1)S(1)}, u32[]{:S(2)}) copy-start(bf16[640,128]{1,0:T(8,128)(2,1)S(1)} %collective-permute-done.13.refs_2_.refs_19_) | copy-start | bytes 491524
  44.2 3.7 %collective-permute-start.20 = (bf16[640,128]{1,0:T(8,128)(2,1)S(1)}, bf16[640,128]{1,0:T(8,128)(2,1)S(1)}, u32[]{:S(2)}, u32[]{:S(2)}) collective-permute-start(bf16[640,128]{1,0:T(8,128)(2,1)S(1)} %collective-permute-done.11.refs_3_.refs_10_), channel_id=1, source_target_pairs={{0,1},{1,0},{2,3},{3,2},{4,5},{5,4},{6,7},{7,6},{8,9},{9,8},{10,11... | collective-permute-start | bytes 491528 | tf_op jit(solution)/shard_map/ppermute | solution.py:495
  44.3 5.0 %collective-permute-start.21 = (bf16[640,128]{1,0:T(8,128)(2,1)S(1)}, bf16[640,128]{1,0:T(8,128)(2,1)S(1)}, u32[]{:S(2)}, u32[]{:S(2)}) collective-permute-start(bf16[640,128]{1,0:T(8,128)(2,1)S(1)} %collective-permute-done.12.refs_4_.refs_13_), channel_id=1, source_target_pairs={{0,1},{1,0},{2,3},{3,2},{4,5},{5,4},{6,7},{7,6},{8,9},{9,8},{10,11... | collective-permute-start | bytes 491528 | tf_op jit(solution)/shard_map/ppermute | solution.py:495
  44.8 14.2 %collective-permute-start.16 = (bf16[2,640,128]{2,1,0:T(8,128)(2,1)S(1)}, bf16[2,640,128]{2,1,0:T(8,128)(2,1)S(1)}, u32[]{:S(2)}, u32[]{:S(2)}) collective-permute-start(bf16[2,640,128]{2,1,0:T(8,128)(2,1)S(1)} %shard_map.134.refs_8_), channel_id=1, source_target_pairs={{0,4},{1,3},{2,6},{3,1},{4,0},{5,7},{6,2},{7,5},{8,12},{9,11},{10,... | collective-permute-start | bytes 983048 | tf_op jit(solution)/shard_map/ppermute | solution.py:495
  46.3 12.6 %collective-permute-start.17 = (bf16[2,640,128]{2,1,0:T(8,128)(2,1)S(1)}, bf16[2,640,128]{2,1,0:T(8,128)(2,1)S(1)}, u32[]{:S(2)}, u32[]{:S(2)}) collective-permute-start(bf16[2,640,128]{2,1,0:T(8,128)(2,1)S(1)} %shard_map.134.refs_8_), channel_id=1, source_target_pairs={{0,2},{1,5},{2,0},{3,7},{4,6},{5,1},{6,4},{7,3},{8,10},{9,13},{10,... | collective-permute-start | bytes 983048 | tf_op jit(solution)/shard_map/ppermute | solution.py:495
  47.9 11.1 %collective-permute-start.19 = (bf16[2,640,128]{2,1,0:T(8,128)(2,1)S(1)}, bf16[2,640,128]{2,1,0:T(8,128)(2,1)S(1)}, u32[]{:S(2)}, u32[]{:S(2)}) collective-permute-start(bf16[2,640,128]{2,1,0:T(8,128)(2,1)S(1)} %shard_map.134.refs_8_), channel_id=1, source_target_pairs={{0,1},{1,0},{2,3},{3,2},{4,5},{5,4},{6,7},{7,6},{8,9},{9,8},{10,11... | collective-permute-start | bytes 983048 | tf_op jit(solution)/shard_map/ppermute | solution.py:495
  47.9 11.0 %collective-permute-start.15 = (bf16[640,128]{1,0:T(8,128)(2,1)S(1)}, bf16[640,128]{1,0:T(8,128)(2,1)S(1)}, u32[]{:S(2)}, u32[]{:S(2)}) collective-permute-start(bf16[640,128]{1,0:T(8,128)(2,1)S(1)} %get-tuple-element.98.refs_1_.refs_7_), channel_id=1, source_target_pairs={{0,16},{1,17},{2,18},{3,19},{4,20},{5,21},{6,22},{7,23},{8,24},{9,... | collective-permute-start | bytes 491528 | tf_op jit(solution)/shard_map/ppermute | solution.py:495
  49.3 9.7 %collective-permute-start.18 = (bf16[640,128]{1,0:T(8,128)(2,1)S(1)}, bf16[640,128]{1,0:T(8,128)(2,1)S(1)}, u32[]{:S(2)}, u32[]{:S(2)}) collective-permute-start(bf16[640,128]{1,0:T(8,128)(2,1)S(1)} %collective-permute-done.11.refs_3_.refs_10_), channel_id=1, source_target_pairs={{0,2},{1,5},{2,0},{3,7},{4,6},{5,1},{6,4},{7,3},{8,10},{9,13},{10,... | collective-permute-start | bytes 491528 | tf_op jit(solution)/shard_map/ppermute | solution.py:495
  59.0 13.9 %collective-permute-start.24 = (bf16[2,640,128]{2,1,0:T(8,128)(2,1)S(1)}, bf16[2,640,128]{2,1,0:T(8,128)(2,1)}, u32[]{:S(2)}, u32[]{:S(2)}) collective-permute-start(bf16[2,640,128]{2,1,0:T(8,128)(2,1)S(1)} %collective-permute-done.16.refs_11_), channel_id=1, source_target_pairs={{0,2},{1,5},{2,0},{3,7},{4,6},{5,1},{6,4},{7,3},{8,10},{9,13},{10,... | collective-permute-start | bytes 983048 | tf_op jit(solution)/shard_map/ppermute | solution.py:495
  59.5 5.2 %collective-permute-start.27 = (bf16[160,256]{1,0:T(8,128)(2,1)S(1)}, bf16[160,256]{1,0:T(8,128)(2,1)S(1)}, u32[]{:S(2)}, u32[]{:S(2)}) collective-permute-start(bf16[160,256]{1,0:T(8,128)(2,1)S(1)} %get-tuple-element.117), channel_id=1, source_target_pairs={{0,1},{1,0},{2,3},{3,2},{4,5},{5,4},{6,7},{7,6},{8,9},{9,8},{10,11... | collective-permute-start | bytes 245768 | tf_op jit(solution)/shard_map/ppermute | solution.py:59
  59.5 13.4 %collective-permute-start.25 = (bf16[144,640]{1,0:T(8,128)(2,1)S(1)}, bf16[144,640]{1,0:T(8,128)(2,1)S(1)}, u32[]{:S(2)}, u32[]{:S(2)}) collective-permute-start(bf16[144,640]{1,0:T(8,128)(2,1)S(1)} %get-tuple-element.114.refs_1_), channel_id=1, source_target_pairs={{0,16},{1,17},{2,18},{3,19},{4,20},{5,21},{6,22},{7,23},{8,24},{9,... | collective-permute-start | bytes 552968 | tf_op jit(solution)/shard_map/ppermute | solution.py:495
  59.6 4.0 %collective-permute-start.26 = (f32[32,128]{1,0:T(8,128)S(1)}, f32[32,128]{1,0:T(8,128)S(1)}, u32[]{:S(2)}, u32[]{:S(2)}) collective-permute-start(f32[32,128]{1,0:T(8,128)S(1)} %get-tuple-element.115), channel_id=1, source_target_pairs={{0,4},{1,5},{2,6},{3,7},{4,0},{5,1},{6,2},{7,3},{8,12},{9,13},{10,... | collective-permute-start | bytes 49160 | tf_op jit(solution)/shard_map/ppermute | solution.py:495
  60.8 7.1 %collective-permute-start.28 = (bf16[160,256]{1,0:T(8,128)(2,1)S(1)}, bf16[160,256]{1,0:T(8,128)(2,1)S(1)}, u32[]{:S(2)}, u32[]{:S(2)}) collective-permute-start(bf16[160,256]{1,0:T(8,128)(2,1)S(1)} %get-tuple-element.118), channel_id=1, source_target_pairs={{0,2},{1,3},{2,0},{3,1},{4,6},{5,7},{6,4},{7,5},{8,10},{9,11},{10,... | collective-permute-start | bytes 245768 | tf_op jit(solution)/shard_map/ppermute | solution.py:59
  63.6 9.3 %collective-permute-start.22 = (bf16[640,128]{1,0:T(8,128)(2,1)S(1)}, bf16[640,128]{1,0:T(8,128)(2,1)}, u32[]{:S(2)}, u32[]{:S(2)}) collective-permute-start(bf16[640,128]{1,0:T(8,128)(2,1)S(1)} %collective-permute-done.15.refs_9_), channel_id=1, source_target_pairs={{0,4},{1,3},{2,6},{3,1},{4,0},{5,7},{6,2},{7,5},{8,12},{9,11},{10,... | collective-permute-start | bytes 491528 | tf_op jit(solution)/shard_map/ppermute | solution.py:495
  64.8 8.2 %collective-permute-start.23 = (bf16[640,128]{1,0:T(8,128)(2,1)S(1)}, bf16[640,128]{1,0:T(8,128)(2,1)}, u32[]{:S(2)}, u32[]{:S(2)}) collective-permute-start(bf16[640,128]{1,0:T(8,128)(2,1)S(1)} %collective-permute-done.15.refs_9_), channel_id=1, source_target_pairs={{0,2},{1,5},{2,0},{3,7},{4,6},{5,1},{6,4},{7,3},{8,10},{9,13},{10,... | collective-permute-start | bytes 491528 | tf_op jit(solution)/shard_map/ppermute | solution.py:495
  67.9 5.0 %collective-permute-start.29 = (bf16[160,256]{1,0:T(8,128)(2,1)S(1)}, bf16[160,256]{1,0:T(8,128)(2,1)S(1)}, u32[]{:S(2)}, u32[]{:S(2)}) collective-permute-start(bf16[160,256]{1,0:T(8,128)(2,1)S(1)} %get-tuple-element.119), channel_id=1, source_target_pairs={{0,3},{1,2},{2,1},{3,0},{4,7},{5,6},{6,5},{7,4},{8,11},{9,10},{10,... | collective-permute-start | bytes 245768 | tf_op jit(solution)/shard_map/ppermute | solution.py:59
  73.0 7.5 %collective-permute-start.31 = (bf16[144,640]{1,0:T(8,128)(2,1)S(1)}, bf16[144,640]{1,0:T(8,128)(2,1)S(1)}, u32[]{:S(2)}, u32[]{:S(2)}) collective-permute-start(bf16[144,640]{1,0:T(8,128)(2,1)S(1)} %collective-permute-done.25.refs_3_), channel_id=1, source_target_pairs={{0,4},{1,5},{2,6},{3,7},{4,0},{5,1},{6,2},{7,3},{8,12},{9,13},{10,... | collective-permute-start | bytes 552968 | tf_op jit(solution)/shard_map/ppermute | solution.py:495
  73.4 5.6 %collective-permute-start.30 = (bf16[640,128]{1,0:T(8,128)(2,1)}, bf16[640,128]{1,0:T(8,128)(2,1)}, u32[]{:S(2)}, u32[]{:S(2)}) collective-permute-start(bf16[640,128]{1,0:T(8,128)(2,1)} %collective-permute-done.22.refs_12_), channel_id=1, source_target_pairs={{0,2},{1,5},{2,0},{3,7},{4,6},{5,1},{6,4},{7,3},{8,10},{9,13},{10,... | collective-permute-start | bytes 491528 | tf_op jit(solution)/shard_map/ppermute | solution.py:495
  73.8 12.3 %collective-permute-start.34 = (bf16[2,640,128]{2,1,0:T(8,128)(2,1)S(1)}, bf16[2,640,128]{2,1,0:T(8,128)(2,1)S(1)}, u32[]{:S(2)}, u32[]{:S(2)}) collective-permute-start(bf16[2,640,128]{2,1,0:T(8,128)(2,1)S(1)} %collective-permute-done.16.refs_11_), channel_id=1, source_target_pairs={{0,1},{1,0},{2,3},{3,2},{4,5},{5,4},{6,7},{7,6},{8,9},{9,8},{10,11... | collective-permute-start | bytes 983048 | tf_op jit(solution)/shard_map/ppermute | solution.py:495
  74.7 3.7 %collective-permute-start.32 = (f32[32,128]{1,0:T(8,128)S(1)}, f32[32,128]{1,0:T(8,128)S(1)}, u32[]{:S(2)}, u32[]{:S(2)}) collective-permute-start(f32[32,128]{1,0:T(8,128)S(1)} %add.9), channel_id=1, source_target_pairs={{0,8},{1,9},{2,10},{3,11},{4,12},{5,13},{6,14},{7,15},{8,0},{9,1},... | collective-permute-start | bytes 49160 | tf_op jit(solution)/shard_map/ppermute | solution.py:495
  76.0 9.4 %collective-permute-start.33 = (bf16[640,128]{1,0:T(8,128)(2,1)S(1)}, bf16[640,128]{1,0:T(8,128)(2,1)S(1)}, u32[]{:S(2)}, u32[]{:S(2)}) collective-permute-start(bf16[640,128]{1,0:T(8,128)(2,1)S(1)} %collective-permute-done.15.refs_9_), channel_id=1, source_target_pairs={{0,1},{1,0},{2,3},{3,2},{4,5},{5,4},{6,7},{7,6},{8,9},{9,8},{10,11... | collective-permute-start | bytes 491528 | tf_op jit(solution)/shard_map/ppermute | solution.py:495
  78.4 7.6 %collective-permute-start.38 = (bf16[640,128]{1,0:T(8,128)(2,1)S(1)}, bf16[640,128]{1,0:T(8,128)(2,1)S(1)}, u32[]{:S(2)}, u32[]{:S(2)}) collective-permute-start(bf16[640,128]{1,0:T(8,128)(2,1)S(1)} %collective-permute-done.18.refs_16_), channel_id=1, source_target_pairs={{0,1},{1,0},{2,3},{3,2},{4,5},{5,4},{6,7},{7,6},{8,9},{9,8},{10,11... | collective-permute-start | bytes 491528 | tf_op jit(solution)/shard_map/ppermute | solution.py:495
  80.5 4.9 %collective-permute-start.41 = (f32[32,128]{1,0:T(8,128)S(1)}, f32[32,128]{1,0:T(8,128)S(1)}, u32[]{:S(2)}, u32[]{:S(2)}) collective-permute-start(f32[32,128]{1,0:T(8,128)S(1)} %add.10), channel_id=1, source_target_pairs={{0,16},{1,17},{2,18},{3,19},{4,20},{5,21},{6,22},{7,23},{8,24},{9,... | collective-permute-start | bytes 49160 | tf_op jit(solution)/shard_map/ppermute | solution.py:495
  81.0 11.3 %collective-permute-start.36 = (bf16[2,640,128]{2,1,0:T(8,128)(2,1)S(1)}, bf16[2,640,128]{2,1,0:T(8,128)(2,1)S(1)}, u32[]{:S(2)}, u32[]{:S(2)}) collective-permute-start(bf16[2,640,128]{2,1,0:T(8,128)(2,1)S(1)} %collective-permute-done.17.refs_14_), channel_id=1, source_target_pairs={{0,1},{1,0},{2,3},{3,2},{4,5},{5,4},{6,7},{7,6},{8,9},{9,8},{10,11... | collective-permute-start | bytes 983048 | tf_op jit(solution)/shard_map/ppermute | solution.py:495
  85.4 6.9 %collective-permute-start.39 = (bf16[2,640,128]{2,1,0:T(8,128)(2,1)}, bf16[2,640,128]{2,1,0:T(8,128)(2,1)}, u32[]{:S(2)}, u32[]{:S(2)}) collective-permute-start(bf16[2,640,128]{2,1,0:T(8,128)(2,1)} %collective-permute-done.24.refs_17_), channel_id=1, source_target_pairs={{0,1},{1,0},{2,3},{3,2},{4,5},{5,4},{6,7},{7,6},{8,9},{9,8},{10,11... | collective-permute-start | bytes 983048 | tf_op jit(solution)/shard_map/ppermute | solution.py:495
  85.5 2.0 %collective-permute-start.42 = (f32[32,128]{1,0:T(8,128)S(1)}, f32[32,128]{1,0:T(8,128)S(1)}, u32[]{:S(2)}, u32[]{:S(2)}) collective-permute-start(f32[32,128]{1,0:T(8,128)S(1)} %add.11.refs_1_), channel_id=1, source_target_pairs={{0,1},{1,0},{2,3},{3,2},{4,5},{5,4},{6,7},{7,6},{8,9},{9,8},{10,11... | collective-permute-start | bytes 49160 | tf_op jit(solution)/shard_map/ppermute | solution.py:59
  86.0 3.7 %collective-permute-start.43 = (f32[32,128]{1,0:T(8,128)S(1)}, f32[32,128]{1,0:T(8,128)S(1)}, u32[]{:S(2)}, u32[]{:S(2)}) collective-permute-start(f32[32,128]{1,0:T(8,128)S(1)} %add.11.refs_1_), channel_id=1, source_target_pairs={{0,2},{1,3},{2,0},{3,1},{4,6},{5,7},{6,4},{7,5},{8,10},{9,11},{10,... | collective-permute-start | bytes 49160 | tf_op jit(solution)/shard_map/ppermute | solution.py:59
  86.1 3.7 %collective-permute-start.44 = (f32[32,128]{1,0:T(8,128)S(1)}, f32[32,128]{1,0:T(8,128)S(1)}, u32[]{:S(2)}, u32[]{:S(2)}) collective-permute-start(f32[32,128]{1,0:T(8,128)S(1)} %add.11.refs_1_), channel_id=1, source_target_pairs={{0,3},{1,2},{2,1},{3,0},{4,7},{5,6},{6,5},{7,4},{8,11},{9,10},{10,... | collective-permute-start | bytes 49160 | tf_op jit(solution)/shard_map/ppermute | solution.py:59
  87.5 4.8 %collective-permute-start.35 = (bf16[640,128]{1,0:T(8,128)(2,1)}, bf16[640,128]{1,0:T(8,128)(2,1)}, u32[]{:S(2)}, u32[]{:S(2)}) collective-permute-start(bf16[640,128]{1,0:T(8,128)(2,1)} %collective-permute-done.22.refs_12_), channel_id=1, source_target_pairs={{0,1},{1,0},{2,3},{3,2},{4,5},{5,4},{6,7},{7,6},{8,9},{9,8},{10,11... | collective-permute-start | bytes 491528 | tf_op jit(solution)/shard_map/ppermute | solution.py:495
  89.8 2.5 %collective-permute-start.37 = (bf16[640,128]{1,0:T(8,128)(2,1)}, bf16[640,128]{1,0:T(8,128)(2,1)}, u32[]{:S(2)}, u32[]{:S(2)}) collective-permute-start(bf16[640,128]{1,0:T(8,128)(2,1)} %collective-permute-done.23.refs_15_), channel_id=1, source_target_pairs={{0,1},{1,0},{2,3},{3,2},{4,5},{5,4},{6,7},{7,6},{8,9},{9,8},{10,11... | collective-permute-start | bytes 491528 | tf_op jit(solution)/shard_map/ppermute | solution.py:495
  89.8 2.5 %collective-permute-start.40 = (bf16[640,128]{1,0:T(8,128)(2,1)}, bf16[640,128]{1,0:T(8,128)(2,1)}, u32[]{:S(2)}, u32[]{:S(2)}) collective-permute-start(bf16[640,128]{1,0:T(8,128)(2,1)} %collective-permute-done.30.refs_18_), channel_id=1, source_target_pairs={{0,1},{1,0},{2,3},{3,2},{4,5},{5,4},{6,7},{7,6},{8,9},{9,8},{10,11... | collective-permute-start | bytes 491528 | tf_op jit(solution)/shard_map/ppermute | solution.py:495
  (25 other events, 602.5 us)
